TPU v7x, 32 devices: a whole 2x2x4 slice. The times are simulated.
32 devices in a mesh: img: 4 (over z), txt: 8 (over y, x, core).
Axes of the slice: x: 2, y: 2, z: 4, core: 2. Of those that a mesh axis runs over, the one named last changes fastest.
Arguments:
- images: bfloat16 [10240, 1024], P('img', 'txt'), may hold values from -1.5 to 1.5
- texts: bfloat16 [10240, 1024], P('txt', 'img'), may hold values from -1.5 to 1.5
- positive: int32 [10240], P('img'), may hold values from 0 to 10239, each once
Outputs:
- mean_loss: float32 [], replicated
- image_grad: bfloat16 [10240, 1024], P('img', 'txt')
- text_grad: bfloat16 [10240, 1024], P('txt', 'img')
All inputs are finite; a program needn't handle non-finite values.
Results may differ from a plain program's by a relative error of at most 0.0095.
Values may be sent and summed in bfloat16 or wider, within the bound.
No kernel may reach another device: no remote copies, remote signals or barrier semaphores. Data moves between devices by JAX's collectives and lax.ppermute only.
A program may use at most 64 MiB of HBM per device.

v0:
```python
import jax
import jax.numpy as jnp
from jax import lax
from jax.sharding import PartitionSpec as P

logit_scale = 100.0


def merged(shard, axis, combine):
    everything = jax.tree.map(lambda part: lax.all_gather(part, axis), shard)
    leading = jax.tree.map(lambda part: part[0], everything)

    def step(k, so_far):
        return combine(so_far, jax.tree.map(lambda part: part[k], everything))

    return lax.fori_loop(1, lax.axis_size(axis), step, leading)


def combine(earlier, latter):
    larger = jnp.maximum(earlier[0], latter[0])
    scaled = earlier[1] * jnp.exp(earlier[0] - larger) + latter[1] * jnp.exp(latter[0] - larger)
    return (larger, scaled, earlier[2] + latter[2])


def tile_logits(image_block, whole_txt):
    return logit_scale * lax.dot_general(
        image_block, whole_txt, (((1,), (1,)), ((), ())), preferred_element_type=jnp.float32
    )


def per_device(images, texts, positive):
    whole_img = lax.all_gather(images, "txt", axis=1, tiled=True)
    whole_txt = lax.all_gather(texts, "img", axis=1, tiled=True)
    img_rows = whole_img.shape[0]
    txt_rows = whole_txt.shape[0]
    width = whole_txt.shape[1]
    height = min(512, img_rows)
    blocks = img_rows // height
    column_ids = lax.axis_index("txt") * txt_rows + jnp.arange(txt_rows, dtype=jnp.int32)
    img_blocks = whole_img.reshape(blocks, height, width)
    target_blocks = positive.reshape(blocks, height)

    def forward(running, inputs):
        col_max, col_sum, col_pos = running
        image_block, targets = inputs
        logits = tile_logits(image_block, whole_txt)
        matches = targets[:, None] == column_ids[None, :]
        picked = jnp.where(matches, logits, jnp.zeros_like(logits))
        row_max = jnp.max(logits, axis=1)
        row_sum = jnp.sum(jnp.exp(logits - row_max[:, None]), axis=1)
        new_max = jnp.maximum(col_max, jnp.max(logits, axis=0))
        col_sum = col_sum * jnp.exp(col_max - new_max) + jnp.sum(
            jnp.exp(logits - new_max[None, :]), axis=0
        )
        return (
            (new_max, col_sum, col_pos + jnp.sum(picked, axis=0)),
            (row_max, row_sum, jnp.sum(picked, axis=1)),
        )

    empty_cols = jnp.zeros((txt_rows,), jnp.float32)
    initial = (jnp.full((txt_rows,), -jnp.inf, jnp.float32), empty_cols, empty_cols)
    (col_max, col_sum, col_pos), (row_max, row_sum, row_pos) = lax.scan(
        forward, initial, (img_blocks, target_blocks)
    )
    row_max, row_sum, row_pos = merged(
        (row_max.reshape(img_rows), row_sum.reshape(img_rows), row_pos.reshape(img_rows)),
        "txt",
        combine,
    )
    col_max, col_sum, col_pos = merged((col_max, col_sum, col_pos), "img", combine)
    row_lse = row_max + jnp.log(row_sum)
    col_lse = col_max + jnp.log(col_sum)
    row_term = jnp.sum(row_lse - row_pos)
    col_term = jnp.sum(col_lse - col_pos)
    pair_count = txt_rows * lax.axis_size("txt")
    loss_total = lax.psum(
        row_term / lax.axis_size("txt") + col_term / lax.axis_size("img"), ("img", "txt")
    )
    mean_loss = loss_total / (2.0 * pair_count)
    lse_blocks = row_lse.reshape(blocks, height)

    def backward(text_total, inputs):
        image_block, targets, lse_rows = inputs
        logits = tile_logits(image_block, whole_txt)
        matches = (targets[:, None] == column_ids[None, :]).astype(jnp.float32)
        weights = (
            jnp.exp(logits - lse_rows[:, None]) + jnp.exp(logits - col_lse[None, :]) - 2.0 * matches
        ).astype(jnp.bfloat16)
        image_part = logit_scale * jnp.dot(weights, whole_txt, preferred_element_type=jnp.float32)
        text_total = text_total + lax.dot_general(
            weights, image_block, (((0,), (0,)), ((), ())), preferred_element_type=jnp.float32
        )
        return (text_total, image_part)

    text_total, image_parts = lax.scan(
        backward, jnp.zeros((txt_rows, width), jnp.float32), (img_blocks, target_blocks, lse_blocks)
    )
    image_parts = image_parts.reshape(img_rows, image_parts.shape[2])
    image_grad = lax.psum_scatter(
        image_parts.astype(jnp.bfloat16), "txt", scatter_dimension=1, tiled=True
    )
    text_grad = lax.psum_scatter(
        (logit_scale * text_total).astype(jnp.bfloat16), "img", scatter_dimension=1, tiled=True
    )
    return (mean_loss, image_grad, text_grad)


def solution(mesh):
    placed = (P("img", "txt"), P("txt", "img"), P("img"))
    return jax.shard_map(
        per_device,
        mesh=mesh,
        in_specs=placed,
        out_specs=(P(), P("img", "txt"), P("txt", "img")),
        check_vma=False,
    )
```

profile of v0, /device:TPU:0, one launch (start us, length us, event | category | flops | bytes accessed | tf_op | source)
XLA Modules:
  0.0 386.3 jit_solution(331247352240581702)
XLA Ops:
  9.5 57.7 %all-gather.14.cloned.1.call-done = bf16[1280,1024]{1,0:T(8,128)(2,1)} async-done(((bf16[1280,256]{1,0:T(8,128)(2,1)}), bf16[1280,1024]{1,0:T(8,128)(2,1)}) %all-gather.14.cloned.1.call-update) | async-done | bytes 2621456 | tf_op jit(solution)/shard_map/all_gather | solution.py:33
  67.1 42.1 %all-gather.12.cloned.1.call-done = bf16[2560,1024]{1,0:T(8,128)(2,1)} async-done(((bf16[2560,128]{1,0:T(8,128)(2,1)}), bf16[2560,1024]{1,0:T(8,128)(2,1)}) %all-gather.12.cloned.1.call-update) | async-done | bytes 5242896 | tf_op jit(solution)/shard_map/all_gather | solution.py:32
  109.3 26.5 %while.74 = (s32[]{:T(128)}, f32[1280]{0:T(1024)S(1)}, f32[1280]{0:T(1024)S(1)}, f32[1280]{0:T(1024)S(1)}, f32[5,512]{1,0:T(8,128)S(1)}, /*index=5*/f32[5,512]{1...) while((s32[]{:T(128)}, f32[1280]{0:T(1024)S(1)}, ...), condition=%wide.region_7.8_spmd.clone, body=%wide.region_0.7_spmd.clone.sunk | while | flops 1349393664 | bytes 9036968 | solution.py:62
  109.3 3.7 fusion.32
  114.6 3.7 fusion.32
  125.2 3.7 fusion.32
  130.6 3.7 fusion.32
  135.8 13.2 %all-gather.8 = f32[4,1,1280]{2,1,0:T(1,128)S(1)} all-gather(f32[1,1,1280]{2,1,0:T(1,128)S(1)} %reshape.50), channel_id=4, replica_groups=mesh['img'=4,'txt'=8] {'img'}, dimensions={0}, use_global_device_ids=true | all-gather | bytes 25600 | tf_op jit(solution)/shard_map/all_gather | solution.py:10
  149.1 13.1 %all-gather.7 = f32[4,1,1280]{2,1,0:T(1,128)S(1)} all-gather(f32[1,1,1280]{2,1,0:T(1,128)S(1)} %reshape.48), channel_id=3, replica_groups=mesh['img'=4,'txt'=8] {'img'}, dimensions={0}, use_global_device_ids=true | all-gather | bytes 25600 | tf_op jit(solution)/shard_map/all_gather | solution.py:10
  162.3 13.1 %all-gather.6 = f32[4,1,1280]{2,1,0:T(1,128)S(1)} all-gather(f32[1,1,1280]{2,1,0:T(1,128)S(1)} %reshape.46), channel_id=2, replica_groups=mesh['img'=4,'txt'=8] {'img'}, dimensions={0}, use_global_device_ids=true | all-gather | bytes 25600 | tf_op jit(solution)/shard_map/all_gather | solution.py:10
  175.5 9.2 %all-gather.4 = f32[8,1,2560]{2,1,0:T(1,128)S(1)} all-gather(f32[1,1,2560]{2,1,0:T(1,128)S(1)} %reshape.42), channel_id=1, replica_groups=mesh['img'=4,'txt'=8] {'txt'}, dimensions={0}, use_global_device_ids=true | all-gather | bytes 92160 | tf_op jit(solution)/shard_map/all_gather | solution.py:10
  184.8 8.3 %all-gather.3 = f32[8,1,2560]{2,1,0:T(1,128)S(1)} all-gather(f32[1,1,2560]{2,1,0:T(1,128)S(1)} %reshape.40), channel_id=1, replica_groups=mesh['img'=4,'txt'=8] {'txt'}, dimensions={0}, use_global_device_ids=true | all-gather | bytes 92160 | tf_op jit(solution)/shard_map/all_gather | solution.py:10
  193.2 9.2 %all-gather.5 = f32[8,1,2560]{2,1,0:T(1,128)S(1)} all-gather(f32[1,1,2560]{2,1,0:T(1,128)S(1)} %reshape.44), channel_id=1, replica_groups=mesh['img'=4,'txt'=8] {'txt'}, dimensions={0}, use_global_device_ids=true | all-gather | bytes 92160 | tf_op jit(solution)/shard_map/all_gather | solution.py:10
  205.3 53.7 %while.75 = (s32[]{:T(128)}, f32[1280,1024]{1,0:T(8,128)}, bf16[5,512,1024]{2,1,0:T(8,128)(2,1)}, bf16[5,512,1024]{2,1,0:T(8,128)(2,1)}, bf16[1280,1024]{1,0:T(8...) while((s32[]{:T(128)}, f32[1280,1024]{1,0:T(8,128)}, ...), condition=%wide.region_16.17_spmd.clone, body=%wide.region_15.16_spmd.clone.sunk | while | flops 4034921728 | bytes 76311792 | solution.py:95
  205.3 4.4 %subtract_convert_fusion.2 = bf16[512,1280]{1,0:T(8,128)(2,1)S(1)} fusion(bf16[1280,1024]{1,0:T(8,128)(2,1)} %get-tuple-element.1011, s32[1280]{0:T(1024)S(1)} %iota_add_fusion.5, f32[1280]{0:T(1024)S(1)} %get-tuple-element.1013, f32[512]{0:T(512)S(1)} %bitcast.90, s32[512]{0:T(512)S(1)} %bitcast.89, bf16[5,512,1024]{2,1,0:T(8,128)(2,1)} %get-tuple-element.1010, ...), kind=kOutput, calls=%fused_computation.19.clone.1 | convolution fusion | flops 1347420160 | bytes 4995076 | tf_op jit(solution)/shard_map/while/body/eval_jaxpr/dot_general | solution.py:26
  216.2 4.4 %subtract_convert_fusion.2 = bf16[512,1280]{1,0:T(8,128)(2,1)S(1)} fusion(bf16[1280,1024]{1,0:T(8,128)(2,1)} %get-tuple-element.1011, s32[1280]{0:T(1024)S(1)} %iota_add_fusion.5, f32[1280]{0:T(1024)S(1)} %get-tuple-element.1013, f32[512]{0:T(512)S(1)} %bitcast.90, s32[512]{0:T(512)S(1)} %bitcast.89, bf16[5,512,1024]{2,1,0:T(8,128)(2,1)} %get-tuple-element.1010, ...), kind=kOutput, calls=%fused_computation.19.clone.1 | convolution fusion | flops 1347420160 | bytes 4995076 | tf_op jit(solution)/shard_map/while/body/eval_jaxpr/dot_general | solution.py:26
  226.9 4.4 %subtract_convert_fusion.2 = bf16[512,1280]{1,0:T(8,128)(2,1)S(1)} fusion(bf16[1280,1024]{1,0:T(8,128)(2,1)} %get-tuple-element.1011, s32[1280]{0:T(1024)S(1)} %iota_add_fusion.5, f32[1280]{0:T(1024)S(1)} %get-tuple-element.1013, f32[512]{0:T(512)S(1)} %bitcast.90, s32[512]{0:T(512)S(1)} %bitcast.89, bf16[5,512,1024]{2,1,0:T(8,128)(2,1)} %get-tuple-element.1010, ...), kind=kOutput, calls=%fused_computation.19.clone.1 | convolution fusion | flops 1347420160 | bytes 4995076 | tf_op jit(solution)/shard_map/while/body/eval_jaxpr/dot_general | solution.py:26
  237.6 4.4 %subtract_convert_fusion.2 = bf16[512,1280]{1,0:T(8,128)(2,1)S(1)} fusion(bf16[1280,1024]{1,0:T(8,128)(2,1)} %get-tuple-element.1011, s32[1280]{0:T(1024)S(1)} %iota_add_fusion.5, f32[1280]{0:T(1024)S(1)} %get-tuple-element.1013, f32[512]{0:T(512)S(1)} %bitcast.90, s32[512]{0:T(512)S(1)} %bitcast.89, bf16[5,512,1024]{2,1,0:T(8,128)(2,1)} %get-tuple-element.1010, ...), kind=kOutput, calls=%fused_computation.19.clone.1 | convolution fusion | flops 1347420160 | bytes 4995076 | tf_op jit(solution)/shard_map/while/body/eval_jaxpr/dot_general | solution.py:26
  248.3 4.4 %subtract_convert_fusion.2 = bf16[512,1280]{1,0:T(8,128)(2,1)S(1)} fusion(bf16[1280,1024]{1,0:T(8,128)(2,1)} %get-tuple-element.1011, s32[1280]{0:T(1024)S(1)} %iota_add_fusion.5, f32[1280]{0:T(1024)S(1)} %get-tuple-element.1013, f32[512]{0:T(512)S(1)} %bitcast.90, s32[512]{0:T(512)S(1)} %bitcast.89, bf16[5,512,1024]{2,1,0:T(8,128)(2,1)} %get-tuple-element.1010, ...), kind=kOutput, calls=%fused_computation.19.clone.1 | convolution fusion | flops 1347420160 | bytes 4995076 | tf_op jit(solution)/shard_map/while/body/eval_jaxpr/dot_general | solution.py:26
  259.0 7.8 %copy.9 = bf16[2560,1024]{0,1:T(8,128)(2,1)} copy(bf16[2560,1024]{1,0:T(8,128)(2,1)} %bitcast.77) | data formatting | bytes 10485760
  266.9 4.8 %multiply_convert_fusion = bf16[1280,1024]{1,0:T(8,128)(2,1)} fusion(f32[1280,1024]{1,0:T(8,128)} %get-tuple-element.482), kind=kLoop, calls=%fused_computation.38 | loop fusion | flops 2621440 | bytes 7864320 | tf_op jit(solution)/shard_map/convert_element_type | solution.py:103
  272.9 39.2 %psum.7 = f32[]{:T(128)} all-reduce(f32[]{:T(128)S(6)} %add.153), channel_id=1, replica_groups=mesh['img'=4,'txt'=8] {'img','txt'}, use_global_device_ids=true, to_apply=%region_14.15 | all-reduce | flops 1 | bytes 8 | tf_op jit(solution)/shard_map/psum | solution.py:76
  312.8 10.9 %reduce-scatter.7.cloned.1.call-done = bf16[128,2560]{1,0:T(8,128)(2,1)} async-done(((bf16[1024,2560]{1,0:T(8,128)(2,1)}), bf16[128,2560]{1,0:T(8,128)(2,1)}) %reduce-scatter.7.cloned.1.call-update) | async-done | bytes 655376
  325.9 52.8 %reduce-scatter.5.cloned.1.call-done = bf16[1280,256]{1,0:T(8,128)(2,1)} async-done(((bf16[1280,1024]{1,0:T(8,128)(2,1)}), bf16[1280,256]{1,0:T(8,128)(2,1)}) %reduce-scatter.5.cloned.1.call-update) | async-done | bytes 655376 | tf_op jit(solution)/shard_map/reduce_scatter | solution.py:102
  (182 shorter events, 51.5 us)
Async XLA Ops:
  7.2 60.0 %all-gather.14.cloned.1.call-start = ((), (), s32[]{:S(2)}) async-start(), calls=%async_computation.3 | async-start | bytes 3276800 | tf_op jit(solution)/shard_map/all_gather | solution.py:33
  7.9 101.4 %all-gather.12.cloned.1.call-start = ((), (), s32[]{:S(2)}) async-start(), calls=%async_computation.2 | async-start | bytes 5898240 | tf_op jit(solution)/shard_map/all_gather | solution.py:32
  8.6 315.0 %reduce-scatter.7.cloned.1.call-start = ((), (), s32[]{:S(2)}) async-start(), calls=%async_computation.5 | async-start | bytes 5898240
  205.3 4.4 %copy-start = (f32[1280,1024]{1,0:T(8,128)S(1)}, f32[1280,1024]{1,0:T(8,128)}, u32[]{:S(2)}) copy-start(f32[1280,1024]{1,0:T(8,128)} %get-tuple-element.997) | copy-start | bytes 15728644 | tf_op jit(solution)/shard_map/while
  209.7 3.6 copy-start.2
  213.4 2.7 copy-start.1
  216.1 4.4 %copy-start = (f32[1280,1024]{1,0:T(8,128)S(1)}, f32[1280,1024]{1,0:T(8,128)}, u32[]{:S(2)}) copy-start(f32[1280,1024]{1,0:T(8,128)} %get-tuple-element.997) | copy-start | bytes 15728644 | tf_op jit(solution)/shard_map/while
  220.6 3.6 copy-start.2
  224.2 2.6 copy-start.1
  226.9 4.4 %copy-start = (f32[1280,1024]{1,0:T(8,128)S(1)}, f32[1280,1024]{1,0:T(8,128)}, u32[]{:S(2)}) copy-start(f32[1280,1024]{1,0:T(8,128)} %get-tuple-element.997) | copy-start | bytes 15728644 | tf_op jit(solution)/shard_map/while
  231.3 3.6 copy-start.2
  234.9 2.6 copy-start.1
  237.6 4.4 %copy-start = (f32[1280,1024]{1,0:T(8,128)S(1)}, f32[1280,1024]{1,0:T(8,128)}, u32[]{:S(2)}) copy-start(f32[1280,1024]{1,0:T(8,128)} %get-tuple-element.997) | copy-start | bytes 15728644 | tf_op jit(solution)/shard_map/while
  242.0 3.6 copy-start.2
  245.6 2.6 copy-start.1
  248.3 4.4 %copy-start = (f32[1280,1024]{1,0:T(8,128)S(1)}, f32[1280,1024]{1,0:T(8,128)}, u32[]{:S(2)}) copy-start(f32[1280,1024]{1,0:T(8,128)} %get-tuple-element.997) | copy-start | bytes 15728644 | tf_op jit(solution)/shard_map/while
  252.7 3.6 copy-start.2
  256.4 2.7 copy-start.1
  266.8 111.9 %reduce-scatter.5.cloned.1.call-start = ((), (), s32[]{:S(2)}) async-start(), calls=%async_computation.4 | async-start | bytes 3276800 | tf_op jit(solution)/shard_map/reduce_scatter | solution.py:102
Sparse Core Ops, SparseCore 0:
  9.6 57.5 all-gather.13
  69.0 40.2 all-gather.11
  266.9 56.7 reduce-scatter.6
  326.5 52.0 reduce-scatter.4
where the time goes:
time: 387 us; the launch traced here: 386 us
  waiting for transfers between devices  165 us (43%)
  blocking collectives  105 us (27%)
  matrix products  71.8 us (19%)
  between operations  17 us (4%)
  other arithmetic  12.9 us (3%)
  local copies, waits for them, and re-layouts  12.9 us (3%)
    all_gather x6, blocking collectives, merged(): everything = jax.tree.map(lambda part: lax.all_gather(part, axis), shard)  66.2 us
    all_gather x1, waiting for transfers between devices, per_device(): whole_txt = lax.all_gather(texts, 'img', axis=1, tiled=True)  57.7 us
    reduce_scatter x1, waiting for transfers between devices, per_device(): lax.psum_scatter((logit_scale * text_total).astype(jnp.bfloat16), 'img',...  52.8 us
    all_gather x1, waiting for transfers between devices, per_device(): whole_img = lax.all_gather(images, 'txt', axis=1, tiled=True)  42.1 us
    dot_general x10, matrix products, tile_logits(): lax.dot_general(image_block, whole_txt, (((1,), (1,)), ((), ())), preferr...  40.5 us
    psum x1, blocking collectives, per_device(): lax.psum(row_term / lax.axis_size('txt') + col_term / lax.axis_size('img'...  39.2 us
    dot_general x5, matrix products, backward(): lax.dot_general(weights, image_block, (((0,), (0,)), ((), ())), preferred...  18.1 us
    dot_general x5, matrix products, backward(): jnp.dot(weights, whole_txt, preferred_element_type=jnp.float32)  13.2 us
  transfers between devices with their start and end apart: 4, of which 4 were waited for; matrix products, arithmetic and copies ran while one was open for 2% of the time, Pallas kernels for 0%

commit v1 on v0

v1 whole, which is shorter than its diff:
```python
import functools
import math
import jax
import jax.numpy as jnp
from jax import lax
from jax.experimental import pallas as pl
from jax.experimental.pallas import tpu as pltpu
from jax.sharding import PartitionSpec as P

logit_scale = 100.0
log2e = math.log2(math.e)
ln2 = math.log(2.0)
strip = 16
vmem_bytes = 28 * 1024 * 1024

VMEM = pl.BlockSpec(memory_space=pltpu.VMEM)
ANY = pl.BlockSpec(memory_space=pl.ANY)


def block_rows(rows, most):
    size = most
    while rows % size:
        size //= 2
    return size


def columns(slot, width):
    return pl.ds(pl.multiple_of(slot * width, width), width)


def params():
    return pltpu.CompilerParams(vmem_limit_bytes=vmem_bytes)


def cost(rows, cols, depth, exps):
    return pl.CostEstimate(
        flops=2 * rows * cols * depth,
        bytes_accessed=rows * cols * 4 + rows * depth * 2,
        transcendentals=rows * cols * exps,
    )


def place_pieces(pieces, width):
    rows = max(first + piece.shape[0] for piece, first, _ in pieces)

    def kernel(*refs):
        *sources, out, sems = refs
        copies = []
        for k, (source, (piece, first, slot)) in enumerate(zip(sources, pieces)):
            wide = piece.shape[1]
            target = out.at[pl.ds(first, piece.shape[0]), columns(slot(), wide)]
            copies.append(pltpu.make_async_copy(source, target, sems.at[k]))
        for copy in copies:
            copy.start()
        for copy in copies:
            copy.wait()

    return pl.pallas_call(
        kernel,
        out_shape=jax.ShapeDtypeStruct((rows, width), pieces[0][0].dtype),
        in_specs=[ANY] * len(pieces),
        out_specs=ANY,
        scratch_shapes=[pltpu.SemaphoreType.DMA((len(pieces),))],
        name="place_pieces",
    )(*[piece for piece, _, _ in pieces])


def log_add(a, b):
    larger = jnp.maximum(a, b)
    return larger + jnp.log(jnp.exp2(a - larger) + jnp.exp2(b - larger)) * log2e


def logits_and_stats(images, pieces, rows, earlier):
    img_rows, width = images.shape
    bm = block_rows(img_rows, 512)
    steps = img_rows // bm

    def kernel(*refs):
        sources = refs[: len(pieces)]
        refs = refs[len(pieces) :]
        if earlier is not None:
            earlier_ref, *refs = refs
        images_ref, u_ref, texts_ref, row_ref, col_ref, d_scr, rows_scr, cm_scr, cs_scr, sems = refs
        step = pl.program_id(0)

        @pl.when(step == 0)
        def _():
            copies = []
            for k, (source, (_, first, slot, condition)) in enumerate(zip(sources, pieces)):
                wide = source.shape[1]
                copy = pltpu.make_async_copy(
                    source.at[pl.ds(first, rows)], texts_ref.at[:, columns(slot(), wide)], sems.at[k]
                )
                if condition is None:
                    copy.start()
                else:
                    pl.when(condition())(copy.start)
                copies.append((copy, condition))
            cm_scr[...] = jnp.full(cm_scr.shape, -jnp.inf, jnp.float32)
            cs_scr[...] = jnp.zeros(cs_scr.shape, jnp.float32)
            rows_scr[...] = jnp.zeros(rows_scr.shape, jnp.float32)
            for copy, condition in copies:
                if condition is None:
                    copy.wait()
                else:
                    pl.when(condition())(copy.wait)

        d_scr[...] = lax.dot_general(
            images_ref[...], texts_ref[...], (((1,), (1,)), ((), ())), preferred_element_type=jnp.float32
        )
        lane = lax.broadcasted_iota(jnp.int32, (strip, 128), 1)

        def first_pass(s, top):
            at = pl.ds(pl.multiple_of(s * strip, strip), strip)
            u = d_scr[at, :] * (logit_scale * log2e)
            u_ref[at, :] = u
            row_max = jnp.max(u, axis=1, keepdims=True)
            row_sum = jnp.sum(jnp.exp2(u - row_max), axis=1, keepdims=True)
            row_lse = row_max + jnp.log(row_sum) * log2e
            rows_scr[at, :] = jnp.where(lane == step, row_lse, rows_scr[at, :])
            return jnp.maximum(top, jnp.max(u.reshape(strip // 8, 8, rows), axis=0))

        old = cm_scr[...]
        new = lax.fori_loop(0, bm // strip, first_pass, old, unroll=4)

        def second_pass(s, total):
            at = pl.ds(pl.multiple_of(s * strip, strip), strip)
            u = u_ref[at, :].reshape(strip // 8, 8, rows)
            return total + jnp.sum(jnp.exp2(u - new[None]), axis=0)

        total = cs_scr[...] * jnp.exp2(old - new)
        total = lax.fori_loop(0, bm // strip, second_pass, total, unroll=4)
        cm_scr[...] = new
        cs_scr[...] = total

        @pl.when(step == steps - 1)
        def _():
            top = jnp.max(new, axis=0, keepdims=True)
            col_sum = jnp.sum(total * jnp.exp2(new - top), axis=0, keepdims=True)
            col_ref[...] = top + jnp.log(col_sum) * log2e
            own = rows_scr[...].T[:8]
            row_ref[...] = own if earlier is None else log_add(own, earlier_ref[...])

    out = pl.pallas_call(
        kernel,
        grid=(steps,),
        out_shape=(
            jax.ShapeDtypeStruct((img_rows, rows), jnp.float32),
            jax.ShapeDtypeStruct((rows, width), jnp.bfloat16),
            jax.ShapeDtypeStruct((8, bm), jnp.float32),
            jax.ShapeDtypeStruct((1, rows), jnp.float32),
        ),
        in_specs=[ANY] * len(pieces)
        + ([] if earlier is None else [VMEM])
        + [pl.BlockSpec((bm, width), lambda i: (i, 0))],
        out_specs=(pl.BlockSpec((bm, rows), lambda i: (i, 0)), VMEM, VMEM, VMEM),
        scratch_shapes=[
            pltpu.VMEM((bm, rows), jnp.float32),
            pltpu.VMEM((bm, 128), jnp.float32),
            pltpu.VMEM((8, rows), jnp.float32),
            pltpu.VMEM((8, rows), jnp.float32),
            pltpu.SemaphoreType.DMA((len(pieces),)),
        ],
        compiler_params=params(),
        cost_estimate=cost(img_rows, rows, width, 2),
        name="logits_and_stats",
    )(*[p[0] for p in pieces], *([] if earlier is None else [earlier]), images)
    return out


def weights_and_text_grad(u, images, targets, row_lse, col_lse, first, parts):
    img_rows, width = images.shape
    rows = u.shape[1]
    bm = row_lse.shape[1]
    steps = img_rows // bm
    wide = width // len(parts)

    def kernel(u_ref, images_ref, targets_ref, row_ref, col_ref, w_ref, pos_ref, *refs):
        *part_refs, acc, rows_scr, pos_scr = refs
        step = pl.program_id(0)

        @pl.when(step == 0)
        def _():
            padded = jnp.concatenate([row_ref[...], jnp.zeros((120, bm), jnp.float32)], axis=0)
            rows_scr[...] = padded.T
            pos_scr[...] = jnp.zeros(pos_scr.shape, jnp.float32)

        lane = lax.broadcasted_iota(jnp.int32, (strip, 128), 1)
        ids = lax.broadcasted_iota(jnp.int32, (strip, rows), 1) + first
        col = col_ref[...]

        def one(s, picked):
            at = pl.ds(pl.multiple_of(s * strip, strip), strip)
            v = u_ref[at, :]
            row = jnp.sum(jnp.where(lane == step, rows_scr[at, :], 0.0), axis=1, keepdims=True)
            matches = targets_ref[at, :] == ids
            weight = jnp.exp2(v - row) + jnp.exp2(v - col) - jnp.where(matches, 2.0, 0.0)
            w_ref[at, :] = weight.astype(jnp.bfloat16)
            return picked + jnp.sum(jnp.where(matches, v, 0.0).reshape(strip // 8, 8, rows), axis=0)

        pos_scr[...] = lax.fori_loop(0, bm // strip, one, pos_scr[...], unroll=4)
        term = lax.dot_general(
            w_ref[...], images_ref[...], (((0,), (0,)), ((), ())), preferred_element_type=jnp.float32
        )

        @pl.when(step == 0)
        def _():
            acc[...] = term

        @pl.when(step > 0)
        def _():
            acc[...] += term

        @pl.when(step == steps - 1)
        def _():
            for ref, slot in zip(part_refs, parts):
                ref[...] = (logit_scale * acc[:, columns(slot(), wide)]).astype(jnp.bfloat16)
            pos_ref[...] = jnp.sum(pos_scr[...], axis=0, keepdims=True)

    return pl.pallas_call(
        kernel,
        grid=(steps,),
        out_shape=(
            jax.ShapeDtypeStruct((img_rows, rows), jnp.bfloat16),
            jax.ShapeDtypeStruct((1, rows), jnp.float32),
        )
        + (jax.ShapeDtypeStruct((rows, wide), jnp.bfloat16),) * len(parts),
        in_specs=[
            pl.BlockSpec((bm, rows), lambda i: (i, 0)),
            pl.BlockSpec((bm, width), lambda i: (i, 0)),
            pl.BlockSpec((bm, 1), lambda i: (i, 0)),
            VMEM,
            VMEM,
        ],
        out_specs=(pl.BlockSpec((bm, rows), lambda i: (i, 0)), VMEM) + (VMEM,) * len(parts),
        scratch_shapes=[
            pltpu.VMEM((rows, width), jnp.float32),
            pltpu.VMEM((bm, 128), jnp.float32),
            pltpu.VMEM((8, rows), jnp.float32),
        ],
        compiler_params=params(),
        cost_estimate=cost(img_rows, rows, width, 2),
        name="weights_and_text_grad",
    )(u, images, targets, row_lse, col_lse)


def image_grad_parts(weights, texts, first, img_rows, groups):
    width = texts[0].shape[1]
    rows = texts[0].shape[0]
    bm = block_rows(math.gcd(first, img_rows) if first else img_rows, 256)
    wide = width // sum(len(g) for g in groups)

    def kernel(*refs):
        w_refs = refs[: len(weights)]
        t_refs = refs[len(weights) : 2 * len(weights)]
        *outs, acc = refs[2 * len(weights) :]
        total = jnp.dot(w_refs[0][...], t_refs[0][...], preferred_element_type=jnp.float32)
        for w_ref, t_ref in zip(w_refs[1:], t_refs[1:]):
            total += jnp.dot(w_ref[...], t_ref[...], preferred_element_type=jnp.float32)
        acc[...] = logit_scale * total
        for out, group in zip(outs, groups):
            for k, slot in enumerate(group):
                out[:, k * wide : (k + 1) * wide] = acc[:, columns(slot(), wide)].astype(jnp.bfloat16)

    return pl.pallas_call(
        kernel,
        grid=(img_rows // bm,),
        out_shape=tuple(jax.ShapeDtypeStruct((img_rows, wide * len(g)), jnp.bfloat16) for g in groups),
        in_specs=[pl.BlockSpec((bm, rows), lambda i: (i + first // bm, 0))] * len(weights)
        + [VMEM] * len(weights),
        out_specs=tuple(pl.BlockSpec((bm, wide * len(g)), lambda i: (i, 0)) for g in groups),
        scratch_shapes=[pltpu.VMEM((bm, width), jnp.float32)],
        compiler_params=params(),
        cost_estimate=cost(img_rows, rows * len(weights), width, 0),
        name="image_grad_parts",
    )(*weights, *texts)


def loss_of(row_lse, col_lses, picked, img_rows, pairs, n_img, n_txt):
    bm = row_lse.shape[1]
    row_term = jnp.sum(row_lse[: img_rows // bm])
    col_term = sum(jnp.sum(c) for c in col_lses)
    pos = sum(jnp.sum(p) for p in picked)
    total = lax.psum(row_term / n_txt + col_term / n_img - 2.0 * pos, ("img", "txt"))
    return total * (ln2 / (2.0 * pairs))


def shifted(count, by, wrap):
    return [(i, (i + by) % count) for i in range(count) if wrap or 0 <= i + by < count]


def paired(count, by):
    return [(i, i ^ by) for i in range(count)]


def per_device_4x8(images, texts, positive):
    img_rows = images.shape[0]
    txt_rows, quarter = texts.shape
    width = quarter * 4
    half = txt_rows // 2
    up_ring, down_ring = shifted(4, 1, True), shifted(4, -1, True)
    up_line, down_line = [(1, 2), (2, 3)], [(1, 0), (2, 1)]

    def swap(part, by):
        return lax.ppermute(part, "txt", paired(8, by))

    def z_gather(part):
        prev = lax.ppermute(part, "img", up_ring)
        following = lax.ppermute(part, "img", down_ring)
        return prev, following, lax.ppermute(prev, "img", up_line), lax.ppermute(following, "img", down_line)

    gathered = [z_gather(texts[:half]), z_gather(texts[half:])]
    image_half = img_rows // 2
    from_x, from_y = swap(images, 2), swap(images, 4)
    diag_x, diag_y = swap(from_y[:image_half], 2), swap(from_x[image_half:], 4)
    mine = [(images, 0, 0), (from_x, 0, 2), (from_y, 0, 4), (diag_x, 0, 6), (diag_y, image_half, 6)]
    pieces = mine + [(swap(part, 1), first, flip ^ 1) for part, first, flip in mine]

    def txt_slot(flip):
        return lambda: lax.axis_index("txt") ^ flip

    def img_slot(by):
        return lambda: lax.rem(lax.axis_index("img") + by, 4)

    def upper():
        return lax.axis_index("img") >= 2

    def lower():
        return lax.axis_index("img") < 2

    whole_img = place_pieces([(part, first, txt_slot(flip)) for part, first, flip in pieces], width)
    targets = (positive - lax.axis_index("txt") * txt_rows)[:, None]

    def text_pieces(k):
        prev, following, up, down = gathered[k]
        return [
            (texts, k * half, img_slot(0), None),
            (prev, 0, img_slot(3), None),
            (following, 0, img_slot(1), None),
            (up, 0, img_slot(2), upper),
            (down, 0, img_slot(2), lower),
        ]

    def over_img(col):
        col = log_add(col, lax.ppermute(col, "img", paired(4, 1)))
        return log_add(col, lax.ppermute(col, "img", paired(4, 2)))

    u0, texts0, row, col0 = logits_and_stats(whole_img, text_pieces(0), half, None)
    col0 = over_img(col0)
    u1, texts1, row, col1 = logits_and_stats(whole_img, text_pieces(1), half, row)
    for by in (1, 2, 4):
        row = log_add(row, swap(row, by))
    col1 = over_img(col1)

    text_slots = [img_slot(2), img_slot(1), img_slot(3), img_slot(0)]
    weights, picked, text_parts = [], [], []
    for k, (u, col) in enumerate(((u0, col0), (u1, col1))):
        w, pos, opposite, following, prev, own = weights_and_text_grad(
            u, whole_img, targets, row, col, k * half, text_slots
        )
        weights.append(w)
        picked.append(pos)
        from_below = lax.ppermute(opposite, "img", [(0, 1), (1, 2)])
        from_above = lax.ppermute(opposite, "img", [(3, 2), (2, 1)])
        from_prev = lax.ppermute(following + from_below, "img", up_ring)
        from_next = lax.ppermute(prev + from_above, "img", down_ring)
        text_parts.append(
            (own.astype(jnp.float32) + from_prev.astype(jnp.float32) + from_next.astype(jnp.float32)).astype(
                jnp.bfloat16
            )
        )
    text_grad = jnp.concatenate(text_parts, axis=0)
    mean_loss = loss_of(row, (col0, col1), picked, img_rows, txt_rows * 8, 4, 8)

    kept = [[txt_slot(0)], [txt_slot(2)], [txt_slot(4)], [txt_slot(6)]]
    sent = [txt_slot(flip) for flip in (1, 3, 5, 7)]
    sums = []
    eighth = width // 8
    for k in range(2):
        *own, other = image_grad_parts(weights, (texts0, texts1), k * image_half, image_half, kept + [sent])
        other = swap(other, 1)
        sums.append([own[j] + other[:, j * eighth : (j + 1) * eighth] for j in range(4)])
    (s0, x0, y0, d0), (s1, x1, y1, d1) = sums
    d0 = swap(d0, 2)
    d1 = swap(d1, 4)
    image_parts = []
    for s, x, y in ((s0, x0, y0 + d0), (s1, x1 + d1, y1)):
        x, y = swap(x, 2), swap(y, 4)
        image_parts.append(
            (s.astype(jnp.float32) + x.astype(jnp.float32) + y.astype(jnp.float32)).astype(jnp.bfloat16)
        )
    return mean_loss, jnp.concatenate(image_parts, axis=0), text_grad


def per_device(images, texts, positive):
    n_img, n_txt = lax.axis_size("img"), lax.axis_size("txt")
    if (n_img, n_txt) == (4, 8):
        return per_device_4x8(images, texts, positive)
    whole_img = lax.all_gather(images, "txt", axis=1, tiled=True)
    whole_txt = lax.all_gather(texts, "img", axis=1, tiled=True)
    img_rows = whole_img.shape[0]
    txt_rows = whole_txt.shape[0]
    half = txt_rows // 2
    targets = (positive - lax.axis_index("txt") * txt_rows)[:, None]

    def merged(part, axis):
        every = lax.all_gather(part, axis)
        top = jnp.max(every, axis=0)
        return top + jnp.log(jnp.sum(jnp.exp2(every - top), axis=0)) * log2e

    def first_slot():
        return jnp.int32(0)

    row, logits, chunks, cols = None, [], [], []
    for k in range(2):
        u, chunk, row, col = logits_and_stats(whole_img, [(whole_txt, k * half, first_slot, None)], half, row)
        logits.append(u)
        chunks.append(chunk)
        cols.append(merged(col, "img"))
    row = merged(row, "txt")
    weights, picked, text_parts = [], [], []
    for k in range(2):
        w, pos, part = weights_and_text_grad(logits[k], whole_img, targets, row, cols[k], k * half, [first_slot])
        weights.append(w)
        picked.append(pos)
        text_parts.append(part)
    (image_part,) = image_grad_parts(weights, chunks, 0, img_rows, [[first_slot]])
    mean_loss = loss_of(row, cols, picked, img_rows, txt_rows * n_txt, n_img, n_txt)
    image_grad = lax.psum_scatter(image_part, "txt", scatter_dimension=1, tiled=True)
    text_grad = lax.psum_scatter(jnp.concatenate(text_parts, axis=0), "img", scatter_dimension=1, tiled=True)
    return mean_loss, image_grad, text_grad


def solution(mesh):
    placed = (P("img", "txt"), P("txt", "img"), P("img"))
    return jax.shard_map(
        per_device,
        mesh=mesh,
        in_specs=placed,
        out_specs=(P(), P("img", "txt"), P("txt", "img")),
        check_vma=False,
    )
```

time: 387 us -> 411 us (1.062)
  Pallas kernels: 0 us -> 230 us
  waiting for transfers between devices: 165 us -> 46.1 us
  matrix products: 71.8 us -> 0 us
  blocking collectives: 105 us -> 39.5 us
  starting transfers between devices: 0.16 us -> 57.1 us
  between operations: 17 us -> 5.88 us
  other arithmetic: 12.9 us -> 19.2 us
    pallas_call x0 -> x7, Pallas kernels: none -> 230 us  [the longest x1 160 us: place_pieces(): pl.pallas_call(kernel, out_shape=jax.ShapeDtypeStruct((rows, width), piec...]
    all_gather x2 -> x0, waiting for transfers between devices: 99.8 us -> none  [the longest x1 57.7 us: per_device(): whole_txt = lax.all_gather(texts, 'img', axis=1, tiled=True)]
    dot_general x20 -> x0, matrix products: 71.8 us -> none  [the longest x10 40.5 us: tile_logits(): lax.dot_general(image_block, whole_txt, (((1,), (1,)), ((), ())), preferr...]
    all_gather x6 -> x0, blocking collectives: 66.2 us -> none  [merged(): everything = jax.tree.map(lambda part: lax.all_gather(part, axis), shard)]
    ppermute x0 -> x40, starting transfers between devices: none -> 57.1 us  [the longest x20 16 us: swap(): return lax.ppermute(part, 'txt', paired(8, by))]
    reduce_scatter x1 -> x0, waiting for transfers between devices: 52.8 us -> none  [per_device(): lax.psum_scatter((logit_scale * text_total).astype(jnp.bfloat16), 'img',...]
    ppermute x0 -> x40, waiting for transfers between devices: none -> 46.1 us  [the longest x20 28 us: swap(): return lax.ppermute(part, 'txt', paired(8, by))]
    unnamed x5 -> x0, waiting for transfers between devices: 12.3 us -> none
  transfers between devices with their start and end apart: 4 -> 40, of which waited for: 4 -> 15; matrix products, arithmetic and copies ran while one was open for 2% -> 5% of each run, Pallas kernels for 0% -> 53%
where the time goes in v1:
time: 411 us; the launch traced here: 410 us
  Pallas kernels  230 us (56%)
  starting transfers between devices  57.1 us (14%)
  waiting for transfers between devices  46.1 us (11%)
  blocking collectives  39.5 us (10%)
  other arithmetic  19.2 us (5%)
  local copies, waits for them, and re-layouts  12.3 us (3%)
  between operations  5.88 us (1%)
    pallas_call x1, Pallas kernels, place_pieces(): pl.pallas_call(kernel, out_shape=jax.ShapeDtypeStruct((rows, width), piec...  160 us
    psum x1, blocking collectives, loss_of(): lax.psum(row_term / n_txt + col_term / n_img - 2.0 * pos, ('img', 'txt'))  39.5 us
    pallas_call x2, Pallas kernels, logits_and_stats(): pl.pallas_call(kernel, grid=(steps,), out_shape=(jax.ShapeDtypeStruct((im...  31.2 us
    ppermute x20, waiting for transfers between devices, swap(): return lax.ppermute(part, 'txt', paired(8, by))  28 us
    pallas_call x2, Pallas kernels, weights_and_text_grad(): pl.pallas_call(kernel, grid=(steps,), out_shape=(jax.ShapeDtypeStruct((im...  25.8 us
    ppermute x20, starting transfers between devices, swap(): return lax.ppermute(part, 'txt', paired(8, by))  16 us
    pallas_call x2, Pallas kernels, image_grad_parts(): pl.pallas_call(kernel, grid=(img_rows // bm,), out_shape=tuple((jax.Shape...  12.8 us
    ppermute x2, starting transfers between devices, over_img(): col = log_add(col, lax.ppermute(col, 'img', paired(4, 1)))  10.3 us
  transfers between devices with their start and end apart: 40, of which 15 were waited for; matrix products, arithmetic and copies ran while one was open for 5% of the time, Pallas kernels for 53%

profile of v1, /device:TPU:0, one launch (start us, length us, event | category | flops | bytes accessed | tf_op | source)
XLA Modules:
  0.0 409.9 jit_solution(4827017020789781406)
XLA Ops:
  0.7 3.0 collective-permute-start.9
  6.3 3.7 collective-permute-start.5
  10.0 3.8 collective-permute-start.1
  13.8 4.9 %collective-permute-done.9.refs_2_ = bf16[2560,128]{1,0:T(8,128)(2,1)S(1)} collective-permute-done((bf16[2560,128]{1,0:T(8,128)(2,1)}, bf16[2560,128]{1,0:T(8,128)(2,1)S(1)}, u32[]{:S(2)}, u32[]{:S(2)}) %collective-permute-start.9) | collective-permute-done | bytes 655392 | tf_op jit(solution)/shard_map/ppermute | solution.py:305
  23.1 3.0 collective-permute-done.4.refs_1_
  26.1 6.1 %collective-permute-done.1.refs_2_ = bf16[640,256]{1,0:T(8,128)(2,1)S(1)} collective-permute-done((bf16[640,256]{1,0:T(8,128)(2,1)S(1)}, bf16[640,256]{1,0:T(8,128)(2,1)S(1)}, u32[]{:S(2)}, u32[]{:S(2)}) %collective-permute-start.1) | collective-permute-done | bytes 327712 | tf_op jit(solution)/shard_map/ppermute | solution.py:309
  32.7 5.7 %collective-permute-done.refs_1_ = bf16[640,256]{1,0:T(8,128)(2,1)S(1)} collective-permute-done((bf16[640,256]{1,0:T(8,128)(2,1)S(1)}, bf16[640,256]{1,0:T(8,128)(2,1)S(1)}, u32[]{:S(2)}, u32[]{:S(2)}) %collective-permute-start) | collective-permute-done | bytes 327712 | tf_op jit(solution)/shard_map/ppermute | solution.py:308
  46.5 160.0 %place_pieces.1.refs_5_.refs_6_.images_ref = bf16[2560,1024]{1,0:T(8,128)(2,1)} custom-call(bf16[2560,128]{1,0:T(8,128)(2,1)} %refs_0_.3, bf16[2560,128]{1,0:T(8,128)(2,1)} %collective-permute-done.8.refs_1_, bf16[2560,128]{1,0:T(8,128)(2,1)} %copy-done.14, bf16[1280,128]{1,0:T(8,128)(2,1)} %copy-done.17, bf16[1280,128]{1,0:T(8,128)(2,1)} %collective-permute-done.11.refs_4_, ...), custom_call_target="tpu_custom_call" | custom-call | tf_op jit(solution)/shard_map/place_pieces/pallas_call | solution.py:58
  209.1 15.6 %logits_and_stats.2 = (f32[2560,640]{1,0:T(8,128)S(1)}, bf16[640,1024]{1,0:T(8,128)(2,1)S(1)}, f32[8,512]{1,0:T(8,128)S(1)}, f32[1,640]{1,0:T(1,128)S(1)}) custom-call(bf16[1280,256]{1,0:T(8,128)(2,1)S(1)} %copy-done.1, bf16[640,256]{1,0:T(8,128)(2,1)S(1)} %collective-permute-done.4.refs_1_, bf16[640,256]{1,0:T(8,128)(2,1)S(1)} %collective-permute-done.5.refs_2_, ...), custom_call_target="tpu_custom_call" | custom-call | flops 3355443200 | bytes 11796480 | tf_op jit(solution)/shard_map/logits_and_stats/pallas_call | solution.py:144
  224.7 10.0 %collective-permute-start.20 = (f32[1,640]{1,0:T(1,128)S(1)}, f32[1,640]{1,0:T(1,128)S(1)}, u32[]{:S(2)}, u32[]{:S(2)}) collective-permute-start(f32[1,640]{1,0:T(1,128)S(1)} %get-tuple-element.35), channel_id=1, source_target_pairs={{0,8},{8,0},{16,24},{24,16},{1,9},{9,1},{17,25},{25,17},{2,10},{10... | collective-permute-start | bytes 7688 | tf_op jit(solution)/shard_map/ppermute | solution.py:345
  234.7 15.6 %logits_and_stats.3 = (f32[2560,640]{1,0:T(8,128)S(1)}, bf16[640,1024]{1,0:T(8,128)(2,1)S(1)}, f32[8,512]{1,0:T(8,128)S(1)}, f32[1,640]{1,0:T(1,128)S(1)}) custom-call(bf16[1280,256]{1,0:T(8,128)(2,1)S(1)} %copy-done.1, bf16[640,256]{1,0:T(8,128)(2,1)S(1)} %collective-permute-done.refs_1_, bf16[640,256]{1,0:T(8,128)(2,1)S(1)} %collective-permute-done.1.refs_2_, ...), custom_call_target="tpu_custom_call" | custom-call | flops 3355443200 | bytes 11796480 | tf_op jit(solution)/shard_map/logits_and_stats/pallas_call | solution.py:144
  251.3 2.7 collective-permute-done.22
  259.2 2.6 collective-permute-done.19
  261.8 12.8 %weights_and_text_grad.3 = (bf16[2560,640]{1,0:T(8,128)(2,1)S(1)}, f32[1,640]{1,0:T(1,128)S(1)}, bf16[640,256]{1,0:T(8,128)(2,1)}, bf16[640,256]{1,0:T(8,128)(2,...) custom-call(f32[2560,640]{1,0:T(8,128)S(1)} %get-tuple-element.39.u_ref, ...), custom_call_target="tpu_custom_call" | custom-call | flops 3355443200 | bytes 11796480 | tf_op jit(solution)/shard_map/weights_and_text_grad/pallas_call | solution.py:220
  275.3 4.7 %collective-permute-start.36 = (bf16[640,256]{1,0:T(8,128)(2,1)}, bf16[640,256]{1,0:T(8,128)(2,1)}, u32[]{:S(2)}, u32[]{:S(2)}) collective-permute-start(bf16[640,256]{1,0:T(8,128)(2,1)} %get-tuple-element.61), channel_id=1, source_target_pairs={{0,8},{8,16},{1,9},{9,17},{2,10},{10,18},{3,11},{11,19},{4,12},{12... | collective-permute-start | bytes 983048 | tf_op jit(solution)/shard_map/ppermute | solution.py:363
  280.0 13.0 %weights_and_text_grad.2 = (bf16[2560,640]{1,0:T(8,128)(2,1)S(1)}, f32[1,640]{1,0:T(1,128)S(1)}, bf16[640,256]{1,0:T(8,128)(2,1)}, bf16[640,256]{1,0:T(8,128)(2,...) custom-call(f32[2560,640]{1,0:T(8,128)S(1)} %get-tuple-element.37.u_ref, ...), custom_call_target="tpu_custom_call" | custom-call | flops 3355443200 | bytes 11796480 | tf_op jit(solution)/shard_map/weights_and_text_grad/pallas_call | solution.py:220
  293.0 6.4 %image_grad_parts.3 = (bf16[1280,128]{1,0:T(8,128)(2,1)S(1)}, bf16[1280,128]{1,0:T(8,128)(2,1)S(1)}, bf16[1280,128]{1,0:T(8,128)(2,1)S(1)}, bf16[1280,128]{1,0:T(8,128)(2,1)S(1)}, bf16[1280,512]{1,0:T(8,128)(2,1)}) custom-call(bf16[2560,640]{1,0:T(8,128)(2,1)S(1)} %get-tuple-element.41.refs_0_, bf16[2560,640]{1,0:T(8,128)(2,1)S(1)} %get-tuple-element.42.refs_1_, ...), custom_call_target="tpu_custom_call" | custom-call | flops 3355443200 | bytes 9175040 | tf_op jit(solution)/shard_map/image_grad_parts/pallas_call | solution.py:265
  300.8 4.5 %collective-permute-start.32 = (bf16[640,256]{1,0:T(8,128)(2,1)}, bf16[640,256]{1,0:T(8,128)(2,1)}, u32[]{:S(2)}, u32[]{:S(2)}) collective-permute-start(bf16[640,256]{1,0:T(8,128)(2,1)} %get-tuple-element.57), channel_id=1, source_target_pairs={{0,8},{8,16},{1,9},{9,17},{2,10},{10,18},{3,11},{11,19},{4,12},{12... | collective-permute-start | bytes 983048 | tf_op jit(solution)/shard_map/ppermute | solution.py:363
  318.9 6.3 %image_grad_parts.2 = (bf16[1280,128]{1,0:T(8,128)(2,1)S(1)}, bf16[1280,128]{1,0:T(8,128)(2,1)S(1)}, bf16[1280,128]{1,0:T(8,128)(2,1)S(1)}, bf16[1280,128]{1,0:T(8,128)(2,1)S(1)}, bf16[1280,512]{1,0:T(8,128)(2,1)}) custom-call(bf16[2560,640]{1,0:T(8,128)(2,1)S(1)} %copy-done.9, bf16[2560,640]{1,0:T(8,128)(2,1)S(1)} %copy-done.7, ...), custom_call_target="tpu_custom_call" | custom-call | flops 3355443200 | bytes 9175040 | tf_op jit(solution)/shard_map/image_grad_parts/pallas_call | solution.py:265
  333.7 39.5 %psum.7 = f32[]{:T(128)} all-reduce(f32[]{:T(128)S(6)} %sub.67), channel_id=1, replica_groups=mesh['img'=4,'txt'=8] {'img','txt'}, use_global_device_ids=true, to_apply=%region_5.0 | all-reduce | flops 1 | bytes 8 | tf_op jit(solution)/shard_map/psum | solution.py:284
  382.9 3.1 collective-permute-done.29
  390.1 8.5 %collective-permute-done.26 = bf16[1280,128]{1,0:T(8,128)(2,1)S(1)} collective-permute-done((bf16[1280,128]{1,0:T(8,128)(2,1)S(1)}, bf16[1280,128]{1,0:T(8,128)(2,1)S(1)}, u32[]{:S(2)}, u32[]{:S(2)}) %collective-permute-start.26) | collective-permute-done | bytes 327712 | tf_op jit(solution)/shard_map/ppermute | solution.py:305
  399.7 2.7 collective-permute-done.30
  403.6 3.2 collective-permute-done.27
  (133 shorter events, 62.7 us)
Async XLA Ops:
  0.7 18.0 %collective-permute-start.9 = (bf16[2560,128]{1,0:T(8,128)(2,1)}, bf16[2560,128]{1,0:T(8,128)(2,1)S(1)}, u32[]{:S(2)}, u32[]{:S(2)}) collective-permute-start(bf16[2560,128]{1,0:T(8,128)(2,1)} %refs_0_.3), channel_id=1, source_target_pairs={{0,4},{1,5},{2,6},{3,7},{4,0},{5,1},{6,2},{7,3},{8,12},{9,13},{10,... | collective-permute-start | bytes 1966088 | tf_op jit(solution)/shard_map/ppermute | solution.py:305
  3.7 16.9 %collective-permute-start.8 = (bf16[2560,128]{1,0:T(8,128)(2,1)}, bf16[2560,128]{1,0:T(8,128)(2,1)}, u32[]{:S(2)}, u32[]{:S(2)}) collective-permute-start(bf16[2560,128]{1,0:T(8,128)(2,1)} %refs_0_.3), channel_id=1, source_target_pairs={{0,2},{1,3},{2,0},{3,1},{4,6},{5,7},{6,4},{7,5},{8,10},{9,11},{10,... | collective-permute-start | bytes 1966088 | tf_op jit(solution)/shard_map/ppermute | solution.py:305
  10.0 22.3 %collective-permute-start.1 = (bf16[640,256]{1,0:T(8,128)(2,1)S(1)}, bf16[640,256]{1,0:T(8,128)(2,1)S(1)}, u32[]{:S(2)}, u32[]{:S(2)}) collective-permute-start(bf16[640,256]{1,0:T(8,128)(2,1)S(1)} %get-tuple-element.72), channel_id=1, source_target_pairs={{0,24},{8,0},{16,8},{24,16},{1,25},{9,1},{17,9},{25,17},{2,26},{10... | collective-permute-start | bytes 983048 | tf_op jit(solution)/shard_map/ppermute | solution.py:309
  18.6 19.7 %collective-permute-start = (bf16[640,256]{1,0:T(8,128)(2,1)S(1)}, bf16[640,256]{1,0:T(8,128)(2,1)S(1)}, u32[]{:S(2)}, u32[]{:S(2)}) collective-permute-start(bf16[640,256]{1,0:T(8,128)(2,1)S(1)} %get-tuple-element.72), channel_id=1, source_target_pairs={{0,8},{8,16},{16,24},{24,0},{1,9},{9,17},{17,25},{25,1},{2,10},{10... | collective-permute-start | bytes 983048 | tf_op jit(solution)/shard_map/ppermute | solution.py:308
  20.5 18.9 %collective-permute-start.12 = (bf16[2560,128]{1,0:T(8,128)(2,1)S(1)}, bf16[2560,128]{1,0:T(8,128)(2,1)S(1)}, u32[]{:S(2)}, u32[]{:S(2)}) collective-permute-start(bf16[2560,128]{1,0:T(8,128)(2,1)S(1)} %copy-done.15), channel_id=1, source_target_pairs={{0,1},{1,0},{2,3},{3,2},{4,5},{5,4},{6,7},{7,6},{8,9},{9,8},{10,11... | collective-permute-start | bytes 1966088 | tf_op jit(solution)/shard_map/ppermute | solution.py:305
  20.6 17.8 %collective-permute-start.10 = (bf16[1280,128]{1,0:T(8,128)(2,1)S(1)}, bf16[1280,128]{1,0:T(8,128)(2,1)S(1)}, u32[]{:S(2)}, u32[]{:S(2)}) collective-permute-start(bf16[1280,128]{1,0:T(8,128)(2,1)S(1)} %slice.52), channel_id=1, source_target_pairs={{0,2},{1,3},{2,0},{3,1},{4,6},{5,7},{6,4},{7,5},{8,10},{9,11},{10,... | collective-permute-start | bytes 983048 | tf_op jit(solution)/shard_map/ppermute | solution.py:305
  26.1 17.3 %collective-permute-start.14 = (bf16[2560,128]{1,0:T(8,128)(2,1)S(1)}, bf16[2560,128]{1,0:T(8,128)(2,1)}, u32[]{:S(2)}, u32[]{:S(2)}) collective-permute-start(bf16[2560,128]{1,0:T(8,128)(2,1)S(1)} %collective-permute-done.9.refs_2_), channel_id=1, source_target_pairs={{0,1},{1,0},{2,3},{3,2},{4,5},{5,4},{6,7},{7,6},{8,9},{9,8},{10,11... | collective-permute-start | bytes 1966088 | tf_op jit(solution)/shard_map/ppermute | solution.py:305
  39.4 167.2 %collective-permute-start.7 = (bf16[640,256]{1,0:T(8,128)(2,1)S(1)}, bf16[640,256]{1,0:T(8,128)(2,1)}, u32[]{:S(2)}, u32[]{:S(2)}) collective-permute-start(bf16[640,256]{1,0:T(8,128)(2,1)S(1)} %collective-permute-done.5.refs_2_), channel_id=1, source_target_pairs={{8,0},{16,8},{9,1},{17,9},{10,2},{18,10},{11,3},{19,11},{12,4},{20... | collective-permute-start | bytes 983048 | tf_op jit(solution)/shard_map/ppermute | solution.py:310
  42.0 164.6 %collective-permute-start.6 = (bf16[640,256]{1,0:T(8,128)(2,1)S(1)}, bf16[640,256]{1,0:T(8,128)(2,1)}, u32[]{:S(2)}, u32[]{:S(2)}) collective-permute-start(bf16[640,256]{1,0:T(8,128)(2,1)S(1)} %collective-permute-done.4.refs_1_), channel_id=1, source_target_pairs={{8,16},{16,24},{9,17},{17,25},{10,18},{18,26},{11,19},{19,27},{12,... | collective-permute-start | bytes 983048 | tf_op jit(solution)/shard_map/ppermute | solution.py:310
  43.4 191.3 %collective-permute-start.3 = (bf16[640,256]{1,0:T(8,128)(2,1)S(1)}, bf16[640,256]{1,0:T(8,128)(2,1)}, u32[]{:S(2)}, u32[]{:S(2)}) collective-permute-start(bf16[640,256]{1,0:T(8,128)(2,1)S(1)} %collective-permute-done.1.refs_2_), channel_id=1, source_target_pairs={{8,0},{16,8},{9,1},{17,9},{10,2},{18,10},{11,3},{19,11},{12,4},{20... | collective-permute-start | bytes 983048 | tf_op jit(solution)/shard_map/ppermute | solution.py:310
  44.7 190.0 %collective-permute-start.2 = (bf16[640,256]{1,0:T(8,128)(2,1)S(1)}, bf16[640,256]{1,0:T(8,128)(2,1)}, u32[]{:S(2)}, u32[]{:S(2)}) collective-permute-start(bf16[640,256]{1,0:T(8,128)(2,1)S(1)} %collective-permute-done.refs_1_), channel_id=1, source_target_pairs={{8,16},{16,24},{9,17},{17,25},{10,18},{18,26},{11,19},{19,27},{12,... | collective-permute-start | bytes 983048 | tf_op jit(solution)/shard_map/ppermute | solution.py:310
  224.7 25.9 %collective-permute-start.20 = (f32[1,640]{1,0:T(1,128)S(1)}, f32[1,640]{1,0:T(1,128)S(1)}, u32[]{:S(2)}, u32[]{:S(2)}) collective-permute-start(f32[1,640]{1,0:T(1,128)S(1)} %get-tuple-element.35), channel_id=1, source_target_pairs={{0,8},{8,0},{16,24},{24,16},{1,9},{9,1},{17,25},{25,17},{2,10},{10... | collective-permute-start | bytes 7688 | tf_op jit(solution)/shard_map/ppermute | solution.py:345
  274.6 30.6 %collective-permute-start.38 = (bf16[640,256]{1,0:T(8,128)(2,1)}, bf16[640,256]{1,0:T(8,128)(2,1)S(1)}, u32[]{:S(2)}, u32[]{:S(2)}) collective-permute-start(bf16[640,256]{1,0:T(8,128)(2,1)} %get-tuple-element.61), channel_id=1, source_target_pairs={{24,16},{16,8},{25,17},{17,9},{26,18},{18,10},{27,19},{19,11},{28,... | collective-permute-start | bytes 983048 | tf_op jit(solution)/shard_map/ppermute | solution.py:364
  275.3 33.6 %collective-permute-start.36 = (bf16[640,256]{1,0:T(8,128)(2,1)}, bf16[640,256]{1,0:T(8,128)(2,1)}, u32[]{:S(2)}, u32[]{:S(2)}) collective-permute-start(bf16[640,256]{1,0:T(8,128)(2,1)} %get-tuple-element.61), channel_id=1, source_target_pairs={{0,8},{8,16},{1,9},{9,17},{2,10},{10,18},{3,11},{11,19},{4,12},{12... | collective-permute-start | bytes 983048 | tf_op jit(solution)/shard_map/ppermute | solution.py:363
  299.4 76.7 %collective-permute-start.28 = (bf16[1280,512]{1,0:T(8,128)(2,1)}, bf16[1280,512]{1,0:T(8,128)(2,1)}, u32[]{:S(2)}, u32[]{:S(2)}) collective-permute-start(bf16[1280,512]{1,0:T(8,128)(2,1)} %get-tuple-element.51), channel_id=1, source_target_pairs={{0,1},{1,0},{2,3},{3,2},{4,5},{5,4},{6,7},{7,6},{8,9},{9,8},{10,11... | collective-permute-start | bytes 3932168 | tf_op jit(solution)/shard_map/ppermute | solution.py:305
  299.4 25.8 %collective-permute-start.34 = (bf16[640,256]{1,0:T(8,128)(2,1)}, bf16[640,256]{1,0:T(8,128)(2,1)}, u32[]{:S(2)}, u32[]{:S(2)}) collective-permute-start(bf16[640,256]{1,0:T(8,128)(2,1)} %get-tuple-element.57), channel_id=1, source_target_pairs={{24,16},{16,8},{25,17},{17,9},{26,18},{18,10},{27,19},{19,11},{28,... | collective-permute-start | bytes 983048 | tf_op jit(solution)/shard_map/ppermute | solution.py:364
  300.8 26.4 %collective-permute-start.32 = (bf16[640,256]{1,0:T(8,128)(2,1)}, bf16[640,256]{1,0:T(8,128)(2,1)}, u32[]{:S(2)}, u32[]{:S(2)}) collective-permute-start(bf16[640,256]{1,0:T(8,128)(2,1)} %get-tuple-element.57), channel_id=1, source_target_pairs={{0,8},{8,16},{1,9},{9,17},{2,10},{10,18},{3,11},{11,19},{4,12},{12... | collective-permute-start | bytes 983048 | tf_op jit(solution)/shard_map/ppermute | solution.py:363
  306.1 25.0 %collective-permute-start.39 = (bf16[640,256]{1,0:T(8,128)(2,1)}, bf16[640,256]{1,0:T(8,128)(2,1)}, u32[]{:S(2)}, u32[]{:S(2)}) collective-permute-start(bf16[640,256]{1,0:T(8,128)(2,1)} %add.156), channel_id=1, source_target_pairs={{0,24},{8,0},{16,8},{24,16},{1,25},{9,1},{17,9},{25,17},{2,26},{10... | collective-permute-start | bytes 983048 | tf_op jit(solution)/shard_map/ppermute | solution.py:366
  310.7 63.2 %collective-permute-start.37 = (bf16[640,256]{1,0:T(8,128)(2,1)}, bf16[640,256]{1,0:T(8,128)(2,1)}, u32[]{:S(2)}, u32[]{:S(2)}) collective-permute-start(bf16[640,256]{1,0:T(8,128)(2,1)} %add.154), channel_id=1, source_target_pairs={{0,8},{8,16},{16,24},{24,0},{1,9},{9,17},{17,25},{25,1},{2,10},{10... | collective-permute-start | bytes 983048 | tf_op jit(solution)/shard_map/ppermute | solution.py:365
  325.2 54.5 %collective-permute-start.24 = (bf16[1280,512]{1,0:T(8,128)(2,1)}, bf16[1280,512]{1,0:T(8,128)(2,1)}, u32[]{:S(2)}, u32[]{:S(2)}) collective-permute-start(bf16[1280,512]{1,0:T(8,128)(2,1)} %get-tuple-element.46), channel_id=1, source_target_pairs={{0,1},{1,0},{2,3},{3,2},{4,5},{5,4},{6,7},{7,6},{8,9},{9,8},{10,11... | collective-permute-start | bytes 3932168 | tf_op jit(solution)/shard_map/ppermute | solution.py:305
  327.2 47.8 %collective-permute-start.35 = (bf16[640,256]{1,0:T(8,128)(2,1)}, bf16[640,256]{1,0:T(8,128)(2,1)S(1)}, u32[]{:S(2)}, u32[]{:S(2)}) collective-permute-start(bf16[640,256]{1,0:T(8,128)(2,1)} %add.152), channel_id=1, source_target_pairs={{0,24},{8,0},{16,8},{24,16},{1,25},{9,1},{17,9},{25,17},{2,26},{10... | collective-permute-start | bytes 983048 | tf_op jit(solution)/shard_map/ppermute | solution.py:366
  331.2 43.9 %collective-permute-start.33 = (bf16[640,256]{1,0:T(8,128)(2,1)}, bf16[640,256]{1,0:T(8,128)(2,1)S(1)}, u32[]{:S(2)}, u32[]{:S(2)}) collective-permute-start(bf16[640,256]{1,0:T(8,128)(2,1)} %add.150), channel_id=1, source_target_pairs={{0,8},{8,16},{16,24},{24,0},{1,9},{9,17},{17,25},{25,1},{2,10},{10... | collective-permute-start | bytes 983048 | tf_op jit(solution)/shard_map/ppermute | solution.py:365
  380.9 22.7 %collective-permute-start.25 = (bf16[1280,128]{1,0:T(8,128)(2,1)S(1)}, bf16[1280,128]{1,0:T(8,128)(2,1)S(1)}, u32[]{:S(2)}, u32[]{:S(2)}) collective-permute-start(bf16[1280,128]{1,0:T(8,128)(2,1)S(1)} %get-tuple-element.67), channel_id=1, source_target_pairs={{0,2},{1,3},{2,0},{3,1},{4,6},{5,7},{6,4},{7,5},{8,10},{9,11},{10,... | collective-permute-start | bytes 983048 | tf_op jit(solution)/shard_map/ppermute | solution.py:305
  381.4 17.1 %collective-permute-start.26 = (bf16[1280,128]{1,0:T(8,128)(2,1)S(1)}, bf16[1280,128]{1,0:T(8,128)(2,1)S(1)}, u32[]{:S(2)}, u32[]{:S(2)}) collective-permute-start(bf16[1280,128]{1,0:T(8,128)(2,1)S(1)} %get-tuple-element.68), channel_id=1, source_target_pairs={{0,2},{1,3},{2,0},{3,1},{4,6},{5,7},{6,4},{7,5},{8,10},{9,11},{10,... | collective-permute-start | bytes 983048 | tf_op jit(solution)/shard_map/ppermute | solution.py:305
  (36 other events, 550.8 us)

commit v2 on v1

v2 whole, which is shorter than its diff:
```python
import functools
import math
import jax
import jax.numpy as jnp
from jax import lax
from jax.experimental import pallas as pl
from jax.experimental.pallas import tpu as pltpu
from jax.sharding import PartitionSpec as P

logit_scale = 100.0
log2e = math.log2(math.e)
ln2 = math.log(2.0)
strip = 32
vmem_bytes = 28 * 1024 * 1024

VMEM = pl.BlockSpec(memory_space=pltpu.VMEM)


def block_rows(rows, most):
    size = most
    while rows % size:
        size //= 2
    return size


def columns(slot, width):
    return pl.ds(pl.multiple_of(slot * width, width), width)


def params():
    return pltpu.CompilerParams(vmem_limit_bytes=vmem_bytes)


def cost(rows, cols, depth, exps):
    return pl.CostEstimate(
        flops=2 * rows * cols * depth,
        bytes_accessed=rows * cols * 4 + rows * depth * 2,
        transcendentals=rows * cols * exps,
    )


def place_pieces(pieces, half, width):
    rows = pieces[0][0].shape[0]
    wide = pieces[0][0].shape[1]
    bm = block_rows(half, 256)
    near = half // bm
    arrays, specs = [], []
    for upper, lower, _ in pieces:
        if lower is None:
            arrays.append(upper)
            specs.append(pl.BlockSpec((bm, wide), lambda i: (i, 0)))
        else:
            arrays.append(upper)
            specs.append(pl.BlockSpec((bm, wide), lambda i: (jnp.minimum(i, near - 1), 0)))
            arrays.append(lower)
            specs.append(pl.BlockSpec((bm, wide), lambda i: (jnp.maximum(i - near, 0), 0)))

    def kernel(*refs):
        *sources, out = refs
        step = pl.program_id(0)
        at = 0
        for _, lower, slot in pieces:
            if lower is None:
                out[:, columns(slot(), wide)] = sources[at][...]
                at += 1
            else:
                out[:, columns(slot(), wide)] = jnp.where(step < near, sources[at][...], sources[at + 1][...])
                at += 2

    return pl.pallas_call(
        kernel,
        grid=(rows // bm,),
        out_shape=jax.ShapeDtypeStruct((rows, width), pieces[0][0].dtype),
        in_specs=specs,
        out_specs=pl.BlockSpec((bm, width), lambda i: (i, 0)),
        compiler_params=params(),
        name="place_pieces",
    )(*arrays)


def log_add(a, b):
    larger = jnp.maximum(a, b)
    return larger + jnp.log(jnp.exp2(a - larger) + jnp.exp2(b - larger)) * log2e


def lanes(x):
    return [x[:, k : k + 128] for k in range(0, x.shape[1], 128)]


def logits_and_stats(images, pieces, rows, earlier):
    img_rows, width = images.shape
    bm = block_rows(img_rows, 512)
    steps = img_rows // bm

    def kernel(*refs):
        sources = refs[: len(pieces)]
        refs = refs[len(pieces) :]
        if earlier is not None:
            earlier_ref, *refs = refs
        images_ref, u_ref, texts_ref, row_ref, col_ref, d_scr, rm_scr, rs_scr, cm_scr, cs_scr = refs
        step = pl.program_id(0)

        @pl.when(step == 0)
        def _():
            for source, (_, first, slot, condition) in zip(sources, pieces):

                def copy(source=source, first=first, slot=slot):
                    texts_ref[:, columns(slot(), source.shape[1])] = source[pl.ds(first, rows), :]

                if condition is None:
                    copy()
                else:
                    pl.when(condition())(copy)
            cm_scr[...] = jnp.full(cm_scr.shape, -jnp.inf, jnp.float32)
            cs_scr[...] = jnp.zeros(cs_scr.shape, jnp.float32)

        d_scr[...] = lax.dot_general(
            images_ref[...], texts_ref[...], (((1,), (1,)), ((), ())), preferred_element_type=jnp.float32
        )

        def first_pass(s, top):
            at = pl.ds(pl.multiple_of(s * strip, strip), strip)
            u = d_scr[at, :] * (logit_scale * log2e)
            u_ref[at, :] = u
            rm_scr[at, :] = functools.reduce(jnp.maximum, lanes(u))
            return jnp.maximum(top, jnp.max(u.reshape(strip // 8, 8, rows), axis=0))

        old = cm_scr[...]
        new = lax.fori_loop(0, bm // strip, first_pass, old, unroll=2)

        def second_pass(s, total):
            at = pl.ds(pl.multiple_of(s * strip, strip), strip)
            u = u_ref[at, :]
            row_max = rm_scr[at, :]
            rs_scr[at, :] = functools.reduce(jnp.add, [jnp.exp2(v - row_max) for v in lanes(u)])
            return total + jnp.sum(jnp.exp2(u.reshape(strip // 8, 8, rows) - new[None]), axis=0)

        total = lax.fori_loop(0, bm // strip, second_pass, cs_scr[...] * jnp.exp2(old - new), unroll=2)
        cm_scr[...] = new
        cs_scr[...] = total
        lane_max = rm_scr[...].T
        top_row = jnp.max(lane_max, axis=0, keepdims=True)
        row_sum = jnp.sum(rs_scr[...].T * jnp.exp2(lane_max - top_row), axis=0, keepdims=True)
        row_lse = top_row + jnp.log(row_sum) * log2e
        if earlier is not None:
            row_lse = log_add(row_lse, earlier_ref[pl.ds(step, 1), :])
        row_ref[pl.ds(step, 1), :] = row_lse

        @pl.when(step == steps - 1)
        def _():
            top = jnp.max(new, axis=0, keepdims=True)
            col_sum = jnp.sum(total * jnp.exp2(new - top), axis=0, keepdims=True)
            col_ref[...] = top + jnp.log(col_sum) * log2e

    return pl.pallas_call(
        kernel,
        grid=(steps,),
        out_shape=(
            jax.ShapeDtypeStruct((img_rows, rows), jnp.float32),
            jax.ShapeDtypeStruct((rows, width), jnp.bfloat16),
            jax.ShapeDtypeStruct((steps, bm), jnp.float32),
            jax.ShapeDtypeStruct((1, rows), jnp.float32),
        ),
        in_specs=[VMEM] * len(pieces)
        + ([] if earlier is None else [VMEM])
        + [pl.BlockSpec((bm, width), lambda i: (i, 0))],
        out_specs=(pl.BlockSpec((bm, rows), lambda i: (i, 0)), VMEM, VMEM, VMEM),
        scratch_shapes=[
            pltpu.VMEM((bm, rows), jnp.float32),
            pltpu.VMEM((bm, 128), jnp.float32),
            pltpu.VMEM((bm, 128), jnp.float32),
            pltpu.VMEM((8, rows), jnp.float32),
            pltpu.VMEM((8, rows), jnp.float32),
        ],
        compiler_params=params(),
        cost_estimate=cost(img_rows, rows, width, 2),
        name="logits_and_stats",
    )(*[p[0] for p in pieces], *([] if earlier is None else [earlier]), images)


def weights_and_text_grad(u, images, targets, row_lse, col_lse, first, parts):
    img_rows, width = images.shape
    rows = u.shape[1]
    bm = row_lse.shape[1]
    steps = img_rows // bm
    wide = width // len(parts)

    def kernel(u_ref, images_ref, targets_ref, row_ref, col_ref, w_ref, pos_ref, *refs):
        *part_refs, acc, row_scr, target_scr, pos_scr = refs
        step = pl.program_id(0)
        row_scr[...] = jnp.broadcast_to(row_ref[pl.ds(step, 1), :], (128, bm)).T
        target_scr[...] = jnp.broadcast_to(targets_ref[pl.ds(step, 1), :] - first, (128, bm)).T

        @pl.when(step == 0)
        def _():
            pos_scr[...] = jnp.zeros(pos_scr.shape, jnp.float32)

        ids = lax.broadcasted_iota(jnp.int32, (strip, 128), 1)
        col = col_ref[...]

        def one(s, picked):
            at = pl.ds(pl.multiple_of(s * strip, strip), strip)
            row = row_scr[at, :]
            target = target_scr[at, :] - ids
            for k in range(0, rows, 128):
                v = u_ref[at, k : k + 128]
                matches = target == k
                weight = jnp.exp2(v - row) + jnp.exp2(v - col[:, k : k + 128]) - jnp.where(matches, 2.0, 0.0)
                w_ref[at, k : k + 128] = weight.astype(jnp.bfloat16)
                picked = picked + jnp.where(matches, v, 0.0)
            return picked

        pos_scr[...] = lax.fori_loop(0, bm // strip, one, pos_scr[...], unroll=2)
        term = lax.dot_general(
            w_ref[...], images_ref[...], (((0,), (0,)), ((), ())), preferred_element_type=jnp.float32
        )

        @pl.when(step == 0)
        def _():
            acc[...] = term

        @pl.when(step > 0)
        def _():
            acc[...] += term

        @pl.when(step == steps - 1)
        def _():
            for ref, slot in zip(part_refs, parts):
                ref[...] = (logit_scale * acc[:, columns(slot(), wide)]).astype(jnp.bfloat16)
            pos_ref[...] = jnp.sum(pos_scr[...], axis=0, keepdims=True)

    return pl.pallas_call(
        kernel,
        grid=(steps,),
        out_shape=(
            jax.ShapeDtypeStruct((img_rows, rows), jnp.bfloat16),
            jax.ShapeDtypeStruct((1, 128), jnp.float32),
        )
        + (jax.ShapeDtypeStruct((rows, wide), jnp.bfloat16),) * len(parts),
        in_specs=[
            pl.BlockSpec((bm, rows), lambda i: (i, 0)),
            pl.BlockSpec((bm, width), lambda i: (i, 0)),
            VMEM,
            VMEM,
            VMEM,
        ],
        out_specs=(pl.BlockSpec((bm, rows), lambda i: (i, 0)), VMEM) + (VMEM,) * len(parts),
        scratch_shapes=[
            pltpu.VMEM((rows, width), jnp.float32),
            pltpu.VMEM((bm, 128), jnp.float32),
            pltpu.VMEM((bm, 128), jnp.int32),
            pltpu.VMEM((strip, 128), jnp.float32),
        ],
        compiler_params=params(),
        cost_estimate=cost(img_rows, rows, width, 2),
        name="weights_and_text_grad",
    )(u, images, targets, row_lse, col_lse)


def image_grad_parts(weights, texts, first, img_rows, groups):
    width = texts[0].shape[1]
    rows = sum(t.shape[0] for t in texts)
    bm = block_rows(math.gcd(first, img_rows) if first else img_rows, 256)
    wide = width // sum(len(g) for g in groups)

    def kernel(*refs):
        w_refs = refs[: len(weights)]
        t_refs = refs[len(weights) : 2 * len(weights)]
        *outs, acc = refs[2 * len(weights) :]
        total = jnp.dot(w_refs[0][...], t_refs[0][...], preferred_element_type=jnp.float32)
        for w_ref, t_ref in zip(w_refs[1:], t_refs[1:]):
            total += jnp.dot(w_ref[...], t_ref[...], preferred_element_type=jnp.float32)
        acc[...] = logit_scale * total
        for out, group in zip(outs, groups):
            for k, slot in enumerate(group):
                out[:, k * wide : (k + 1) * wide] = acc[:, columns(slot(), wide)].astype(jnp.bfloat16)

    return pl.pallas_call(
        kernel,
        grid=(img_rows // bm,),
        out_shape=tuple(jax.ShapeDtypeStruct((img_rows, wide * len(g)), jnp.bfloat16) for g in groups),
        in_specs=[pl.BlockSpec((bm, w.shape[1]), lambda i: (i + first // bm, 0)) for w in weights]
        + [VMEM] * len(weights),
        out_specs=tuple(pl.BlockSpec((bm, wide * len(g)), lambda i: (i, 0)) for g in groups),
        scratch_shapes=[pltpu.VMEM((bm, width), jnp.float32)],
        compiler_params=params(),
        cost_estimate=cost(img_rows, rows, width, 0),
        name="image_grad_parts",
    )(*weights, *texts)


def loss_terms(row_lse, col_lses, picked, n_img, n_txt):
    pos = sum(jnp.sum(p) for p in picked)
    return jnp.sum(row_lse) / n_txt + sum(jnp.sum(c) for c in col_lses) / n_img - 2.0 * pos


def chunk_rows(rows):
    units = rows // 256
    first = (units + 1) // 2 * 256 if rows % 256 == 0 and units > 1 else rows // 2
    return first, rows - first


def shifted(count, by, wrap):
    return [(i, (i + by) % count) for i in range(count) if wrap or 0 <= i + by < count]


def paired(count, by):
    return [(i, i ^ by) for i in range(count)]


def per_device_4x8(images, texts, positive):
    img_rows = images.shape[0]
    txt_rows, quarter = texts.shape
    width = quarter * 4
    chunks = chunk_rows(txt_rows)
    firsts = (0, chunks[0])
    up_ring, down_ring = shifted(4, 1, True), shifted(4, -1, True)
    up_line, down_line = [(1, 2), (2, 3)], [(1, 0), (2, 1)]

    def swap(part, by):
        return lax.ppermute(part, "txt", paired(8, by))

    def z_gather(part):
        prev = lax.ppermute(part, "img", up_ring)
        following = lax.ppermute(part, "img", down_ring)
        return prev, following, lax.ppermute(prev, "img", up_line), lax.ppermute(following, "img", down_line)

    gathered = [z_gather(texts[f : f + c]) for f, c in zip(firsts, chunks)]
    image_half = img_rows // 2
    from_x, from_y = swap(images, 2), swap(images, 4)
    diag_x, diag_y = swap(from_y[:image_half], 2), swap(from_x[image_half:], 4)
    mine = [(images, None, 0), (from_x, None, 2), (from_y, None, 4), (diag_x, diag_y, 6)]
    pieces = mine + [
        (swap(upper, 1), None if lower is None else swap(lower, 1), flip ^ 1) for upper, lower, flip in mine
    ]

    def txt_slot(flip):
        return lambda: lax.axis_index("txt") ^ flip

    def img_slot(by):
        return lambda: lax.rem(lax.axis_index("img") + by, 4)

    def upper():
        return lax.axis_index("img") >= 2

    def lower():
        return lax.axis_index("img") < 2

    whole_img = place_pieces([(a, b, txt_slot(flip)) for a, b, flip in pieces], image_half, width)

    def text_pieces(k):
        prev, following, up, down = gathered[k]
        return [
            (texts, firsts[k], img_slot(0), None),
            (prev, 0, img_slot(3), None),
            (following, 0, img_slot(1), None),
            (up, 0, img_slot(2), upper),
            (down, 0, img_slot(2), lower),
        ]

    def over_img(col):
        col = log_add(col, lax.ppermute(col, "img", paired(4, 1)))
        return log_add(col, lax.ppermute(col, "img", paired(4, 2)))

    u0, texts0, row, col0 = logits_and_stats(whole_img, text_pieces(0), chunks[0], None)
    col0 = over_img(col0)
    u1, texts1, row, col1 = logits_and_stats(whole_img, text_pieces(1), chunks[1], row)
    for by in (1, 2, 4):
        row = log_add(row, swap(row, by))
    col1 = over_img(col1)

    targets = (positive - lax.axis_index("txt") * txt_rows).reshape(row.shape)
    text_slots = [img_slot(2), img_slot(1), img_slot(3), img_slot(0)]
    weights, picked, text_parts = [], [], []
    for k, (u, col) in enumerate(((u0, col0), (u1, col1))):
        w, pos, opposite, following, prev, own = weights_and_text_grad(
            u, whole_img, targets, row, col, firsts[k], text_slots
        )
        weights.append(w)
        picked.append(pos)
        from_below = lax.ppermute(opposite, "img", [(0, 1), (1, 2)])
        from_above = lax.ppermute(opposite, "img", [(3, 2), (2, 1)])
        from_prev = lax.ppermute(following + from_below, "img", up_ring)
        from_next = lax.ppermute(prev + from_above, "img", down_ring)
        text_parts.append(
            (own.astype(jnp.float32) + from_prev.astype(jnp.float32) + from_next.astype(jnp.float32)).astype(
                jnp.bfloat16
            )
        )
    text_grad = jnp.concatenate(text_parts, axis=0)
    loss = loss_terms(row, (col0, col1), picked, 4, 8)[None]
    for by in (1, 2, 4):
        loss += swap(loss, by)
    for by in (1, 2):
        loss += lax.ppermute(loss, "img", paired(4, by))
    mean_loss = loss[0] * (ln2 / (2.0 * txt_rows * 8))

    kept = [[txt_slot(0)], [txt_slot(2)], [txt_slot(4)], [txt_slot(6)]]
    sent = [txt_slot(flip) for flip in (1, 3, 5, 7)]
    sums = []
    eighth = width // 8
    for k in range(2):
        *own, other = image_grad_parts(weights, (texts0, texts1), k * image_half, image_half, kept + [sent])
        other = swap(other, 1)
        sums.append([own[j] + other[:, j * eighth : (j + 1) * eighth] for j in range(4)])
    (s0, x0, y0, d0), (s1, x1, y1, d1) = sums
    d0 = swap(d0, 2)
    d1 = swap(d1, 4)
    image_parts = []
    for s, x, y in ((s0, x0, y0 + d0), (s1, x1 + d1, y1)):
        x, y = swap(x, 2), swap(y, 4)
        image_parts.append(
            (s.astype(jnp.float32) + x.astype(jnp.float32) + y.astype(jnp.float32)).astype(jnp.bfloat16)
        )
    return mean_loss, jnp.concatenate(image_parts, axis=0), text_grad


def per_device(images, texts, positive):
    n_img, n_txt = lax.axis_size("img"), lax.axis_size("txt")
    if (n_img, n_txt) == (4, 8):
        return per_device_4x8(images, texts, positive)
    whole_img = lax.all_gather(images, "txt", axis=1, tiled=True)
    whole_txt = lax.all_gather(texts, "img", axis=1, tiled=True)
    img_rows = whole_img.shape[0]
    txt_rows = whole_txt.shape[0]
    sizes = chunk_rows(txt_rows)
    firsts = (0, sizes[0])

    def merged(part, axis):
        every = lax.all_gather(part, axis)
        top = jnp.max(every, axis=0)
        return top + jnp.log(jnp.sum(jnp.exp2(every - top), axis=0)) * log2e

    def first_slot():
        return jnp.int32(0)

    row, logits, chunks, cols = None, [], [], []
    for k in range(2):
        u, chunk, row, col = logits_and_stats(whole_img, [(whole_txt, firsts[k], first_slot, None)], sizes[k], row)
        logits.append(u)
        chunks.append(chunk)
        cols.append(merged(col, "img"))
    row = merged(row, "txt")
    targets = (positive - lax.axis_index("txt") * txt_rows).reshape(row.shape)
    weights, picked, text_parts = [], [], []
    for k in range(2):
        w, pos, part = weights_and_text_grad(logits[k], whole_img, targets, row, cols[k], firsts[k], [first_slot])
        weights.append(w)
        picked.append(pos)
        text_parts.append(part)
    (image_part,) = image_grad_parts(weights, chunks, 0, img_rows, [[first_slot]])
    loss = lax.psum(loss_terms(row, cols, picked, n_img, n_txt), ("img", "txt"))
    mean_loss = loss * (ln2 / (2.0 * txt_rows * n_txt))
    image_grad = lax.psum_scatter(image_part, "txt", scatter_dimension=1, tiled=True)
    text_grad = lax.psum_scatter(jnp.concatenate(text_parts, axis=0), "img", scatter_dimension=1, tiled=True)
    return mean_loss, image_grad, text_grad


def solution(mesh):
    placed = (P("img", "txt"), P("txt", "img"), P("img"))
    return jax.shard_map(
        per_device,
        mesh=mesh,
        in_specs=placed,
        out_specs=(P(), P("img", "txt"), P("txt", "img")),
        check_vma=False,
    )
```

time: 411 us -> 242 us (0.59)
  Pallas kernels: 230 us -> 55.3 us
  blocking collectives: 39.5 us -> 0 us
  waiting for transfers between devices: 46.1 us -> 74.2 us
  local copies, waits for them, and re-layouts: 12.3 us -> 26.7 us
  other arithmetic: 19.2 us -> 8.19 us
  starting transfers between devices: 57.1 us -> 67.5 us
    pallas_call x1, Pallas kernels: 160 us -> 5.48 us  [place_pieces(): pl.pallas_call(kernel, grid=(rows // bm,), out_shape=jax.ShapeDtypeStruct...]
    psum x1 -> x0, blocking collectives: 39.5 us -> none  [loss_of(): lax.psum(row_term / n_txt + col_term / n_img - 2.0 * pos, ('img', 'txt'))]
    unnamed x40 -> x52, local copies, waits for them, and re-layouts: 9.77 us -> 24.7 us
    pallas_call x2, Pallas kernels: 31.2 us -> 20.9 us  [logits_and_stats(): pl.pallas_call(kernel, grid=(steps,), out_shape=(jax.ShapeDtypeStruct((im...]
    ppermute x2, waiting for transfers between devices: 0.01 us -> 9.6 us  [per_device_4x8(): from_prev = lax.ppermute(following + from_below, 'img', up_ring)]
    ppermute x20 -> x23, waiting for transfers between devices: 28 us -> 37.5 us  [swap(): return lax.ppermute(part, 'txt', paired(8, by))]
    ppermute x2, waiting for transfers between devices: 0.01 us -> 7.9 us  [per_device_4x8(): from_next = lax.ppermute(prev + from_above, 'img', down_ring)]
    ppermute x2, waiting for transfers between devices: 8.64 us -> 16.1 us  [z_gather(): prev = lax.ppermute(part, 'img', up_ring)]
  transfers between devices with their start and end apart: 40 -> 45, of which waited for: 15 -> 19; matrix products, arithmetic and copies ran while one was open for 5% -> 4% of each run, Pallas kernels for 53% -> 16%
where the time goes in v2:
time: 242 us; the launch traced here: 241 us
  waiting for transfers between devices  74.2 us (31%)
  starting transfers between devices  67.5 us (28%)
  Pallas kernels  55.3 us (23%)
  local copies, waits for them, and re-layouts  26.7 us (11%)
  between operations  8.96 us (4%)
  other arithmetic  8.19 us (3%)
    ppermute x23, waiting for transfers between devices, swap(): return lax.ppermute(part, 'txt', paired(8, by))  37.5 us
    unnamed x52, local copies, waits for them, and re-layouts  24.7 us
    pallas_call x2, Pallas kernels, logits_and_stats(): pl.pallas_call(kernel, grid=(steps,), out_shape=(jax.ShapeDtypeStruct((im...  20.9 us
    pallas_call x2, Pallas kernels, weights_and_text_grad(): pl.pallas_call(kernel, grid=(steps,), out_shape=(jax.ShapeDtypeStruct((im...  19 us
    ppermute x23, starting transfers between devices, swap(): return lax.ppermute(part, 'txt', paired(8, by))  18.6 us
    ppermute x2, waiting for transfers between devices, z_gather(): prev = lax.ppermute(part, 'img', up_ring)  16.1 us
    pallas_call x2, Pallas kernels, image_grad_parts(): pl.pallas_call(kernel, grid=(img_rows // bm,), out_shape=tuple((jax.Shape...  9.89 us
    ppermute x2, waiting for transfers between devices, per_device_4x8(): from_prev = lax.ppermute(following + from_below, 'img', up_ring)  9.6 us
  transfers between devices with their start and end apart: 45, of which 19 were waited for; matrix products, arithmetic and copies ran while one was open for 4% of the time, Pallas kernels for 16%

profile of v2, /device:TPU:0, one launch (start us, length us, event | category | flops | bytes accessed | tf_op | source)
XLA Modules:
  0.0 240.8 jit_solution(1811702188406777860)
XLA Ops:
  0.6 3.0 %collective-permute-start.9 = (bf16[2560,128]{1,0:T(8,128)(2,1)}, bf16[2560,128]{1,0:T(8,128)(2,1)S(1)}, u32[]{:S(2)}, u32[]{:S(2)}) collective-permute-start(bf16[2560,128]{1,0:T(8,128)(2,1)} %refs_0_.3), channel_id=1, source_target_pairs={{0,4},{1,5},{2,6},{3,7},{4,0},{5,1},{6,2},{7,3},{8,12},{9,13},{10,... | collective-permute-start | bytes 1966088 | tf_op jit(solution)/shard_map/ppermute | solution.py:321
  6.1 3.7 %collective-permute-start.1 = (bf16[512,256]{1,0:T(8,128)(2,1)S(1)}, bf16[512,256]{1,0:T(8,128)(2,1)S(1)}, u32[]{:S(2)}, u32[]{:S(2)}) collective-permute-start(bf16[512,256]{1,0:T(8,128)(2,1)S(1)} %slice.36), channel_id=1, source_target_pairs={{0,24},{8,0},{16,8},{24,16},{1,25},{9,1},{17,9},{25,17},{2,26},{10... | collective-permute-start | bytes 786440 | tf_op jit(solution)/shard_map/ppermute | solution.py:325
  12.9 5.7 %collective-permute-done.9.refs_2_ = bf16[2560,128]{1,0:T(8,128)(2,1)S(1)} collective-permute-done((bf16[2560,128]{1,0:T(8,128)(2,1)}, bf16[2560,128]{1,0:T(8,128)(2,1)S(1)}, u32[]{:S(2)}, u32[]{:S(2)}) %collective-permute-start.9) | collective-permute-done | bytes 655392 | tf_op jit(solution)/shard_map/ppermute | solution.py:321
  22.0 16.1 %collective-permute-done.refs_1_ = bf16[512,256]{1,0:T(8,128)(2,1)S(1)} collective-permute-done((bf16[512,256]{1,0:T(8,128)(2,1)S(1)}, bf16[512,256]{1,0:T(8,128)(2,1)S(1)}, u32[]{:S(2)}, u32[]{:S(2)}) %collective-permute-start) | collective-permute-done | bytes 262176 | tf_op jit(solution)/shard_map/ppermute | solution.py:324
  41.3 5.0 %collective-permute-done.11.refs_4_ = bf16[1280,128]{1,0:T(8,128)(2,1)} collective-permute-done((bf16[1280,128]{1,0:T(8,128)(2,1)S(1)}, bf16[1280,128]{1,0:T(8,128)(2,1)}, u32[]{:S(2)}, u32[]{:S(2)}) %collective-permute-start.11) | collective-permute-done | bytes 327712 | tf_op jit(solution)/shard_map/ppermute | solution.py:321
  53.0 5.5 %place_pieces.1.refs_5_.refs_6_.images_ref = bf16[2560,1024]{1,0:T(8,128)(2,1)S(1)} custom-call(bf16[2560,128]{1,0:T(8,128)(2,1)S(1)} %copy-done.4, bf16[2560,128]{1,0:T(8,128)(2,1)S(1)} %collective-permute-done.8.refs_1_, bf16[2560,128]{1,0:T(8,128)(2,1)S(1)} %collective-permute-done.9.refs_2_, bf16[1280,128]{1,0:T(8,128)(2,1)S(1)} %copy-done.7, ...), custom_call_target="tpu_custom_call" | custom-call | tf_op jit(solution)/shard_map/place_pieces/pallas_call | solution.py:70
  58.5 13.0 %logits_and_stats.2 = (f32[2560,768]{1,0:T(8,128)S(1)}, bf16[768,1024]{1,0:T(8,128)(2,1)S(1)}, f32[5,512]{1,0:T(8,128)S(1)}, f32[1,768]{1,0:T(1,128)S(1)}) custom-call(bf16[1280,256]{1,0:T(8,128)(2,1)S(1)} %copy-done.5, bf16[768,256]{1,0:T(8,128)(2,1)} %collective-permute-done.4.refs_1_, bf16[768,256]{1,0:T(8,128)(2,1)} %collective-permute-done.5.refs_2_, ...), custom_call_target="tpu_custom_call" | custom-call | flops 4026531840 | bytes 13107200 | tf_op jit(solution)/shard_map/logits_and_stats/pallas_call | solution.py:155
  71.6 3.1 %copy-done.14 = f32[2560,768]{1,0:T(8,128)} copy-done((f32[2560,768]{1,0:T(8,128)}, f32[2560,768]{1,0:T(8,128)S(1)}, u32[]{:S(2)}) %copy-start.14) | copy-done | bytes 7864344
  74.7 7.9 %logits_and_stats.3 = (f32[2560,512]{1,0:T(8,128)S(1)}, bf16[512,1024]{1,0:T(8,128)(2,1)S(1)}, f32[5,512]{1,0:T(8,128)S(1)}, f32[1,512]{1,0:T(1,128)S(1)}) custom-call(bf16[1280,256]{1,0:T(8,128)(2,1)S(1)} %copy-done.5, bf16[512,256]{1,0:T(8,128)(2,1)S(1)} %copy-done.13, bf16[512,256]{1,0:T(8,128)(2,1)S(1)} %collective-permute-done.1.refs_2_, ...), custom_call_target="tpu_custom_call" | custom-call | flops 2684354560 | bytes 10485760 | tf_op jit(solution)/shard_map/logits_and_stats/pallas_call | solution.py:155
  85.8 9.4 %collective-permute-start.22 = (f32[1,512]{1,0:T(1,128)S(1)}, f32[1,512]{1,0:T(1,128)S(1)}, u32[]{:S(2)}, u32[]{:S(2)}) collective-permute-start(f32[1,512]{1,0:T(1,128)S(1)} %get-tuple-element.36), channel_id=1, source_target_pairs={{0,8},{8,0},{16,24},{24,16},{1,9},{9,1},{17,25},{25,17},{2,10},{10... | collective-permute-start | bytes 6152 | tf_op jit(solution)/shard_map/ppermute | solution.py:362
  113.2 8.1 %weights_and_text_grad.3 = (bf16[2560,512]{1,0:T(8,128)(2,1)S(1)}, f32[1,128]{1,0:T(1,128)S(1)}, bf16[512,256]{1,0:T(8,128)(2,1)S(1)}, bf16[512,256]{1,0:T(8,128...) custom-call(f32[2560,512]{1,0:T(8,128)S(1)} %copy-done.3, bf16[2560,1024]{1,0:T(8,128)(2,1)S(1)} %copy-done.1, ...), custom_call_target="tpu_custom_call" | custom-call | flops 2684354560 | bytes 10485760 | tf_op jit(solution)/shard_map/weights_and_text_grad/pallas_call | solution.py:232
  124.1 4.6 %collective-permute-start.41 = (bf16[512,256]{1,0:T(8,128)(2,1)S(1)}, bf16[512,256]{1,0:T(8,128)(2,1)}, u32[]{:S(2)}, u32[]{:S(2)}) collective-permute-start(bf16[512,256]{1,0:T(8,128)(2,1)S(1)} %get-tuple-element.61), channel_id=1, source_target_pairs={{0,8},{8,16},{1,9},{9,17},{2,10},{10,18},{3,11},{11,19},{4,12},{12... | collective-permute-start | bytes 786440 | tf_op jit(solution)/shard_map/ppermute | solution.py:381
  128.7 11.0 %weights_and_text_grad.2 = (bf16[2560,768]{1,0:T(8,128)(2,1)S(1)}, f32[1,128]{1,0:T(1,128)S(1)}, bf16[768,256]{1,0:T(8,128)(2,1)S(1)}, bf16[768,256]{1,0:T(8,128...) custom-call(f32[2560,768]{1,0:T(8,128)S(1)} %copy-done.15, bf16[2560,1024]{1,0:T(8,128)(2,1)S(1)} %copy-done.1, ...), custom_call_target="tpu_custom_call" | custom-call | flops 4026531840 | bytes 13107200 | tf_op jit(solution)/shard_map/weights_and_text_grad/pallas_call | solution.py:232
  142.3 4.5 %collective-permute-start.37 = (bf16[768,256]{1,0:T(8,128)(2,1)S(1)}, bf16[768,256]{1,0:T(8,128)(2,1)S(1)}, u32[]{:S(2)}, u32[]{:S(2)}) collective-permute-start(bf16[768,256]{1,0:T(8,128)(2,1)S(1)} %get-tuple-element.57), channel_id=1, source_target_pairs={{0,8},{8,16},{1,9},{9,17},{2,10},{10,18},{3,11},{11,19},{4,12},{12... | collective-permute-start | bytes 1179656 | tf_op jit(solution)/shard_map/ppermute | solution.py:381
  157.3 4.9 %image_grad_parts.3 = (bf16[1280,128]{1,0:T(8,128)(2,1)S(1)}, bf16[1280,128]{1,0:T(8,128)(2,1)S(1)}, bf16[1280,128]{1,0:T(8,128)(2,1)S(1)}, bf16[1280,128]{1,0:T(8,128)(2,1)S(1)}, bf16[1280,512]{1,0:T(8,128)(2,1)S(1)}) custom-call(bf16[2560,768]{1,0:T(8,128)(2,1)S(1)} %copy-done.17, bf16[2560,512]{1,0:T(8,128)(2,1)S(1)} %copy-done.11, ...), custom_call_target="tpu_custom_call" | custom-call | flops 3355443200 | bytes 9175040 | tf_op jit(solution)/shard_map/image_grad_parts/pallas_call | solution.py:278
  171.5 4.0 %collective-permute-start.27 = (f32[1]{0:T(128)}, f32[1]{0:T(128)}, u32[]{:S(2)}, u32[]{:S(2)}) collective-permute-start(f32[1]{0:T(128)} %add.151), channel_id=1, source_target_pairs={{0,8},{8,0},{16,24},{24,16},{1,9},{9,1},{17,25},{25,17},{2,10},{10... | collective-permute-start | bytes 20 | tf_op jit(solution)/shard_map/ppermute | solution.py:395
  179.7 3.6 %collective-permute-start.44 = (bf16[512,256]{1,0:T(8,128)(2,1)S(1)}, bf16[512,256]{1,0:T(8,128)(2,1)S(1)}, u32[]{:S(2)}, u32[]{:S(2)}) collective-permute-start(bf16[512,256]{1,0:T(8,128)(2,1)S(1)} %add.174), channel_id=1, source_target_pairs={{0,24},{8,0},{16,8},{24,16},{1,25},{9,1},{17,9},{25,17},{2,26},{10... | collective-permute-start | bytes 786440 | tf_op jit(solution)/shard_map/ppermute | solution.py:384
  184.5 3.9 %collective-permute-start.40 = (bf16[768,256]{1,0:T(8,128)(2,1)S(1)}, bf16[768,256]{1,0:T(8,128)(2,1)S(1)}, u32[]{:S(2)}, u32[]{:S(2)}) collective-permute-start(bf16[768,256]{1,0:T(8,128)(2,1)S(1)} %add.170), channel_id=1, source_target_pairs={{0,24},{8,0},{16,8},{24,16},{1,25},{9,1},{17,9},{25,17},{2,26},{10... | collective-permute-start | bytes 1179656 | tf_op jit(solution)/shard_map/ppermute | solution.py:384
  188.6 5.0 %image_grad_parts.2 = (bf16[1280,128]{1,0:T(8,128)(2,1)S(1)}, bf16[1280,128]{1,0:T(8,128)(2,1)S(1)}, bf16[1280,128]{1,0:T(8,128)(2,1)S(1)}, bf16[1280,128]{1,0:T(8,128)(2,1)S(1)}, bf16[1280,512]{1,0:T(8,128)(2,1)S(1)}) custom-call(bf16[2560,768]{1,0:T(8,128)(2,1)S(1)} %copy-done.18, bf16[2560,512]{1,0:T(8,128)(2,1)S(1)} %copy-done.11, ...), custom_call_target="tpu_custom_call" | custom-call | flops 3355443200 | bytes 9175040 | tf_op jit(solution)/shard_map/image_grad_parts/pallas_call | solution.py:278
  196.2 7.9 %collective-permute-done.40 = bf16[768,256]{1,0:T(8,128)(2,1)S(1)} collective-permute-done((bf16[768,256]{1,0:T(8,128)(2,1)S(1)}, bf16[768,256]{1,0:T(8,128)(2,1)S(1)}, u32[]{:S(2)}, u32[]{:S(2)}) %collective-permute-start.40) | collective-permute-done | bytes 393248 | tf_op jit(solution)/shard_map/ppermute | solution.py:384
  204.1 7.8 %collective-permute-done.38 = bf16[768,256]{1,0:T(8,128)(2,1)S(1)} collective-permute-done((bf16[768,256]{1,0:T(8,128)(2,1)S(1)}, bf16[768,256]{1,0:T(8,128)(2,1)S(1)}, u32[]{:S(2)}, u32[]{:S(2)}) %collective-permute-start.38) | collective-permute-done | bytes 393248 | tf_op jit(solution)/shard_map/ppermute | solution.py:383
  215.8 6.0 %collective-permute-done.34 = bf16[1280,128]{1,0:T(8,128)(2,1)S(1)} collective-permute-done((bf16[1280,128]{1,0:T(8,128)(2,1)S(1)}, bf16[1280,128]{1,0:T(8,128)(2,1)S(1)}, u32[]{:S(2)}, u32[]{:S(2)}) %collective-permute-start.34) | collective-permute-done | bytes 327712 | tf_op jit(solution)/shard_map/ppermute | solution.py:321
  223.0 8.4 %collective-permute-done.31 = bf16[1280,128]{1,0:T(8,128)(2,1)S(1)} collective-permute-done((bf16[1280,128]{1,0:T(8,128)(2,1)S(1)}, bf16[1280,128]{1,0:T(8,128)(2,1)S(1)}, u32[]{:S(2)}, u32[]{:S(2)}) %collective-permute-start.31) | collective-permute-done | bytes 327712 | tf_op jit(solution)/shard_map/ppermute | solution.py:321
  233.1 3.1 %collective-permute-done.35 = bf16[1280,128]{1,0:T(8,128)(2,1)S(1)} collective-permute-done((bf16[1280,128]{1,0:T(8,128)(2,1)S(1)}, bf16[1280,128]{1,0:T(8,128)(2,1)S(1)}, u32[]{:S(2)}, u32[]{:S(2)}) %collective-permute-start.35) | collective-permute-done | bytes 327712 | tf_op jit(solution)/shard_map/ppermute | solution.py:321
  (154 shorter events, 76.8 us)
Async XLA Ops:
  0.6 18.0 %collective-permute-start.9 = (bf16[2560,128]{1,0:T(8,128)(2,1)}, bf16[2560,128]{1,0:T(8,128)(2,1)S(1)}, u32[]{:S(2)}, u32[]{:S(2)}) collective-permute-start(bf16[2560,128]{1,0:T(8,128)(2,1)} %refs_0_.3), channel_id=1, source_target_pairs={{0,4},{1,5},{2,6},{3,7},{4,0},{5,1},{6,2},{7,3},{8,12},{9,13},{10,... | collective-permute-start | bytes 1966088 | tf_op jit(solution)/shard_map/ppermute | solution.py:321
  3.7 16.8 %collective-permute-start.8 = (bf16[2560,128]{1,0:T(8,128)(2,1)}, bf16[2560,128]{1,0:T(8,128)(2,1)S(1)}, u32[]{:S(2)}, u32[]{:S(2)}) collective-permute-start(bf16[2560,128]{1,0:T(8,128)(2,1)} %refs_0_.3), channel_id=1, source_target_pairs={{0,2},{1,3},{2,0},{3,1},{4,6},{5,7},{6,4},{7,5},{8,10},{9,11},{10,... | collective-permute-start | bytes 1966088 | tf_op jit(solution)/shard_map/ppermute | solution.py:321
  6.1 12.5 %collective-permute-start.1 = (bf16[512,256]{1,0:T(8,128)(2,1)S(1)}, bf16[512,256]{1,0:T(8,128)(2,1)S(1)}, u32[]{:S(2)}, u32[]{:S(2)}) collective-permute-start(bf16[512,256]{1,0:T(8,128)(2,1)S(1)} %slice.36), channel_id=1, source_target_pairs={{0,24},{8,0},{16,8},{24,16},{1,25},{9,1},{17,9},{25,17},{2,26},{10... | collective-permute-start | bytes 786440 | tf_op jit(solution)/shard_map/ppermute | solution.py:325
  10.8 27.9 %collective-permute-start.5 = (bf16[768,256]{1,0:T(8,128)(2,1)S(1)}, bf16[768,256]{1,0:T(8,128)(2,1)}, u32[]{:S(2)}, u32[]{:S(2)}) collective-permute-start(bf16[768,256]{1,0:T(8,128)(2,1)S(1)} %slice.37), channel_id=1, source_target_pairs={{0,24},{8,0},{16,8},{24,16},{1,25},{9,1},{17,9},{25,17},{2,26},{10... | collective-permute-start | bytes 1179656 | tf_op jit(solution)/shard_map/ppermute | solution.py:325
  11.3 28.6 %collective-permute-start.4 = (bf16[768,256]{1,0:T(8,128)(2,1)S(1)}, bf16[768,256]{1,0:T(8,128)(2,1)}, u32[]{:S(2)}, u32[]{:S(2)}) collective-permute-start(bf16[768,256]{1,0:T(8,128)(2,1)S(1)} %slice.37), channel_id=1, source_target_pairs={{0,8},{8,16},{16,24},{24,0},{1,9},{9,17},{17,25},{25,1},{2,10},{10... | collective-permute-start | bytes 1179656 | tf_op jit(solution)/shard_map/ppermute | solution.py:324
  18.6 21.4 %collective-permute-start.12 = (bf16[2560,128]{1,0:T(8,128)(2,1)}, bf16[2560,128]{1,0:T(8,128)(2,1)S(1)}, u32[]{:S(2)}, u32[]{:S(2)}) collective-permute-start(bf16[2560,128]{1,0:T(8,128)(2,1)} %refs_0_.3), channel_id=1, source_target_pairs={{0,1},{1,0},{2,3},{3,2},{4,5},{5,4},{6,7},{7,6},{8,9},{9,8},{10,11... | collective-permute-start | bytes 1966088 | tf_op jit(solution)/shard_map/ppermute | solution.py:321
  18.7 20.0 %collective-permute-start.10 = (bf16[1280,128]{1,0:T(8,128)(2,1)S(1)}, bf16[1280,128]{1,0:T(8,128)(2,1)S(1)}, u32[]{:S(2)}, u32[]{:S(2)}) collective-permute-start(bf16[1280,128]{1,0:T(8,128)(2,1)S(1)} %slice.48), channel_id=1, source_target_pairs={{0,2},{1,3},{2,0},{3,1},{4,6},{5,7},{6,4},{7,5},{8,10},{9,11},{10,... | collective-permute-start | bytes 983048 | tf_op jit(solution)/shard_map/ppermute | solution.py:321
  20.4 17.7 %collective-permute-start = (bf16[512,256]{1,0:T(8,128)(2,1)S(1)}, bf16[512,256]{1,0:T(8,128)(2,1)S(1)}, u32[]{:S(2)}, u32[]{:S(2)}) collective-permute-start(bf16[512,256]{1,0:T(8,128)(2,1)S(1)} %slice.36), channel_id=1, source_target_pairs={{0,8},{8,16},{16,24},{24,0},{1,9},{9,17},{17,25},{25,1},{2,10},{10... | collective-permute-start | bytes 786440 | tf_op jit(solution)/shard_map/ppermute | solution.py:324
  40.0 18.5 %collective-permute-start.7 = (bf16[768,256]{1,0:T(8,128)(2,1)}, bf16[768,256]{1,0:T(8,128)(2,1)}, u32[]{:S(2)}, u32[]{:S(2)}) collective-permute-start(bf16[768,256]{1,0:T(8,128)(2,1)} %collective-permute-done.5.refs_2_), channel_id=1, source_target_pairs={{8,0},{16,8},{9,1},{17,9},{10,2},{18,10},{11,3},{19,11},{12,4},{20... | collective-permute-start | bytes 1179656 | tf_op jit(solution)/shard_map/ppermute | solution.py:326
  48.4 26.3 %collective-permute-start.3 = (bf16[512,256]{1,0:T(8,128)(2,1)S(1)}, bf16[512,256]{1,0:T(8,128)(2,1)S(1)}, u32[]{:S(2)}, u32[]{:S(2)}) collective-permute-start(bf16[512,256]{1,0:T(8,128)(2,1)S(1)} %collective-permute-done.1.refs_2_), channel_id=1, source_target_pairs={{8,0},{16,8},{9,1},{17,9},{10,2},{18,10},{11,3},{19,11},{12,4},{20... | collective-permute-start | bytes 786440 | tf_op jit(solution)/shard_map/ppermute | solution.py:326
  50.3 24.3 %collective-permute-start.2 = (bf16[512,256]{1,0:T(8,128)(2,1)}, bf16[512,256]{1,0:T(8,128)(2,1)S(1)}, u32[]{:S(2)}, u32[]{:S(2)}) collective-permute-start(bf16[512,256]{1,0:T(8,128)(2,1)} %copy-done.12), channel_id=1, source_target_pairs={{8,16},{16,24},{9,17},{17,25},{10,18},{18,26},{11,19},{19,27},{12,... | collective-permute-start | bytes 786440 | tf_op jit(solution)/shard_map/ppermute | solution.py:326
  122.8 53.5 %collective-permute-start.43 = (bf16[512,256]{1,0:T(8,128)(2,1)S(1)}, bf16[512,256]{1,0:T(8,128)(2,1)}, u32[]{:S(2)}, u32[]{:S(2)}) collective-permute-start(bf16[512,256]{1,0:T(8,128)(2,1)S(1)} %get-tuple-element.61), channel_id=1, source_target_pairs={{24,16},{16,8},{25,17},{17,9},{26,18},{18,10},{27,19},{19,11},{28,... | collective-permute-start | bytes 786440 | tf_op jit(solution)/shard_map/ppermute | solution.py:382
  124.1 55.6 %collective-permute-start.41 = (bf16[512,256]{1,0:T(8,128)(2,1)S(1)}, bf16[512,256]{1,0:T(8,128)(2,1)}, u32[]{:S(2)}, u32[]{:S(2)}) collective-permute-start(bf16[512,256]{1,0:T(8,128)(2,1)S(1)} %get-tuple-element.61), channel_id=1, source_target_pairs={{0,8},{8,16},{1,9},{9,17},{2,10},{10,18},{3,11},{11,19},{4,12},{12... | collective-permute-start | bytes 786440 | tf_op jit(solution)/shard_map/ppermute | solution.py:381
  141.6 42.7 %collective-permute-start.39 = (bf16[768,256]{1,0:T(8,128)(2,1)S(1)}, bf16[768,256]{1,0:T(8,128)(2,1)S(1)}, u32[]{:S(2)}, u32[]{:S(2)}) collective-permute-start(bf16[768,256]{1,0:T(8,128)(2,1)S(1)} %get-tuple-element.57), channel_id=1, source_target_pairs={{24,16},{16,8},{25,17},{17,9},{26,18},{18,10},{27,19},{19,11},{28,... | collective-permute-start | bytes 1179656 | tf_op jit(solution)/shard_map/ppermute | solution.py:382
  142.3 42.2 %collective-permute-start.37 = (bf16[768,256]{1,0:T(8,128)(2,1)S(1)}, bf16[768,256]{1,0:T(8,128)(2,1)S(1)}, u32[]{:S(2)}, u32[]{:S(2)}) collective-permute-start(bf16[768,256]{1,0:T(8,128)(2,1)S(1)} %get-tuple-element.57), channel_id=1, source_target_pairs={{0,8},{8,16},{1,9},{9,17},{2,10},{10,18},{3,11},{11,19},{4,12},{12... | collective-permute-start | bytes 1179656 | tf_op jit(solution)/shard_map/ppermute | solution.py:381
  175.6 37.4 %collective-permute-start.33 = (bf16[1280,512]{1,0:T(8,128)(2,1)S(1)}, bf16[1280,512]{1,0:T(8,128)(2,1)S(1)}, u32[]{:S(2)}, u32[]{:S(2)}) collective-permute-start(bf16[1280,512]{1,0:T(8,128)(2,1)S(1)} %get-tuple-element.51), channel_id=1, source_target_pairs={{0,1},{1,0},{2,3},{3,2},{4,5},{5,4},{6,7},{7,6},{8,9},{9,8},{10,11... | collective-permute-start | bytes 3932168 | tf_op jit(solution)/shard_map/ppermute | solution.py:321
  179.7 13.9 %collective-permute-start.44 = (bf16[512,256]{1,0:T(8,128)(2,1)S(1)}, bf16[512,256]{1,0:T(8,128)(2,1)S(1)}, u32[]{:S(2)}, u32[]{:S(2)}) collective-permute-start(bf16[512,256]{1,0:T(8,128)(2,1)S(1)} %add.174), channel_id=1, source_target_pairs={{0,24},{8,0},{16,8},{24,16},{1,25},{9,1},{17,9},{25,17},{2,26},{10... | collective-permute-start | bytes 786440 | tf_op jit(solution)/shard_map/ppermute | solution.py:384
  184.5 19.6 %collective-permute-start.40 = (bf16[768,256]{1,0:T(8,128)(2,1)S(1)}, bf16[768,256]{1,0:T(8,128)(2,1)S(1)}, u32[]{:S(2)}, u32[]{:S(2)}) collective-permute-start(bf16[768,256]{1,0:T(8,128)(2,1)S(1)} %add.170), channel_id=1, source_target_pairs={{0,24},{8,0},{16,8},{24,16},{1,25},{9,1},{17,9},{25,17},{2,26},{10... | collective-permute-start | bytes 1179656 | tf_op jit(solution)/shard_map/ppermute | solution.py:384
  188.5 23.4 %collective-permute-start.38 = (bf16[768,256]{1,0:T(8,128)(2,1)S(1)}, bf16[768,256]{1,0:T(8,128)(2,1)S(1)}, u32[]{:S(2)}, u32[]{:S(2)}) collective-permute-start(bf16[768,256]{1,0:T(8,128)(2,1)S(1)} %add.168), channel_id=1, source_target_pairs={{0,8},{8,16},{16,24},{24,0},{1,9},{9,17},{17,25},{25,1},{2,10},{10... | collective-permute-start | bytes 1179656 | tf_op jit(solution)/shard_map/ppermute | solution.py:383
  193.6 20.0 %collective-permute-start.29 = (bf16[1280,512]{1,0:T(8,128)(2,1)S(1)}, bf16[1280,512]{1,0:T(8,128)(2,1)S(1)}, u32[]{:S(2)}, u32[]{:S(2)}) collective-permute-start(bf16[1280,512]{1,0:T(8,128)(2,1)S(1)} %get-tuple-element.46), channel_id=1, source_target_pairs={{0,1},{1,0},{2,3},{3,2},{4,5},{5,4},{6,7},{7,6},{8,9},{9,8},{10,11... | collective-permute-start | bytes 3932168 | tf_op jit(solution)/shard_map/ppermute | solution.py:321
  213.7 22.7 %collective-permute-start.30 = (bf16[1280,128]{1,0:T(8,128)(2,1)S(1)}, bf16[1280,128]{1,0:T(8,128)(2,1)S(1)}, u32[]{:S(2)}, u32[]{:S(2)}) collective-permute-start(bf16[1280,128]{1,0:T(8,128)(2,1)S(1)} %get-tuple-element.69), channel_id=1, source_target_pairs={{0,2},{1,3},{2,0},{3,1},{4,6},{5,7},{6,4},{7,5},{8,10},{9,11},{10,... | collective-permute-start | bytes 983048 | tf_op jit(solution)/shard_map/ppermute | solution.py:321
  214.3 17.1 %collective-permute-start.31 = (bf16[1280,128]{1,0:T(8,128)(2,1)S(1)}, bf16[1280,128]{1,0:T(8,128)(2,1)S(1)}, u32[]{:S(2)}, u32[]{:S(2)}) collective-permute-start(bf16[1280,128]{1,0:T(8,128)(2,1)S(1)} %get-tuple-element.70), channel_id=1, source_target_pairs={{0,2},{1,3},{2,0},{3,1},{4,6},{5,7},{6,4},{7,5},{8,10},{9,11},{10,... | collective-permute-start | bytes 983048 | tf_op jit(solution)/shard_map/ppermute | solution.py:321
  221.9 14.3 %collective-permute-start.35 = (bf16[1280,128]{1,0:T(8,128)(2,1)S(1)}, bf16[1280,128]{1,0:T(8,128)(2,1)S(1)}, u32[]{:S(2)}, u32[]{:S(2)}) collective-permute-start(bf16[1280,128]{1,0:T(8,128)(2,1)S(1)} %get-tuple-element.71), channel_id=1, source_target_pairs={{0,2},{1,3},{2,0},{3,1},{4,6},{5,7},{6,4},{7,5},{8,10},{9,11},{10,... | collective-permute-start | bytes 983048 | tf_op jit(solution)/shard_map/ppermute | solution.py:321
  222.4 13.8 %collective-permute-start.36 = (bf16[1280,128]{1,0:T(8,128)(2,1)S(1)}, bf16[1280,128]{1,0:T(8,128)(2,1)S(1)}, u32[]{:S(2)}, u32[]{:S(2)}) collective-permute-start(bf16[1280,128]{1,0:T(8,128)(2,1)S(1)} %get-tuple-element.72), channel_id=1, source_target_pairs={{0,4},{1,5},{2,6},{3,7},{4,0},{5,1},{6,2},{7,3},{8,12},{9,13},{10,... | collective-permute-start | bytes 983048 | tf_op jit(solution)/shard_map/ppermute | solution.py:321
  (47 other events, 395.9 us)

commit v3 on v0

v3 whole, which is shorter than its diff:
```python
import functools
import math
import jax
import jax.numpy as jnp
from jax import lax
from jax.experimental import pallas as pl
from jax.experimental.pallas import tpu as pltpu
from jax.sharding import PartitionSpec as P

logit_scale = 100.0
log2e = math.log2(math.e)
ln2 = math.log(2.0)
strip = 32
vmem_bytes = 48 * 1024 * 1024

VMEM = pl.BlockSpec(memory_space=pltpu.VMEM)


def columns(slot, width):
    return pl.ds(pl.multiple_of(slot * width, width), width)


def in_hbm(array):
    return pltpu.with_memory_space_constraint(array, pltpu.HBM)


def params():
    return pltpu.CompilerParams(vmem_limit_bytes=vmem_bytes)


def cost(microseconds):
    return pl.CostEstimate(flops=int(1.1e9 * microseconds), bytes_accessed=1, transcendentals=0)


def log_add(*terms):
    larger = functools.reduce(jnp.maximum, terms)
    return larger + jnp.log(sum(jnp.exp2(term - larger) for term in terms)) * log2e


def lanes(x):
    return [x[:, k : k + 128] for k in range(0, x.shape[1], 128)]


def side_by_side(image_pieces, text_pieces, width):
    img_rows = image_pieces[0][0].shape[0]
    rows = text_pieces[0][0].shape[0]
    steps = 4
    bm, bt = img_rows // steps, rows // steps
    pieces = text_pieces + image_pieces

    def kernel(*refs):
        *sources, texts_ref, images_ref = refs
        texts_ref[...] = jnp.zeros(texts_ref.shape, jnp.bfloat16)
        for k, (source, (_, slot)) in enumerate(zip(sources, pieces)):
            target = texts_ref if k < len(text_pieces) else images_ref
            target[:, columns(slot(), source.shape[1])] = source[...]

    return pl.pallas_call(
        kernel,
        grid=(steps,),
        out_shape=(
            jax.ShapeDtypeStruct((rows, width), jnp.bfloat16),
            pltpu.HBM((img_rows, width), jnp.bfloat16),
        ),
        in_specs=[pl.BlockSpec((bt, piece.shape[1]), lambda i: (i, 0)) for piece, _ in text_pieces]
        + [pl.BlockSpec((bm, piece.shape[1]), lambda i: (i, 0)) for piece, _ in image_pieces],
        out_specs=(pl.BlockSpec((bt, width), lambda i: (i, 0)), pl.BlockSpec((bm, width), lambda i: (i, 0))),
        compiler_params=params(),
        cost_estimate=cost(10),
        name="side_by_side",
    )(*[in_hbm(piece) for piece, _ in pieces])


def logits_and_stats(images, texts, far, targets):
    img_rows, width = images.shape
    rows = texts.shape[0]
    steps, bm = targets.shape
    pieces = rows // 256
    some = bm // pieces

    def before(i):
        return jnp.maximum(i - 1, 0)

    def kernel(images_ref, texts_ref, targets_ref, *refs):
        if far is not None:
            one_ref, other_ref, *refs = refs
        u_ref, row_ref, col_ref, whole_ref, d_scr, rm_scr, rs_scr, cm_scr, cs_scr, target_scr, pos_scr = refs
        step = pl.program_id(0)

        @pl.when(step == 0)
        def _():
            cm_scr[...] = jnp.full(cm_scr.shape, -jnp.inf, jnp.float32)
            cs_scr[...] = jnp.zeros(cs_scr.shape, jnp.float32)
            pos_scr[...] = jnp.zeros(pos_scr.shape, jnp.float32)
            whole_ref[...] = texts_ref[...]
            if far is not None:
                whole_ref[:, columns(far[1](), one_ref.shape[1])] = jnp.where(far[2](), one_ref[...], other_ref[...])

        def matmul(j):
            at = slice(j * 256, (j + 1) * 256)
            d_scr[step % 2, :, at] = lax.dot_general(
                images_ref[...], whole_ref[at, :], (((1,), (1,)), ((), ())), preferred_element_type=jnp.float32
            )

        def elementwise(j):
            slot = (step + 1) % 2
            old = cm_scr[...]
            new = old
            ids = lax.broadcasted_iota(jnp.int32, (strip, 128), 1)
            picked = jnp.zeros((strip, 128), jnp.float32)
            for first in range(j * some, (j + 1) * some, strip):
                at = slice(first, first + strip)
                u = d_scr[slot, at, :] * (logit_scale * log2e)
                u_ref[at, :] = u
                target = target_scr[at, :] - ids
                for k, v in enumerate(lanes(u)):
                    picked = picked + jnp.where(target == 128 * k, v, 0.0)
                rm_scr[at, :] = functools.reduce(jnp.maximum, lanes(u))
                new = jnp.maximum(new, jnp.max(u.reshape(strip // 8, 8, rows), axis=0))
            pos_scr[...] += picked
            cm_scr[...] = new
            total = cs_scr[...] * jnp.exp2(old - new)
            for first in range(j * some, (j + 1) * some, strip):
                at = slice(first, first + strip)
                u = u_ref[at, :]
                row_max = rm_scr[at, :]
                rs_scr[at, :] = functools.reduce(jnp.add, [jnp.exp2(v - row_max) for v in lanes(u)])
                total = total + jnp.sum(jnp.exp2(u.reshape(strip // 8, 8, rows) - new[None]), axis=0)
            cs_scr[...] = total

        @pl.when(step > 0)
        def _():
            target_scr[...] = jnp.broadcast_to(targets_ref[pl.ds(step - 1, 1), :], (128, bm)).T

        @pl.when(step == 0)
        def _():
            for j in range(pieces):
                matmul(j)

        @pl.when(jnp.logical_and(step > 0, step < steps))
        def _():
            for j in range(pieces):
                matmul(j)
                elementwise(j)

        @pl.when(step == steps)
        def _():
            for j in range(pieces):
                elementwise(j)

        @pl.when(step > 0)
        def _():
            lane_max, lane_sum = rm_scr[...].T, rs_scr[...].T
            top = jnp.max(lane_max, axis=0, keepdims=True)
            row_sum = jnp.sum(lane_sum * jnp.exp2(lane_max - top), axis=0, keepdims=True)
            row_ref[pl.ds(step - 1, 1), :] = top + jnp.log(row_sum) * log2e

        @pl.when(step == steps)
        def _():
            top = jnp.max(cm_scr[...], axis=0, keepdims=True)
            col_sum = jnp.sum(cs_scr[...] * jnp.exp2(cm_scr[...] - top), axis=0, keepdims=True)
            col_ref[...] = top + jnp.log(col_sum) * log2e
            row_ref[pl.ds(steps, 1), :] = jnp.full((1, bm), jnp.sum(pos_scr[...]))

    return pl.pallas_call(
        kernel,
        grid=(steps + 1,),
        out_shape=(
            pltpu.HBM((img_rows, rows), jnp.float32),
            jax.ShapeDtypeStruct((steps + 1, bm), jnp.float32),
            jax.ShapeDtypeStruct((1, rows), jnp.float32),
            pltpu.HBM((rows, width), jnp.bfloat16),
        ),
        in_specs=[pl.BlockSpec((bm, width), lambda i: (jnp.minimum(i, steps - 1), 0)), VMEM, VMEM]
        + ([] if far is None else [VMEM, VMEM]),
        out_specs=(pl.BlockSpec((bm, rows), lambda i: (before(i), 0)), VMEM, VMEM, VMEM),
        scratch_shapes=[
            pltpu.VMEM((2, bm, rows), jnp.float32),
            pltpu.VMEM((bm, 128), jnp.float32),
            pltpu.VMEM((bm, 128), jnp.float32),
            pltpu.VMEM((8, rows), jnp.float32),
            pltpu.VMEM((8, rows), jnp.float32),
            pltpu.VMEM((bm, 128), jnp.int32),
            pltpu.VMEM((strip, 128), jnp.float32),
        ],
        compiler_params=params(),
        cost_estimate=cost(13),
        name="logits_and_stats",
    )(in_hbm(images), texts, targets, *(() if far is None else far[0]))


def weights_and_far(u, images, targets, row_lses, col_lses, slot, wide):
    img_rows = images.shape[0]
    rows = u.shape[1]
    steps, bm = targets.shape
    n_row, n_col = len(row_lses), len(col_lses)

    def now(i):
        return jnp.minimum(i, steps - 1)

    def before(i):
        return jnp.maximum(i - 1, 0)

    def kernel(u_ref, images_ref, targets_ref, *refs):
        row_refs, col_refs, refs = refs[:n_row], refs[n_row : n_row + n_col], refs[n_row + n_col :]
        w_ref, far_ref, loss_ref, w_scr, acc, row_ref, col_ref, row_scr, target_scr = refs
        step = pl.program_id(0)

        @pl.when(step == 0)
        def _():
            acc[...] = jnp.zeros(acc.shape, jnp.float32)
            row_ref[...] = log_add(*[ref[:steps, :] for ref in row_refs])
            col_ref[...] = log_add(*[ref[...] for ref in col_refs])
            picked = sum(ref[steps:, :1] for ref in row_refs)
            row_loss = jnp.sum(row_ref[...], keepdims=True) - 2.0 * picked
            col_loss = jnp.sum(col_ref[...], keepdims=True)
            lane = lax.broadcasted_iota(jnp.int32, (1, 128), 1)
            loss_ref[...] = jnp.where(lane == 0, row_loss, jnp.where(lane == 1, col_loss, 0.0))

        def elementwise():
            row_scr[...] = jnp.broadcast_to(row_ref[pl.ds(step, 1), :], (128, bm)).T
            target_scr[...] = jnp.broadcast_to(targets_ref[pl.ds(step, 1), :], (128, bm)).T
            ids = lax.broadcasted_iota(jnp.int32, (strip, 128), 1)
            col = col_ref[...]
            for first in range(0, bm, strip):
                at = slice(first, first + strip)
                row = row_scr[at, :]
                target = target_scr[at, :] - ids
                for k in range(0, rows, 128):
                    v = u_ref[at, k : k + 128]
                    weight = jnp.exp2(v - row) + jnp.exp2(v - col[:, k : k + 128]) - jnp.where(target == k, 2.0, 0.0)
                    weight = weight.astype(jnp.bfloat16)
                    w_ref[at, k : k + 128] = weight
                    w_scr[step % 2, at, k : k + 128] = weight

        def matmul():
            acc[...] += lax.dot_general(
                w_scr[(step + 1) % 2],
                images_ref[...],
                (((0,), (0,)), ((), ())),
                preferred_element_type=jnp.float32,
            )

        @pl.when(step == 0)
        def _():
            elementwise()

        @pl.when(jnp.logical_and(step > 0, step < steps))
        def _():
            elementwise()
            matmul()

        @pl.when(step == steps)
        def _():
            matmul()
            far_ref[...] = (logit_scale * acc[...]).astype(jnp.bfloat16)

    return pl.pallas_call(
        kernel,
        grid=(steps + 1,),
        out_shape=(
            pltpu.HBM((img_rows, rows), jnp.bfloat16),
            jax.ShapeDtypeStruct((rows, wide), jnp.bfloat16),
            jax.ShapeDtypeStruct((1, 128), jnp.float32),
        ),
        in_specs=[
            pl.BlockSpec((bm, rows), lambda i: (now(i), 0)),
            pl.BlockSpec((bm, wide), lambda i: (before(i), slot())),
        ]
        + [VMEM] * (1 + n_row + n_col),
        out_specs=(pl.BlockSpec((bm, rows), lambda i: (now(i), 0)), VMEM, VMEM),
        scratch_shapes=[
            pltpu.VMEM((2, bm, rows), jnp.bfloat16),
            pltpu.VMEM((rows, wide), jnp.float32),
            pltpu.VMEM((steps, bm), jnp.float32),
            pltpu.VMEM((1, rows), jnp.float32),
            pltpu.VMEM((bm, 128), jnp.float32),
            pltpu.VMEM((bm, 128), jnp.int32),
        ],
        compiler_params=params(),
        cost_estimate=cost(8),
        name="weights_and_far",
    )(in_hbm(u), in_hbm(images), targets, *row_lses, *col_lses)


def gradients(weights, images, texts, slots, text_wide, groups):
    img_rows, rows = weights.shape
    width = texts.shape[1]
    steps = 4
    bm = img_rows // steps
    wide = width // sum(len(group) for group in groups)
    n_text = len(slots)

    def kernel(w_ref, texts_ref, *refs):
        image_refs, text_outs, (*image_outs, acc, image_acc) = refs[:n_text], refs[n_text : 2 * n_text], refs[2 * n_text :]
        step = pl.program_id(0)

        @pl.when(step == 0)
        def _():
            acc[...] = jnp.zeros(acc.shape, jnp.float32)

        for k, image_ref in enumerate(image_refs):
            acc[k] += lax.dot_general(
                w_ref[...], image_ref[...], (((0,), (0,)), ((), ())), preferred_element_type=jnp.float32
            )
        image_acc[...] = logit_scale * jnp.dot(w_ref[...], texts_ref[...], preferred_element_type=jnp.float32)
        for out, group in zip(image_outs, groups):
            for k, slot in enumerate(group):
                out[:, k * wide : (k + 1) * wide] = image_acc[:, columns(slot(), wide)].astype(jnp.bfloat16)

        @pl.when(step == steps - 1)
        def _():
            for k, out in enumerate(text_outs):
                out[...] = (logit_scale * acc[k]).astype(jnp.bfloat16)

    def image_spec(slot):
        return pl.BlockSpec((bm, text_wide), lambda i: (i, slot()))

    return pl.pallas_call(
        kernel,
        grid=(steps,),
        out_shape=(jax.ShapeDtypeStruct((rows, text_wide), jnp.bfloat16),) * n_text
        + tuple(jax.ShapeDtypeStruct((img_rows, wide * len(group)), jnp.bfloat16) for group in groups),
        in_specs=[pl.BlockSpec((bm, rows), lambda i: (i, 0)), VMEM] + [image_spec(slot) for slot in slots],
        out_specs=(VMEM,) * n_text + tuple(pl.BlockSpec((bm, wide * len(g)), lambda i: (i, 0)) for g in groups),
        scratch_shapes=[
            pltpu.VMEM((n_text, rows, text_wide), jnp.float32),
            pltpu.VMEM((bm, width), jnp.float32),
        ],
        compiler_params=params(),
        cost_estimate=cost(18),
        name="gradients",
    )(in_hbm(weights), texts, *[in_hbm(images)] * n_text)


def together(*values):
    return lax.optimization_barrier(values)


def as_bf16_sum(*terms):
    return sum(term.astype(jnp.float32) for term in terms).astype(jnp.bfloat16)


def shifted(count, by):
    return [(i, (i + by) % count) for i in range(count)]


def paired(count, by):
    return [(i, i ^ by) for i in range(count)]


def per_device_4x8(images, texts, positive):
    img_rows = images.shape[0]
    txt_rows, quarter = texts.shape
    width = quarter * 4

    def swap(part, by):
        return lax.ppermute(part, "txt", paired(8, by))

    def over_z(part, by):
        return lax.ppermute(part, "img", paired(4, by))

    def across(part, by_z, by_txt):
        pairs = [(8 * z + c, 8 * (z ^ by_z) + (c ^ by_txt)) for z in range(4) for c in range(8)]
        return lax.ppermute(part, ("img", "txt"), pairs)

    def txt_slot(flip):
        return lambda: lax.axis_index("txt") ^ flip

    def img_slot(by):
        return lambda: lax.rem(lax.axis_index("img") + by, 4)

    targets = (positive - lax.axis_index("txt") * txt_rows).reshape(4, img_rows // 4)
    from_prev = lax.ppermute(texts, "img", shifted(4, 1))
    from_next = lax.ppermute(texts, "img", shifted(4, -1))
    parts = [images, swap(images, 2), swap(images, 4), swap(images, 6)]
    targets, from_prev, from_next, *parts = together(targets, from_prev, from_next, *parts)
    from_below = lax.ppermute(from_prev, "img", [(1, 2), (2, 3)])
    from_above = lax.ppermute(from_next, "img", [(1, 0), (2, 1)])
    parts += [swap(part, 1) for part in parts]
    image_pieces = [(part, txt_slot(flip)) for part, flip in zip(parts, (0, 2, 4, 6, 1, 3, 5, 7))]
    text_pieces = [(texts, img_slot(0)), (from_prev, img_slot(3)), (from_next, img_slot(1))]
    most_txt, whole_img = side_by_side(image_pieces, text_pieces, width)
    from_below, from_above, most_txt = together(from_below, from_above, most_txt)
    far = ((from_below, from_above), img_slot(2), lambda: lax.axis_index("img") >= 2)
    u, row, col, whole_txt = logits_and_stats(whole_img, most_txt, far, targets)

    other = swap(row, 1)
    last = lax.broadcasted_iota(jnp.int32, row.shape, 0) == 4
    row = jnp.where(last, row + other, log_add(row, other))
    rows = [row] + [swap(row, by) for by in (2, 4, 6)]
    cols = [col] + [over_z(col, by) for by in (1, 2, 3)]

    w, far_grad, loss = weights_and_far(u, whole_img, targets, rows, cols, img_slot(2), quarter)
    below = lax.ppermute(far_grad, "img", [(0, 1), (1, 2)])
    above = lax.ppermute(far_grad, "img", [(3, 2), (2, 1)])
    image_groups = [[txt_slot(flip)] for flip in (0, 2, 4, 6)] + [[txt_slot(flip) for flip in (1, 3, 5, 7)]]
    text_slots = [img_slot(1), img_slot(3), img_slot(0)]
    to_next, to_prev, own, *image_parts = gradients(w, whole_img, whole_txt, text_slots, quarter, image_groups)
    loss += across(loss, 1, 1)
    below, above, to_next, to_prev, *image_parts, loss = together(below, above, to_next, to_prev, *image_parts, loss)

    other = swap(image_parts.pop(), 1)
    eighth = width // 8
    s, x, y, d = [part + other[:, j * eighth : (j + 1) * eighth] for j, part in enumerate(image_parts)]
    losses = [across(loss, 2, 2), swap(loss, 4), swap(loss, 6)]
    to_next, to_prev = to_next + below, to_prev + above
    to_next, to_prev, s, x, y, d, *losses = together(to_next, to_prev, s, x, y, d, *losses)

    from_prev = lax.ppermute(to_next, "img", shifted(4, 1))
    from_next = lax.ppermute(to_prev, "img", shifted(4, -1))
    image_grad = as_bf16_sum(s, swap(x, 2), swap(y, 4), swap(d, 6))
    text_grad = as_bf16_sum(own, from_prev, from_next)
    loss = (loss + losses[0])[0, 0] + (loss + sum(losses))[0, 1]
    return loss * (ln2 / (2.0 * txt_rows * 8)), image_grad, text_grad


def per_device(images, texts, positive):
    n_img, n_txt = lax.axis_size("img"), lax.axis_size("txt")
    if (n_img, n_txt) == (4, 8):
        return per_device_4x8(images, texts, positive)

    def first_slot():
        return jnp.int32(0)

    def gathered(part, axis):
        every = lax.all_gather(part, axis)
        return [every[k] for k in range(lax.axis_size(axis))]

    whole_img = lax.all_gather(images, "txt", axis=1, tiled=True)
    whole_txt = lax.all_gather(texts, "img", axis=1, tiled=True)
    txt_rows, width = whole_txt.shape
    targets = (positive - lax.axis_index("txt") * txt_rows).reshape(4, whole_img.shape[0] // 4)
    u, row, col, whole_txt = logits_and_stats(whole_img, whole_txt, None, targets)
    rows, cols = gathered(row, "txt"), gathered(col, "img")
    w, _, loss = weights_and_far(u, whole_img, targets, rows, cols, first_slot, 256)
    text_part, image_part = gradients(w, whole_img, whole_txt, [first_slot], width, [[first_slot]])
    loss = lax.psum(loss[0, 0] / n_txt + loss[0, 1] / n_img, ("img", "txt"))
    mean_loss = loss * (ln2 / (2.0 * txt_rows * n_txt))
    image_grad = lax.psum_scatter(image_part, "txt", scatter_dimension=1, tiled=True)
    text_grad = lax.psum_scatter(text_part, "img", scatter_dimension=1, tiled=True)
    return mean_loss, image_grad, text_grad


def solution(mesh):
    placed = (P("img", "txt"), P("txt", "img"), P("img"))
    return jax.shard_map(
        per_device,
        mesh=mesh,
        in_specs=placed,
        out_specs=(P(), P("img", "txt"), P("txt", "img")),
        check_vma=False,
    )
```

time: 387 us -> 173 us (0.45)
  blocking collectives: 105 us -> 0 us
  waiting for transfers between devices: 165 us -> 74.4 us
  matrix products: 71.8 us -> 0 us
  Pallas kernels: 0 us -> 55.6 us
  starting transfers between devices: 0.16 us -> 33.7 us
  between operations: 17 us -> 2.64 us
  local copies, waits for them, and re-layouts: 12.9 us -> 2.11 us
  other arithmetic: 12.9 us -> 3.74 us
    all_gather x2 -> x0, waiting for transfers between devices: 99.8 us -> none  [the longest x1 57.7 us: per_device(): whole_txt = lax.all_gather(texts, 'img', axis=1, tiled=True)]
    ppermute x0 -> x30, waiting for transfers between devices: none -> 74.4 us  [the longest x1 12.6 us: per_device_4x8(): from_next = lax.ppermute(texts, 'img', shifted(4, -1))]
    dot_general x20 -> x0, matrix products: 71.8 us -> none  [the longest x10 40.5 us: tile_logits(): lax.dot_general(image_block, whole_txt, (((1,), (1,)), ((), ())), preferr...]
    all_gather x6 -> x0, blocking collectives: 66.2 us -> none  [merged(): everything = jax.tree.map(lambda part: lax.all_gather(part, axis), shard)]
    pallas_call x0 -> x4, Pallas kernels: none -> 55.6 us  [the longest x1 19.5 us: gradients(): pl.pallas_call(kernel, grid=(steps,), out_shape=(jax.ShapeDtypeStruct((ro...]
    reduce_scatter x1 -> x0, waiting for transfers between devices: 52.8 us -> none  [per_device(): lax.psum_scatter((logit_scale * text_total).astype(jnp.bfloat16), 'img',...]
    psum x1 -> x0, blocking collectives: 39.2 us -> none  [per_device(): lax.psum(row_term / lax.axis_size('txt') + col_term / lax.axis_size('img'...]
    ppermute x0 -> x30, starting transfers between devices: none -> 33.7 us  [the longest x17 17.2 us: swap(): return lax.ppermute(part, 'txt', paired(8, by))]
  transfers between devices with their start and end apart: 4 -> 30, of which waited for: 4 -> 16; matrix products, arithmetic and copies ran while one was open for 2% -> 2% of each run, Pallas kernels for 0% -> 15%
where the time goes in v3:
time: 173 us; the launch traced here: 172 us
  waiting for transfers between devices  74.4 us (43%)
  Pallas kernels  55.6 us (32%)
  starting transfers between devices  33.7 us (19%)
  other arithmetic  3.74 us (2%)
  between operations  2.64 us (2%)
  local copies, waits for them, and re-layouts  2.11 us (1%)
    pallas_call x1, Pallas kernels, gradients(): pl.pallas_call(kernel, grid=(steps,), out_shape=(jax.ShapeDtypeStruct((ro...  19.5 us
    pallas_call x1, Pallas kernels, logits_and_stats(): pl.pallas_call(kernel, grid=(steps + 1,), out_shape=(pltpu.HBM((img_rows,...  17.4 us
    ppermute x17, starting transfers between devices, swap(): return lax.ppermute(part, 'txt', paired(8, by))  17.2 us
    ppermute x1, waiting for transfers between devices, per_device_4x8(): from_next = lax.ppermute(texts, 'img', shifted(4, -1))  12.6 us
    pallas_call x1, Pallas kernels, weights_and_far(): pl.pallas_call(kernel, grid=(steps + 1,), out_shape=(pltpu.HBM((img_rows,...  12.1 us
    ppermute x17, waiting for transfers between devices, swap(): return lax.ppermute(part, 'txt', paired(8, by))  11.7 us
    ppermute x1, waiting for transfers between devices, per_device_4x8(): from_prev = lax.ppermute(texts, 'img', shifted(4, 1))  11.5 us
    ppermute x1, waiting for transfers between devices, per_device_4x8(): from_prev = lax.ppermute(to_next, 'img', shifted(4, 1))  10.9 us
  transfers between devices with their start and end apart: 30, of which 16 were waited for; matrix products, arithmetic and copies ran while one was open for 2% of the time, Pallas kernels for 15%

profile of v3, /device:TPU:0, one launch (start us, length us, event | category | flops | bytes accessed | tf_op | source)
XLA Modules:
  0.0 172.2 jit_solution(3546185446770050124)
XLA Ops:
  0.6 3.1 %collective-permute-start = (bf16[1280,256]{1,0:T(8,128)(2,1)}, bf16[1280,256]{1,0:T(8,128)(2,1)S(1)}, u32[]{:S(2)}, u32[]{:S(2)}) collective-permute-start(bf16[1280,256]{1,0:T(8,128)(2,1)} %refs_0_.1), channel_id=1, source_target_pairs={{0,8},{8,16},{16,24},{24,0},{1,9},{9,17},{17,25},{25,1},{2,10},{10... | collective-permute-start | bytes 1966088 | tf_op jit(solution)/shard_map/ppermute | solution.py:374
  3.7 2.1 %collective-permute-start.1 = (bf16[1280,256]{1,0:T(8,128)(2,1)}, bf16[1280,256]{1,0:T(8,128)(2,1)S(1)}, u32[]{:S(2)}, u32[]{:S(2)}) collective-permute-start(bf16[1280,256]{1,0:T(8,128)(2,1)} %refs_0_.1), channel_id=1, source_target_pairs={{0,24},{8,0},{16,8},{24,16},{1,25},{9,1},{17,9},{25,17},{2,26},{10... | collective-permute-start | bytes 1966088 | tf_op jit(solution)/shard_map/ppermute | solution.py:375
  5.8 1.7 collective-permute-start.3
  10.0 11.5 %collective-permute-done.refs_1_ = bf16[1280,256]{1,0:T(8,128)(2,1)S(1)} collective-permute-done((bf16[1280,256]{1,0:T(8,128)(2,1)}, bf16[1280,256]{1,0:T(8,128)(2,1)S(1)}, u32[]{:S(2)}, u32[]{:S(2)}) %collective-permute-start) | collective-permute-done | bytes 655392 | tf_op jit(solution)/shard_map/ppermute | solution.py:374
  21.6 12.6 %collective-permute-done.1.refs_2_ = bf16[1280,256]{1,0:T(8,128)(2,1)S(1)} collective-permute-done((bf16[1280,256]{1,0:T(8,128)(2,1)}, bf16[1280,256]{1,0:T(8,128)(2,1)S(1)}, u32[]{:S(2)}, u32[]{:S(2)}) %collective-permute-start.1) | collective-permute-done | bytes 655392 | tf_op jit(solution)/shard_map/ppermute | solution.py:375
  34.2 3.3 %collective-permute-done.4.refs_6_ = bf16[2560,128]{1,0:T(8,128)(2,1)S(1)} collective-permute-done((bf16[2560,128]{1,0:T(8,128)(2,1)}, bf16[2560,128]{1,0:T(8,128)(2,1)S(1)}, u32[]{:S(2)}, u32[]{:S(2)}) %collective-permute-start.4) | collective-permute-done | bytes 655392 | tf_op jit(solution)/shard_map/ppermute | solution.py:358
  43.9 6.7 %side_by_side.1 = (bf16[1280,1024]{1,0:T(8,128)(2,1)S(1)}, bf16[2560,1024]{1,0:T(8,128)(2,1)}) custom-call(bf16[1280,256]{1,0:T(8,128)(2,1)} %refs_0_.1, bf16[1280,256]{1,0:T(8,128)(2,1)} %copy-done, bf16[1280,256]{1,0:T(8,128)(2,1)} %copy-done.1, bf16[2560,128]{1,0:T(8,128)(2,1)} %refs_3_, bf16[2560,128]{1,0:T(8,128)(2,1)} %copy-done.3, ...), custom_call_target="tpu_custom_call" | custom-call | flops 11000000512 | bytes 1 | tf_op jit(solution)/shard_map/side_by_side/pallas_call | solution.py:58
  50.6 8.7 %collective-permute-done.10.refs_1_ = bf16[1280,256]{1,0:T(8,128)(2,1)S(1)} collective-permute-done((bf16[1280,256]{1,0:T(8,128)(2,1)S(1)}, bf16[1280,256]{1,0:T(8,128)(2,1)S(1)}, u32[]{:S(2)}, u32[]{:S(2)}) %collective-permute-start.10) | collective-permute-done | bytes 655392 | tf_op jit(solution)/shard_map/ppermute | solution.py:379
  59.3 17.4 %logits_and_stats.1 = (f32[2560,1280]{1,0:T(8,128)}, f32[5,640]{1,0:T(8,128)S(1)}, f32[1,1280]{1,0:T(1,128)S(1)}, bf16[1280,1024]{1,0:T(8,128)(2,1)}) custom-call(bf16[2560,1024]{1,0:T(8,128)(2,1)} %get-tuple-element.55.images_ref.refs_0_.refs_1_.refs_2_, bf16[1280,1024]{1,0:T(8,128)(2,1)S(1)} %get-tuple-element.57.texts_ref, ...), custom_call_target="tpu_custom_call" | custom-call | flops 14300000256 | bytes 1 | tf_op jit(solution)/shard_map/logits_and_stats/pallas_call | solution.py:165
  77.9 2.5 %collective-permute-start.14 = (f32[5,640]{1,0:T(8,128)S(1)}, f32[5,640]{1,0:T(8,128)S(1)}, u32[]{:S(2)}, u32[]{:S(2)}) collective-permute-start(f32[5,640]{1,0:T(8,128)S(1)} %add_select_fusion.refs_0_), channel_id=1, source_target_pairs={{0,6},{1,7},{2,4},{3,5},{4,2},{5,3},{6,0},{7,1},{8,14},{9,15},{10,... | collective-permute-start | bytes 38408 | tf_op jit(solution)/shard_map/ppermute | solution.py:358
  81.4 2.1 %collective-permute-start.16 = (f32[1,1280]{1,0:T(1,128)S(1)}, f32[1,1280]{1,0:T(1,128)S(1)}, u32[]{:S(2)}, u32[]{:S(2)}) collective-permute-start(f32[1,1280]{1,0:T(1,128)S(1)} %get-tuple-element.63.refs_4_), channel_id=1, source_target_pairs={{0,16},{8,24},{16,0},{24,8},{1,17},{9,25},{17,1},{25,9},{2,18},{10... | collective-permute-start | bytes 15368 | tf_op jit(solution)/shard_map/ppermute | solution.py:361
  83.5 3.4 %collective-permute-done.17.refs_7_ = f32[1,1280]{1,0:T(1,128)S(1)} collective-permute-done((f32[1,1280]{1,0:T(1,128)S(1)}, f32[1,1280]{1,0:T(1,128)S(1)}, u32[]{:S(2)}, u32[]{:S(2)}) %collective-permute-start.17) | collective-permute-done | bytes 5152 | tf_op jit(solution)/shard_map/ppermute | solution.py:361
  86.9 3.6 %collective-permute-done.15.refs_5_ = f32[1,1280]{1,0:T(1,128)S(1)} collective-permute-done((f32[1,1280]{1,0:T(1,128)S(1)}, f32[1,1280]{1,0:T(1,128)S(1)}, u32[]{:S(2)}, u32[]{:S(2)}) %collective-permute-start.15) | collective-permute-done | bytes 5152 | tf_op jit(solution)/shard_map/ppermute | solution.py:361
  90.5 12.1 %weights_and_far.1 = (bf16[2560,1280]{1,0:T(8,128)(2,1)}, bf16[1280,256]{1,0:T(8,128)(2,1)S(1)}, f32[1,128]{1,0:T(1,128)S(1)}) custom-call(f32[2560,1280]{1,0:T(8,128)} %get-tuple-element.61.u_ref, bf16[2560,1024]{1,0:T(8,128)(2,1)} %get-tuple-element.55.images_ref.refs_0_.refs_1_.refs_2_, s32[4,640]{1,0:T(4,128)S(1)} %reshape.12.targets_ref, ...), custom_call_target="tpu_custom_call" | custom-call | flops 8800000000 | bytes 1 | tf_op jit(solution)/shard_map/weights_and_far/pallas_call | solution.py:258
  103.3 2.7 %collective-permute-start.18 = (bf16[1280,256]{1,0:T(8,128)(2,1)S(1)}, bf16[1280,256]{1,0:T(8,128)(2,1)S(1)}, u32[]{:S(2)}, u32[]{:S(2)}) collective-permute-start(bf16[1280,256]{1,0:T(8,128)(2,1)S(1)} %get-tuple-element.64), channel_id=1, source_target_pairs={{0,8},{8,16},{1,9},{9,17},{2,10},{10,18},{3,11},{11,19},{4,12},{12... | collective-permute-start | bytes 1966088 | tf_op jit(solution)/shard_map/ppermute | solution.py:395
  106.1 19.5 %gradients.1 = (bf16[1280,256]{1,0:T(8,128)(2,1)S(1)}, bf16[1280,256]{1,0:T(8,128)(2,1)S(1)}, bf16[1280,256]{1,0:T(8,128)(2,1)S(1)}, bf16[2560,128]{1,0:T(8,128)...) custom-call(bf16[2560,1280]{1,0:T(8,128)(2,1)} %get-tuple-element.65, ...), custom_call_target="tpu_custom_call" | custom-call | flops 19800000512 | bytes 1 | tf_op jit(solution)/shard_map/gradients/pallas_call | solution.py:319
  125.6 2.7 %collective-permute-start.21 = (bf16[2560,512]{1,0:T(8,128)(2,1)}, bf16[2560,512]{1,0:T(8,128)(2,1)S(1)}, u32[]{:S(2)}, u32[]{:S(2)}) collective-permute-start(bf16[2560,512]{1,0:T(8,128)(2,1)} %get-tuple-element.81), channel_id=1, source_target_pairs={{0,1},{1,0},{2,3},{3,2},{4,5},{5,4},{6,7},{7,6},{8,9},{9,8},{10,11... | collective-permute-start | bytes 7864328 | tf_op jit(solution)/shard_map/ppermute | solution.py:358
  128.3 2.5 %collective-permute-start.24 = (f32[1,128]{1,0:T(1,128)S(1)}, f32[1,128]{1,0:T(1,128)S(1)}, u32[]{:S(2)}, u32[]{:S(2)}) collective-permute-start(f32[1,128]{1,0:T(1,128)S(1)} %add.64), channel_id=1, source_target_pairs={{0,6},{1,7},{2,4},{3,5},{4,2},{5,3},{6,0},{7,1},{8,14},{9,15},{10,... | collective-permute-start | bytes 1544 | tf_op jit(solution)/shard_map/ppermute | solution.py:358
  134.3 2.3 %collective-permute-done.22 = f32[1,128]{1,0:T(1,128)S(1)} collective-permute-done((f32[1,128]{1,0:T(1,128)S(1)}, f32[1,128]{1,0:T(1,128)S(1)}, u32[]{:S(2)}, u32[]{:S(2)}) %collective-permute-start.22) | collective-permute-done | bytes 544 | tf_op jit(solution)/shard_map/ppermute | solution.py:365
  136.6 3.8 %collective-permute-start.29 = (bf16[1280,256]{1,0:T(8,128)(2,1)S(1)}, bf16[1280,256]{1,0:T(8,128)(2,1)S(1)}, u32[]{:S(2)}, u32[]{:S(2)}) collective-permute-start(bf16[1280,256]{1,0:T(8,128)(2,1)S(1)} %add.66), channel_id=1, source_target_pairs={{0,24},{8,0},{16,8},{24,16},{1,25},{9,1},{17,9},{25,17},{2,26},{10... | collective-permute-start | bytes 1966088 | tf_op jit(solution)/shard_map/ppermute | solution.py:411
  141.0 1.5 collective-permute-start.26
  145.2 10.9 %collective-permute-done.28 = bf16[1280,256]{1,0:T(8,128)(2,1)S(1)} collective-permute-done((bf16[1280,256]{1,0:T(8,128)(2,1)S(1)}, bf16[1280,256]{1,0:T(8,128)(2,1)S(1)}, u32[]{:S(2)}, u32[]{:S(2)}) %collective-permute-start.28) | collective-permute-done | bytes 655392 | tf_op jit(solution)/shard_map/ppermute | solution.py:410
  156.1 9.7 %collective-permute-done.29 = bf16[1280,256]{1,0:T(8,128)(2,1)S(1)} collective-permute-done((bf16[1280,256]{1,0:T(8,128)(2,1)S(1)}, bf16[1280,256]{1,0:T(8,128)(2,1)S(1)}, u32[]{:S(2)}, u32[]{:S(2)}) %collective-permute-start.29) | collective-permute-done | bytes 655392 | tf_op jit(solution)/shard_map/ppermute | solution.py:411
  168.3 1.6 collective-permute-done.27
  (70 shorter events, 21.7 us)
Async XLA Ops:
  0.6 20.9 %collective-permute-start = (bf16[1280,256]{1,0:T(8,128)(2,1)}, bf16[1280,256]{1,0:T(8,128)(2,1)S(1)}, u32[]{:S(2)}, u32[]{:S(2)}) collective-permute-start(bf16[1280,256]{1,0:T(8,128)(2,1)} %refs_0_.1), channel_id=1, source_target_pairs={{0,8},{8,16},{16,24},{24,0},{1,9},{9,17},{17,25},{25,1},{2,10},{10... | collective-permute-start | bytes 1966088 | tf_op jit(solution)/shard_map/ppermute | solution.py:374
  3.7 30.4 %collective-permute-start.1 = (bf16[1280,256]{1,0:T(8,128)(2,1)}, bf16[1280,256]{1,0:T(8,128)(2,1)S(1)}, u32[]{:S(2)}, u32[]{:S(2)}) collective-permute-start(bf16[1280,256]{1,0:T(8,128)(2,1)} %refs_0_.1), channel_id=1, source_target_pairs={{0,24},{8,0},{16,8},{24,16},{1,25},{9,1},{17,9},{25,17},{2,26},{10... | collective-permute-start | bytes 1966088 | tf_op jit(solution)/shard_map/ppermute | solution.py:375
  5.8 28.4 %collective-permute-start.3 = (bf16[2560,128]{1,0:T(8,128)(2,1)}, bf16[2560,128]{1,0:T(8,128)(2,1)S(1)}, u32[]{:S(2)}, u32[]{:S(2)}) collective-permute-start(bf16[2560,128]{1,0:T(8,128)(2,1)} %refs_3_), channel_id=1, source_target_pairs={{0,4},{1,5},{2,6},{3,7},{4,0},{5,1},{6,2},{7,3},{8,12},{9,13},{10,... | collective-permute-start | bytes 1966088 | tf_op jit(solution)/shard_map/ppermute | solution.py:358
  7.5 26.7 %collective-permute-start.2 = (bf16[2560,128]{1,0:T(8,128)(2,1)}, bf16[2560,128]{1,0:T(8,128)(2,1)S(1)}, u32[]{:S(2)}, u32[]{:S(2)}) collective-permute-start(bf16[2560,128]{1,0:T(8,128)(2,1)} %refs_3_), channel_id=1, source_target_pairs={{0,2},{1,3},{2,0},{3,1},{4,6},{5,7},{6,4},{7,5},{8,10},{9,11},{10,... | collective-permute-start | bytes 1966088 | tf_op jit(solution)/shard_map/ppermute | solution.py:358
  9.0 28.5 %collective-permute-start.4 = (bf16[2560,128]{1,0:T(8,128)(2,1)}, bf16[2560,128]{1,0:T(8,128)(2,1)S(1)}, u32[]{:S(2)}, u32[]{:S(2)}) collective-permute-start(bf16[2560,128]{1,0:T(8,128)(2,1)} %refs_3_), channel_id=1, source_target_pairs={{0,6},{1,7},{2,4},{3,5},{4,2},{5,3},{6,0},{7,1},{8,14},{9,15},{10,... | collective-permute-start | bytes 1966088 | tf_op jit(solution)/shard_map/ppermute | solution.py:358
  37.4 4.5 %collective-permute-start.6 = (bf16[2560,128]{1,0:T(8,128)(2,1)S(1)}, bf16[2560,128]{1,0:T(8,128)(2,1)S(1)}, u32[]{:S(2)}, u32[]{:S(2)}) collective-permute-start(bf16[2560,128]{1,0:T(8,128)(2,1)S(1)} %collective-permute-done.2.refs_4_), channel_id=1, source_target_pairs={{0,1},{1,0},{2,3},{3,2},{4,5},{5,4},{6,7},{7,6},{8,9},{9,8},{10,11... | collective-permute-start | bytes 1966088 | tf_op jit(solution)/shard_map/ppermute | solution.py:358
  38.5 12.1 %collective-permute-start.9 = (bf16[1280,256]{1,0:T(8,128)(2,1)S(1)}, bf16[1280,256]{1,0:T(8,128)(2,1)S(1)}, u32[]{:S(2)}, u32[]{:S(2)}) collective-permute-start(bf16[1280,256]{1,0:T(8,128)(2,1)S(1)} %collective-permute-done.refs_1_), channel_id=1, source_target_pairs={{8,16},{16,24},{9,17},{17,25},{10,18},{18,26},{11,19},{19,27},{12,... | collective-permute-start | bytes 1966088 | tf_op jit(solution)/shard_map/ppermute | solution.py:378
  40.6 18.7 %collective-permute-start.10 = (bf16[1280,256]{1,0:T(8,128)(2,1)S(1)}, bf16[1280,256]{1,0:T(8,128)(2,1)S(1)}, u32[]{:S(2)}, u32[]{:S(2)}) collective-permute-start(bf16[1280,256]{1,0:T(8,128)(2,1)S(1)} %collective-permute-done.1.refs_2_), channel_id=1, source_target_pairs={{8,0},{16,8},{9,1},{17,9},{10,2},{18,10},{11,3},{19,11},{12,4},{20... | collective-permute-start | bytes 1966088 | tf_op jit(solution)/shard_map/ppermute | solution.py:379
  77.9 12.6 %collective-permute-start.14 = (f32[5,640]{1,0:T(8,128)S(1)}, f32[5,640]{1,0:T(8,128)S(1)}, u32[]{:S(2)}, u32[]{:S(2)}) collective-permute-start(f32[5,640]{1,0:T(8,128)S(1)} %add_select_fusion.refs_0_), channel_id=1, source_target_pairs={{0,6},{1,7},{2,4},{3,5},{4,2},{5,3},{6,0},{7,1},{8,14},{9,15},{10,... | collective-permute-start | bytes 38408 | tf_op jit(solution)/shard_map/ppermute | solution.py:358
  80.4 10.1 %collective-permute-start.13 = (f32[5,640]{1,0:T(8,128)S(1)}, f32[5,640]{1,0:T(8,128)S(1)}, u32[]{:S(2)}, u32[]{:S(2)}) collective-permute-start(f32[5,640]{1,0:T(8,128)S(1)} %add_select_fusion.refs_0_), channel_id=1, source_target_pairs={{0,4},{1,5},{2,6},{3,7},{4,0},{5,1},{6,2},{7,3},{8,12},{9,13},{10,... | collective-permute-start | bytes 38408 | tf_op jit(solution)/shard_map/ppermute | solution.py:358
  80.9 9.6 %collective-permute-start.12 = (f32[5,640]{1,0:T(8,128)S(1)}, f32[5,640]{1,0:T(8,128)S(1)}, u32[]{:S(2)}, u32[]{:S(2)}) collective-permute-start(f32[5,640]{1,0:T(8,128)S(1)} %add_select_fusion.refs_0_), channel_id=1, source_target_pairs={{0,2},{1,3},{2,0},{3,1},{4,6},{5,7},{6,4},{7,5},{8,10},{9,11},{10,... | collective-permute-start | bytes 38408 | tf_op jit(solution)/shard_map/ppermute | solution.py:358
  81.4 5.4 %collective-permute-start.17 = (f32[1,1280]{1,0:T(1,128)S(1)}, f32[1,1280]{1,0:T(1,128)S(1)}, u32[]{:S(2)}, u32[]{:S(2)}) collective-permute-start(f32[1,1280]{1,0:T(1,128)S(1)} %get-tuple-element.63.refs_4_), channel_id=1, source_target_pairs={{0,24},{8,16},{16,8},{24,0},{1,25},{9,17},{17,9},{25,1},{2,26},{10... | collective-permute-start | bytes 15368 | tf_op jit(solution)/shard_map/ppermute | solution.py:361
  81.4 5.4 %collective-permute-start.16 = (f32[1,1280]{1,0:T(1,128)S(1)}, f32[1,1280]{1,0:T(1,128)S(1)}, u32[]{:S(2)}, u32[]{:S(2)}) collective-permute-start(f32[1,1280]{1,0:T(1,128)S(1)} %get-tuple-element.63.refs_4_), channel_id=1, source_target_pairs={{0,16},{8,24},{16,0},{24,8},{1,17},{9,25},{17,1},{25,9},{2,18},{10... | collective-permute-start | bytes 15368 | tf_op jit(solution)/shard_map/ppermute | solution.py:361
  102.6 23.0 %collective-permute-start.19 = (bf16[1280,256]{1,0:T(8,128)(2,1)S(1)}, bf16[1280,256]{1,0:T(8,128)(2,1)S(1)}, u32[]{:S(2)}, u32[]{:S(2)}) collective-permute-start(bf16[1280,256]{1,0:T(8,128)(2,1)S(1)} %get-tuple-element.64), channel_id=1, source_target_pairs={{24,16},{16,8},{25,17},{17,9},{26,18},{18,10},{27,19},{19,11},{28,... | collective-permute-start | bytes 1966088 | tf_op jit(solution)/shard_map/ppermute | solution.py:396
  103.3 22.3 %collective-permute-start.18 = (bf16[1280,256]{1,0:T(8,128)(2,1)S(1)}, bf16[1280,256]{1,0:T(8,128)(2,1)S(1)}, u32[]{:S(2)}, u32[]{:S(2)}) collective-permute-start(bf16[1280,256]{1,0:T(8,128)(2,1)S(1)} %get-tuple-element.64), channel_id=1, source_target_pairs={{0,8},{8,16},{1,9},{9,17},{2,10},{10,18},{3,11},{11,19},{4,12},{12... | collective-permute-start | bytes 1966088 | tf_op jit(solution)/shard_map/ppermute | solution.py:395
  106.0 19.6 %collective-permute-start.20 = (f32[1,128]{1,0:T(1,128)S(1)}, f32[1,128]{1,0:T(1,128)S(1)}, u32[]{:S(2)}, u32[]{:S(2)}) collective-permute-start(f32[1,128]{1,0:T(1,128)S(1)} %get-tuple-element.74), channel_id=1, source_target_pairs={{0,9},{1,8},{2,11},{3,10},{4,13},{5,12},{6,15},{7,14},{8,1},{9,0},... | collective-permute-start | bytes 1544 | tf_op jit(solution)/shard_map/ppermute | solution.py:365
  125.6 7.5 %collective-permute-start.21 = (bf16[2560,512]{1,0:T(8,128)(2,1)}, bf16[2560,512]{1,0:T(8,128)(2,1)S(1)}, u32[]{:S(2)}, u32[]{:S(2)}) collective-permute-start(bf16[2560,512]{1,0:T(8,128)(2,1)} %get-tuple-element.81), channel_id=1, source_target_pairs={{0,1},{1,0},{2,3},{3,2},{4,5},{5,4},{6,7},{7,6},{8,9},{9,8},{10,11... | collective-permute-start | bytes 7864328 | tf_op jit(solution)/shard_map/ppermute | solution.py:358
  128.3 5.0 %collective-permute-start.24 = (f32[1,128]{1,0:T(1,128)S(1)}, f32[1,128]{1,0:T(1,128)S(1)}, u32[]{:S(2)}, u32[]{:S(2)}) collective-permute-start(f32[1,128]{1,0:T(1,128)S(1)} %add.64), channel_id=1, source_target_pairs={{0,6},{1,7},{2,4},{3,5},{4,2},{5,3},{6,0},{7,1},{8,14},{9,15},{10,... | collective-permute-start | bytes 1544 | tf_op jit(solution)/shard_map/ppermute | solution.py:358
  131.3 5.3 %collective-permute-start.22 = (f32[1,128]{1,0:T(1,128)S(1)}, f32[1,128]{1,0:T(1,128)S(1)}, u32[]{:S(2)}, u32[]{:S(2)}) collective-permute-start(f32[1,128]{1,0:T(1,128)S(1)} %add.64), channel_id=1, source_target_pairs={{0,18},{1,19},{2,16},{3,17},{4,22},{5,23},{6,20},{7,21},{8,26},{9,... | collective-permute-start | bytes 1544 | tf_op jit(solution)/shard_map/ppermute | solution.py:365
  136.6 19.5 %collective-permute-start.28 = (bf16[1280,256]{1,0:T(8,128)(2,1)S(1)}, bf16[1280,256]{1,0:T(8,128)(2,1)S(1)}, u32[]{:S(2)}, u32[]{:S(2)}) collective-permute-start(bf16[1280,256]{1,0:T(8,128)(2,1)S(1)} %add.65), channel_id=1, source_target_pairs={{0,8},{8,16},{16,24},{24,0},{1,9},{9,17},{17,25},{25,1},{2,10},{10... | collective-permute-start | bytes 1966088 | tf_op jit(solution)/shard_map/ppermute | solution.py:410
  136.6 29.1 %collective-permute-start.29 = (bf16[1280,256]{1,0:T(8,128)(2,1)S(1)}, bf16[1280,256]{1,0:T(8,128)(2,1)S(1)}, u32[]{:S(2)}, u32[]{:S(2)}) collective-permute-start(bf16[1280,256]{1,0:T(8,128)(2,1)S(1)} %add.66), channel_id=1, source_target_pairs={{0,24},{8,0},{16,8},{24,16},{1,25},{9,1},{17,9},{25,17},{2,26},{10... | collective-permute-start | bytes 1966088 | tf_op jit(solution)/shard_map/ppermute | solution.py:411
  140.4 26.5 %collective-permute-start.25 = (bf16[2560,128]{1,0:T(8,128)(2,1)S(1)}, bf16[2560,128]{1,0:T(8,128)(2,1)S(1)}, u32[]{:S(2)}, u32[]{:S(2)}) collective-permute-start(bf16[2560,128]{1,0:T(8,128)(2,1)S(1)} %get-tuple-element.89), channel_id=1, source_target_pairs={{0,2},{1,3},{2,0},{3,1},{4,6},{5,7},{6,4},{7,5},{8,10},{9,11},{10,... | collective-permute-start | bytes 1966088 | tf_op jit(solution)/shard_map/ppermute | solution.py:358
  141.0 27.3 %collective-permute-start.26 = (bf16[2560,128]{1,0:T(8,128)(2,1)S(1)}, bf16[2560,128]{1,0:T(8,128)(2,1)S(1)}, u32[]{:S(2)}, u32[]{:S(2)}) collective-permute-start(bf16[2560,128]{1,0:T(8,128)(2,1)S(1)} %get-tuple-element.90), channel_id=1, source_target_pairs={{0,4},{1,5},{2,6},{3,7},{4,0},{5,1},{6,2},{7,3},{8,12},{9,13},{10,... | collective-permute-start | bytes 1966088 | tf_op jit(solution)/shard_map/ppermute | solution.py:358
  142.5 27.4 %collective-permute-start.27 = (bf16[2560,128]{1,0:T(8,128)(2,1)S(1)}, bf16[2560,128]{1,0:T(8,128)(2,1)S(1)}, u32[]{:S(2)}, u32[]{:S(2)}) collective-permute-start(bf16[2560,128]{1,0:T(8,128)(2,1)S(1)} %get-tuple-element.91), channel_id=1, source_target_pairs={{0,6},{1,7},{2,4},{3,5},{4,2},{5,3},{6,0},{7,1},{8,14},{9,15},{10,... | collective-permute-start | bytes 1966088 | tf_op jit(solution)/shard_map/ppermute | solution.py:358
  (15 other events, 74.7 us)

commit v4 on v3

--- a/solution.py
+++ b/solution.py
@@ -66,7 +66,7 @@
         + [pl.BlockSpec((bm, piece.shape[1]), lambda i: (i, 0)) for piece, _ in image_pieces],
         out_specs=(pl.BlockSpec((bt, width), lambda i: (i, 0)), pl.BlockSpec((bm, width), lambda i: (i, 0))),
         compiler_params=params(),
-        cost_estimate=cost(10),
+        cost_estimate=cost(0.01),
         name="side_by_side",
     )(*[in_hbm(piece) for piece, _ in pieces])
 
@@ -113,8 +113,10 @@
                 u = d_scr[slot, at, :] * (logit_scale * log2e)
                 u_ref[at, :] = u
                 target = target_scr[at, :] - ids
+                found = jnp.zeros((strip, 128), jnp.float32)
                 for k, v in enumerate(lanes(u)):
-                    picked = picked + jnp.where(target == 128 * k, v, 0.0)
+                    found = jnp.where(target == 128 * k, v, found)
+                picked = picked + found
                 rm_scr[at, :] = functools.reduce(jnp.maximum, lanes(u))
                 new = jnp.maximum(new, jnp.max(u.reshape(strip // 8, 8, rows), axis=0))
             pos_scr[...] += picked
@@ -189,21 +191,15 @@
     )(in_hbm(images), texts, targets, *(() if far is None else far[0]))
 
 
-def weights_and_far(u, images, targets, row_lses, col_lses, slot, wide):
+def weights_and_far(u, images, targets, row_lses, col_lses, slot, wide, cuts):
     img_rows = images.shape[0]
     rows = u.shape[1]
     steps, bm = targets.shape
     n_row, n_col = len(row_lses), len(col_lses)
 
-    def now(i):
-        return jnp.minimum(i, steps - 1)
-
-    def before(i):
-        return jnp.maximum(i - 1, 0)
-
     def kernel(u_ref, images_ref, targets_ref, *refs):
         row_refs, col_refs, refs = refs[:n_row], refs[n_row : n_row + n_col], refs[n_row + n_col :]
-        w_ref, far_ref, loss_ref, w_scr, acc, row_ref, col_ref, row_scr, target_scr = refs
+        w_ref, loss_ref, *far_refs, acc, row_ref, col_ref, row_scr, target_scr = refs
         step = pl.program_id(0)
 
         @pl.when(step == 0)
@@ -217,60 +213,47 @@
             lane = lax.broadcasted_iota(jnp.int32, (1, 128), 1)
             loss_ref[...] = jnp.where(lane == 0, row_loss, jnp.where(lane == 1, col_loss, 0.0))
 
-        def elementwise():
-            row_scr[...] = jnp.broadcast_to(row_ref[pl.ds(step, 1), :], (128, bm)).T
-            target_scr[...] = jnp.broadcast_to(targets_ref[pl.ds(step, 1), :], (128, bm)).T
-            ids = lax.broadcasted_iota(jnp.int32, (strip, 128), 1)
-            col = col_ref[...]
-            for first in range(0, bm, strip):
+        row_scr[...] = jnp.broadcast_to(row_ref[pl.ds(step, 1), :], (128, bm)).T
+        target_scr[...] = jnp.broadcast_to(targets_ref[pl.ds(step, 1), :], (128, bm)).T
+        ids = lax.broadcasted_iota(jnp.int32, (strip, 128), 1)
+        col = col_ref[...]
+        for group in range(0, bm, 256):
+            end = min(group + 256, bm)
+            for first in range(group, end, strip):
                 at = slice(first, first + strip)
                 row = row_scr[at, :]
                 target = target_scr[at, :] - ids
                 for k in range(0, rows, 128):
                     v = u_ref[at, k : k + 128]
                     weight = jnp.exp2(v - row) + jnp.exp2(v - col[:, k : k + 128]) - jnp.where(target == k, 2.0, 0.0)
-                    weight = weight.astype(jnp.bfloat16)
-                    w_ref[at, k : k + 128] = weight
-                    w_scr[step % 2, at, k : k + 128] = weight
-
-        def matmul():
+                    w_ref[at, k : k + 128] = weight.astype(jnp.bfloat16)
             acc[...] += lax.dot_general(
-                w_scr[(step + 1) % 2],
-                images_ref[...],
+                w_ref[group:end, :],
+                images_ref[group:end, :],
                 (((0,), (0,)), ((), ())),
                 preferred_element_type=jnp.float32,
             )
 
-        @pl.when(step == 0)
-        def _():
-            elementwise()
-
-        @pl.when(jnp.logical_and(step > 0, step < steps))
-        def _():
-            elementwise()
-            matmul()
-
-        @pl.when(step == steps)
-        def _():
-            matmul()
-            far_ref[...] = (logit_scale * acc[...]).astype(jnp.bfloat16)
+        @pl.when(step == steps - 1)
+        def _():
+            for far_ref, first, end in zip(far_refs, cuts, cuts[1:]):
+                far_ref[...] = (logit_scale * acc[first:end, :]).astype(jnp.bfloat16)
 
     return pl.pallas_call(
         kernel,
-        grid=(steps + 1,),
+        grid=(steps,),
         out_shape=(
             pltpu.HBM((img_rows, rows), jnp.bfloat16),
-            jax.ShapeDtypeStruct((rows, wide), jnp.bfloat16),
             jax.ShapeDtypeStruct((1, 128), jnp.float32),
-        ),
+        )
+        + tuple(jax.ShapeDtypeStruct((end - first, wide), jnp.bfloat16) for first, end in zip(cuts, cuts[1:])),
         in_specs=[
-            pl.BlockSpec((bm, rows), lambda i: (now(i), 0)),
-            pl.BlockSpec((bm, wide), lambda i: (before(i), slot())),
+            pl.BlockSpec((bm, rows), lambda i: (i, 0)),
+            pl.BlockSpec((bm, wide), lambda i: (i, slot())),
         ]
         + [VMEM] * (1 + n_row + n_col),
-        out_specs=(pl.BlockSpec((bm, rows), lambda i: (now(i), 0)), VMEM, VMEM),
+        out_specs=(pl.BlockSpec((bm, rows), lambda i: (i, 0)), VMEM) + (VMEM,) * (len(cuts) - 1),
         scratch_shapes=[
-            pltpu.VMEM((2, bm, rows), jnp.bfloat16),
             pltpu.VMEM((rows, wide), jnp.float32),
             pltpu.VMEM((steps, bm), jnp.float32),
             pltpu.VMEM((1, rows), jnp.float32),
@@ -283,27 +266,32 @@
     )(in_hbm(u), in_hbm(images), targets, *row_lses, *col_lses)
 
 
-def gradients(weights, images, texts, slots, text_wide, groups):
+def gradients(weights, images, texts, slots, text_wide, groups, order, microseconds=10):
     img_rows, rows = weights.shape
-    width = texts.shape[1]
+    width = images.shape[1]
     steps = 4
     bm = img_rows // steps
-    wide = width // sum(len(group) for group in groups)
+    wide = width // max(1, sum(len(group) for group in groups))
     n_text = len(slots)
 
-    def kernel(w_ref, texts_ref, *refs):
+    def kernel(w_ref, _, *refs):
+        if groups:
+            texts_ref, *refs = refs
         image_refs, text_outs, (*image_outs, acc, image_acc) = refs[:n_text], refs[n_text : 2 * n_text], refs[2 * n_text :]
         step = pl.program_id(0)
 
-        @pl.when(step == 0)
-        def _():
-            acc[...] = jnp.zeros(acc.shape, jnp.float32)
+        if slots:
+
+            @pl.when(step == 0)
+            def _():
+                acc[...] = jnp.zeros(acc.shape, jnp.float32)
 
         for k, image_ref in enumerate(image_refs):
             acc[k] += lax.dot_general(
                 w_ref[...], image_ref[...], (((0,), (0,)), ((), ())), preferred_element_type=jnp.float32
             )
-        image_acc[...] = logit_scale * jnp.dot(w_ref[...], texts_ref[...], preferred_element_type=jnp.float32)
+        if groups:
+            image_acc[...] = logit_scale * jnp.dot(w_ref[...], texts_ref[...], preferred_element_type=jnp.float32)
         for out, group in zip(image_outs, groups):
             for k, slot in enumerate(group):
                 out[:, k * wide : (k + 1) * wide] = image_acc[:, columns(slot(), wide)].astype(jnp.bfloat16)
@@ -321,16 +309,16 @@
         grid=(steps,),
         out_shape=(jax.ShapeDtypeStruct((rows, text_wide), jnp.bfloat16),) * n_text
         + tuple(jax.ShapeDtypeStruct((img_rows, wide * len(group)), jnp.bfloat16) for group in groups),
-        in_specs=[pl.BlockSpec((bm, rows), lambda i: (i, 0)), VMEM] + [image_spec(slot) for slot in slots],
+        in_specs=[pl.BlockSpec((bm, rows), lambda i: (i, 0)), VMEM] + [VMEM] * bool(groups) + [image_spec(slot) for slot in slots],
         out_specs=(VMEM,) * n_text + tuple(pl.BlockSpec((bm, wide * len(g)), lambda i: (i, 0)) for g in groups),
         scratch_shapes=[
-            pltpu.VMEM((n_text, rows, text_wide), jnp.float32),
+            pltpu.VMEM((max(1, n_text), rows, text_wide), jnp.float32),
             pltpu.VMEM((bm, width), jnp.float32),
         ],
         compiler_params=params(),
-        cost_estimate=cost(18),
+        cost_estimate=cost(microseconds),
         name="gradients",
-    )(in_hbm(weights), texts, *[in_hbm(images)] * n_text)
+    )(in_hbm(weights), order, *([texts] if groups else []), *[in_hbm(images)] * n_text)
 
 
 def together(*values):
@@ -374,15 +362,15 @@
     from_prev = lax.ppermute(texts, "img", shifted(4, 1))
     from_next = lax.ppermute(texts, "img", shifted(4, -1))
     parts = [images, swap(images, 2), swap(images, 4), swap(images, 6)]
-    targets, from_prev, from_next, *parts = together(targets, from_prev, from_next, *parts)
-    from_below = lax.ppermute(from_prev, "img", [(1, 2), (2, 3)])
-    from_above = lax.ppermute(from_next, "img", [(1, 0), (2, 1)])
+    is_first = lax.axis_index("img") == 1
+    from_middle = lax.ppermute(jnp.where(is_first, from_prev, from_next), "img", [(1, 2), (2, 1)])
+    from_inner = lax.ppermute(jnp.where(is_first, from_next, from_prev), "img", [(1, 0), (2, 3)])
     parts += [swap(part, 1) for part in parts]
     image_pieces = [(part, txt_slot(flip)) for part, flip in zip(parts, (0, 2, 4, 6, 1, 3, 5, 7))]
     text_pieces = [(texts, img_slot(0)), (from_prev, img_slot(3)), (from_next, img_slot(1))]
     most_txt, whole_img = side_by_side(image_pieces, text_pieces, width)
-    from_below, from_above, most_txt = together(from_below, from_above, most_txt)
-    far = ((from_below, from_above), img_slot(2), lambda: lax.axis_index("img") >= 2)
+    from_middle, from_inner, most_txt, whole_img = together(from_middle, from_inner, most_txt, whole_img)
+    far = ((from_middle, from_inner), img_slot(2), lambda: lax.rem(lax.axis_index("img"), 3) > 0)
     u, row, col, whole_txt = logits_and_stats(whole_img, most_txt, far, targets)
 
     other = swap(row, 1)
@@ -391,27 +379,32 @@
     rows = [row] + [swap(row, by) for by in (2, 4, 6)]
     cols = [col] + [over_z(col, by) for by in (1, 2, 3)]
 
-    w, far_grad, loss = weights_and_far(u, whole_img, targets, rows, cols, img_slot(2), quarter)
-    below = lax.ppermute(far_grad, "img", [(0, 1), (1, 2)])
-    above = lax.ppermute(far_grad, "img", [(3, 2), (2, 1)])
+    w, loss, far_grad = weights_and_far(u, whole_img, targets, rows, cols, img_slot(2), quarter, (0, txt_rows))
+    middle = lax.ppermute(far_grad, "img", [(1, 2), (2, 1)])
+    outer = lax.ppermute(far_grad, "img", [(0, 1), (3, 2)])
     image_groups = [[txt_slot(flip)] for flip in (0, 2, 4, 6)] + [[txt_slot(flip) for flip in (1, 3, 5, 7)]]
-    text_slots = [img_slot(1), img_slot(3), img_slot(0)]
-    to_next, to_prev, own, *image_parts = gradients(w, whole_img, whole_txt, text_slots, quarter, image_groups)
+    to_next, to_prev, *image_parts = gradients(
+        w, whole_img, whole_txt, [img_slot(1), img_slot(3)], quarter, image_groups, row
+    )
     loss += across(loss, 1, 1)
-    below, above, to_next, to_prev, *image_parts, loss = together(below, above, to_next, to_prev, *image_parts, loss)
+    middle, outer, to_next, to_prev, *image_parts, loss = together(
+        middle, outer, to_next, to_prev, *image_parts, loss
+    )
 
     other = swap(image_parts.pop(), 1)
+    loss += across(loss, 2, 2)
+    to_next += jnp.where(is_first, outer, middle)
+    to_prev += jnp.where(is_first, middle, outer)
     eighth = width // 8
     s, x, y, d = [part + other[:, j * eighth : (j + 1) * eighth] for j, part in enumerate(image_parts)]
-    losses = [across(loss, 2, 2), swap(loss, 4), swap(loss, 6)]
-    to_next, to_prev = to_next + below, to_prev + above
-    to_next, to_prev, s, x, y, d, *losses = together(to_next, to_prev, s, x, y, d, *losses)
+    to_next, to_prev, s, x, y, d, loss = together(to_next, to_prev, s, x, y, d, loss)
 
     from_prev = lax.ppermute(to_next, "img", shifted(4, 1))
     from_next = lax.ppermute(to_prev, "img", shifted(4, -1))
+    own = gradients(w, whole_img, None, [img_slot(0)], quarter, [], loss, 0.01)[0]
     image_grad = as_bf16_sum(s, swap(x, 2), swap(y, 4), swap(d, 6))
     text_grad = as_bf16_sum(own, from_prev, from_next)
-    loss = (loss + losses[0])[0, 0] + (loss + sum(losses))[0, 1]
+    loss = loss[0, 0] + (loss + swap(loss, 4))[0, 1]
     return loss * (ln2 / (2.0 * txt_rows * 8)), image_grad, text_grad
 
 
@@ -433,8 +426,8 @@
     targets = (positive - lax.axis_index("txt") * txt_rows).reshape(4, whole_img.shape[0] // 4)
     u, row, col, whole_txt = logits_and_stats(whole_img, whole_txt, None, targets)
     rows, cols = gathered(row, "txt"), gathered(col, "img")
-    w, _, loss = weights_and_far(u, whole_img, targets, rows, cols, first_slot, 256)
-    text_part, image_part = gradients(w, whole_img, whole_txt, [first_slot], width, [[first_slot]])
+    w, loss, _ = weights_and_far(u, whole_img, targets, rows, cols, first_slot, 256, (0, txt_rows))
+    text_part, image_part = gradients(w, whole_img, whole_txt, [first_slot], width, [[first_slot]], row)
     loss = lax.psum(loss[0, 0] / n_txt + loss[0, 1] / n_img, ("img", "txt"))
     mean_loss = loss * (ln2 / (2.0 * txt_rows * n_txt))
     image_grad = lax.psum_scatter(image_part, "txt", scatter_dimension=1, tiled=True)

time: 173 us -> 167 us (0.965)
  waiting for transfers between devices: 74.4 us -> 59.8 us
  starting transfers between devices: 33.7 us -> 40.9 us
  Pallas kernels: 55.6 us -> 58 us
    ppermute x1, waiting for transfers between devices: 12.6 us -> 0.01 us  [per_device_4x8(): from_next = lax.ppermute(texts, 'img', shifted(4, -1))]
    ppermute x1, waiting for transfers between devices: 10.9 us -> 3.42 us  [per_device_4x8(): from_prev = lax.ppermute(to_next, 'img', shifted(4, 1))]
    ppermute x17 -> x16, waiting for transfers between devices: 11.7 us -> 18.8 us  [swap(): return lax.ppermute(part, 'txt', paired(8, by))]
    ppermute x3, starting transfers between devices: 2.07 us -> 8.17 us  [over_z(): return lax.ppermute(part, 'img', paired(4, by))]
    ppermute x3, waiting for transfers between devices: 6.97 us -> 1.6 us  [over_z(): return lax.ppermute(part, 'img', paired(4, by))]
    pallas_call x1 -> x2, Pallas kernels: 19.5 us -> 22.5 us  [gradients(): pl.pallas_call(kernel, grid=(steps,), out_shape=(jax.ShapeDtypeStruct((ro...]
    ppermute x17 -> x16, starting transfers between devices: 17.2 us -> 15 us  [swap(): return lax.ppermute(part, 'txt', paired(8, by))]
    ppermute x2, starting transfers between devices: 0.07 us -> 1.89 us  [across(): return lax.ppermute(part, ('img', 'txt'), pairs)]
  transfers between devices with their start and end apart: 30 -> 29, of which waited for: 16 -> 11; matrix products, arithmetic and copies ran while one was open for 2% -> 2% of each run, Pallas kernels for 15% -> 17%
where the time goes in v4:
time: 167 us
  waiting for transfers between devices  59.8 us (36%)
  Pallas kernels  58 us (35%)
  starting transfers between devices  40.9 us (24%)
  other arithmetic  4.24 us (3%)
  between operations  2.64 us (2%)
    pallas_call x2, Pallas kernels, gradients(): pl.pallas_call(kernel, grid=(steps,), out_shape=(jax.ShapeDtypeStruct((ro...  22.5 us
    ppermute x16, waiting for transfers between devices, swap(): return lax.ppermute(part, 'txt', paired(8, by))  18.8 us
    pallas_call x1, Pallas kernels, logits_and_stats(): pl.pallas_call(kernel, grid=(steps + 1,), out_shape=(pltpu.HBM((img_rows,...  17.2 us
    ppermute x16, starting transfers between devices, swap(): return lax.ppermute(part, 'txt', paired(8, by))  15 us
    ppermute x1, waiting for transfers between devices, per_device_4x8(): from_prev = lax.ppermute(texts, 'img', shifted(4, 1))  12.2 us
    pallas_call x1, Pallas kernels, weights_and_far(): pl.pallas_call(kernel, grid=(steps,), out_shape=(pltpu.HBM((img_rows, row...  11.6 us
    ppermute x1, waiting for transfers between devices, per_device_4x8(): from_next = lax.ppermute(to_prev, 'img', shifted(4, -1))  11.1 us
    ppermute x1, waiting for transfers between devices, per_device_4x8(): lax.ppermute(jnp.where(is_first, from_next, from_prev), 'img', [(1, 0), (...  9.22 us
  transfers between devices with their start and end apart: 29, of which 11 were waited for; matrix products, arithmetic and copies ran while one was open for 2% of the time, Pallas kernels for 17%

profile of v4, /device:TPU:0, one launch (start us, length us, event | category | flops | bytes accessed | tf_op | source)
XLA Modules:
  0.0 167.1 jit_solution(11208511328730073324)
XLA Ops:
  0.6 3.1 %collective-permute-start = (bf16[1280,256]{1,0:T(8,128)(2,1)}, bf16[1280,256]{1,0:T(8,128)(2,1)S(1)}, u32[]{:S(2)}, u32[]{:S(2)}) collective-permute-start(bf16[1280,256]{1,0:T(8,128)(2,1)} %refs_0_.1), channel_id=1, source_target_pairs={{0,8},{8,16},{16,24},{24,0},{1,9},{9,17},{17,25},{25,1},{2,10},{10... | collective-permute-start | bytes 1966088 | tf_op jit(solution)/shard_map/ppermute | solution.py:362
  3.7 2.4 %collective-permute-start.6 = (bf16[2560,128]{1,0:T(8,128)(2,1)}, bf16[2560,128]{1,0:T(8,128)(2,1)S(1)}, u32[]{:S(2)}, u32[]{:S(2)}) collective-permute-start(bf16[2560,128]{1,0:T(8,128)(2,1)} %refs_3_.1), channel_id=1, source_target_pairs={{0,6},{1,7},{2,4},{3,5},{4,2},{5,3},{6,0},{7,1},{8,14},{9,15},{10,... | collective-permute-start | bytes 1966088 | tf_op jit(solution)/shard_map/ppermute | solution.py:346
  7.2 2.1 %collective-permute-start.1 = (bf16[1280,256]{1,0:T(8,128)(2,1)}, bf16[1280,256]{1,0:T(8,128)(2,1)S(1)}, u32[]{:S(2)}, u32[]{:S(2)}) collective-permute-start(bf16[1280,256]{1,0:T(8,128)(2,1)} %refs_0_.1), channel_id=1, source_target_pairs={{0,24},{8,0},{16,8},{24,16},{1,25},{9,1},{17,9},{25,17},{2,26},{10... | collective-permute-start | bytes 1966088 | tf_op jit(solution)/shard_map/ppermute | solution.py:363
  9.3 12.2 %collective-permute-done.refs_1_ = bf16[1280,256]{1,0:T(8,128)(2,1)S(1)} collective-permute-done((bf16[1280,256]{1,0:T(8,128)(2,1)}, bf16[1280,256]{1,0:T(8,128)(2,1)S(1)}, u32[]{:S(2)}, u32[]{:S(2)}) %collective-permute-start) | collective-permute-done | bytes 655392 | tf_op jit(solution)/shard_map/ppermute | solution.py:362
  22.5 12.6 %collective-permute-done.5.refs_5_ = bf16[2560,128]{1,0:T(8,128)(2,1)} collective-permute-done((bf16[2560,128]{1,0:T(8,128)(2,1)}, bf16[2560,128]{1,0:T(8,128)(2,1)}, u32[]{:S(2)}, u32[]{:S(2)}) %collective-permute-start.5) | collective-permute-done | bytes 655392 | tf_op jit(solution)/shard_map/ppermute | solution.py:346
  39.9 6.7 %side_by_side.1 = (bf16[1280,1024]{1,0:T(8,128)(2,1)S(1)}, bf16[2560,1024]{1,0:T(8,128)(2,1)}) custom-call(bf16[1280,256]{1,0:T(8,128)(2,1)} %refs_0_.1, bf16[1280,256]{1,0:T(8,128)(2,1)} %copy-done, bf16[1280,256]{1,0:T(8,128)(2,1)} %copy-done.1, bf16[2560,128]{1,0:T(8,128)(2,1)} %refs_3_.1, bf16[2560,128]{1,0:T(8,128)(2,1)} %collective-permute-done.4.refs_4_, ...), custom_call_target="tpu_custom_call" | custom-call | flops 11000000 | bytes 1 | tf_op jit(solution)/shard_map/side_by_side/pallas_call | solution.py:58
  46.6 9.2 %collective-permute-done.3.refs_1_ = bf16[1280,256]{1,0:T(8,128)(2,1)S(1)} collective-permute-done((bf16[1280,256]{1,0:T(8,128)(2,1)}, bf16[1280,256]{1,0:T(8,128)(2,1)S(1)}, u32[]{:S(2)}, u32[]{:S(2)}) %collective-permute-start.3) | collective-permute-done | bytes 655392 | tf_op jit(solution)/shard_map/ppermute | solution.py:367
  55.8 17.2 %logits_and_stats.1 = (f32[2560,1280]{1,0:T(8,128)}, f32[5,640]{1,0:T(8,128)S(1)}, f32[1,1280]{1,0:T(1,128)S(1)}, bf16[1280,1024]{1,0:T(8,128)(2,1)}) custom-call(bf16[2560,1024]{1,0:T(8,128)(2,1)} %get-tuple-element.42.images_ref.refs_1_.refs_2_.refs_0_, bf16[1280,1024]{1,0:T(8,128)(2,1)S(1)} %get-tuple-element.43.texts_ref, ...), custom_call_target="tpu_custom_call" | custom-call | flops 14300000256 | bytes 1 | tf_op jit(solution)/shard_map/logits_and_stats/pallas_call | solution.py:167
  74.3 1.7 %collective-permute-start.14 = (f32[5,640]{1,0:T(8,128)S(1)}, f32[5,640]{1,0:T(8,128)S(1)}, u32[]{:S(2)}, u32[]{:S(2)}) collective-permute-start(f32[5,640]{1,0:T(8,128)S(1)} %add_select_fusion.refs_0_._), channel_id=1, source_target_pairs={{0,6},{1,7},{2,4},{3,5},{4,2},{5,3},{6,0},{7,1},{8,14},{9,15},{10,... | collective-permute-start | bytes 38408 | tf_op jit(solution)/shard_map/ppermute | solution.py:346
  77.8 2.4 %collective-permute-start.17 = (f32[1,1280]{1,0:T(1,128)S(1)}, f32[1,1280]{1,0:T(1,128)S(1)}, u32[]{:S(2)}, u32[]{:S(2)}) collective-permute-start(f32[1,1280]{1,0:T(1,128)S(1)} %get-tuple-element.48.refs_4_), channel_id=1, source_target_pairs={{0,24},{8,16},{16,8},{24,0},{1,25},{9,17},{17,9},{25,1},{2,26},{10... | collective-permute-start | bytes 15368 | tf_op jit(solution)/shard_map/ppermute | solution.py:349
  80.2 3.6 %collective-permute-start.16 = (f32[1,1280]{1,0:T(1,128)S(1)}, f32[1,1280]{1,0:T(1,128)S(1)}, u32[]{:S(2)}, u32[]{:S(2)}) collective-permute-start(f32[1,1280]{1,0:T(1,128)S(1)} %get-tuple-element.48.refs_4_), channel_id=1, source_target_pairs={{0,16},{8,24},{16,0},{24,8},{1,17},{9,25},{17,1},{25,9},{2,18},{10... | collective-permute-start | bytes 15368 | tf_op jit(solution)/shard_map/ppermute | solution.py:349
  83.8 2.2 %collective-permute-start.15 = (f32[1,1280]{1,0:T(1,128)S(1)}, f32[1,1280]{1,0:T(1,128)S(1)}, u32[]{:S(2)}, u32[]{:S(2)}) collective-permute-start(f32[1,1280]{1,0:T(1,128)S(1)} %get-tuple-element.48.refs_4_), channel_id=1, source_target_pairs={{0,8},{8,0},{16,24},{24,16},{1,9},{9,1},{17,25},{25,17},{2,10},{10... | collective-permute-start | bytes 15368 | tf_op jit(solution)/shard_map/ppermute | solution.py:349
  87.6 11.6 %weights_and_far.1 = (bf16[2560,1280]{1,0:T(8,128)(2,1)}, f32[1,128]{1,0:T(1,128)S(1)}, bf16[1280,256]{1,0:T(8,128)(2,1)S(1)}) custom-call(f32[2560,1280]{1,0:T(8,128)} %get-tuple-element.46.u_ref, bf16[2560,1024]{1,0:T(8,128)(2,1)} %get-tuple-element.42.images_ref.refs_1_.refs_2_.refs_0_, s32[4,640]{1,0:T(4,128)S(1)} %reshape.12.targets_ref, ...), custom_call_target="tpu_custom_call" | custom-call | flops 8800000000 | bytes 1 | tf_op jit(solution)/shard_map/weights_and_far/pallas_call | solution.py:242
  99.2 4.0 %collective-permute-start.19 = (bf16[1280,256]{1,0:T(8,128)(2,1)S(1)}, bf16[1280,256]{1,0:T(8,128)(2,1)S(1)}, u32[]{:S(2)}, u32[]{:S(2)}) collective-permute-start(bf16[1280,256]{1,0:T(8,128)(2,1)S(1)} %get-tuple-element.49), channel_id=1, source_target_pairs={{0,8},{24,16},{1,9},{25,17},{2,10},{26,18},{3,11},{27,19},{4,12},{... | collective-permute-start | bytes 1966088 | tf_op jit(solution)/shard_map/ppermute | solution.py:384
  104.1 17.0 %gradients.2 = (bf16[1280,256]{1,0:T(8,128)(2,1)S(1)}, bf16[1280,256]{1,0:T(8,128)(2,1)S(1)}, bf16[2560,128]{1,0:T(8,128)(2,1)S(1)}, bf16[2560,128]{1,0:T(8,128)...) custom-call(bf16[2560,1280]{1,0:T(8,128)(2,1)} %get-tuple-element.50.w_ref, ...), custom_call_target="tpu_custom_call" | custom-call | flops 11000000512 | bytes 1 | tf_op jit(solution)/shard_map/gradients/pallas_call | solution.py:307
  121.2 2.2 %collective-permute-start.21 = (bf16[2560,512]{1,0:T(8,128)(2,1)}, bf16[2560,512]{1,0:T(8,128)(2,1)S(1)}, u32[]{:S(2)}, u32[]{:S(2)}) collective-permute-start(bf16[2560,512]{1,0:T(8,128)(2,1)} %get-tuple-element.65), channel_id=1, source_target_pairs={{0,1},{1,0},{2,3},{3,2},{4,5},{5,4},{6,7},{7,6},{8,9},{9,8},{10,11... | collective-permute-start | bytes 7864328 | tf_op jit(solution)/shard_map/ppermute | solution.py:346
  123.4 1.8 %collective-permute-start.22 = (f32[1,128]{1,0:T(1,128)S(1)}, f32[1,128]{1,0:T(1,128)S(1)}, u32[]{:S(2)}, u32[]{:S(2)}) collective-permute-start(f32[1,128]{1,0:T(1,128)S(1)} %add.58), channel_id=1, source_target_pairs={{0,18},{1,19},{2,16},{3,17},{4,22},{5,23},{6,20},{7,21},{8,26},{9,... | collective-permute-start | bytes 1544 | tf_op jit(solution)/shard_map/ppermute | solution.py:353
  125.3 3.4 %collective-permute-done.22 = f32[1,128]{1,0:T(1,128)S(1)} collective-permute-done((f32[1,128]{1,0:T(1,128)S(1)}, f32[1,128]{1,0:T(1,128)S(1)}, u32[]{:S(2)}, u32[]{:S(2)}) %collective-permute-start.22) | collective-permute-done | bytes 544 | tf_op jit(solution)/shard_map/ppermute | solution.py:353
  129.2 3.8 %collective-permute-start.28 = (bf16[1280,256]{1,0:T(8,128)(2,1)S(1)}, bf16[1280,256]{1,0:T(8,128)(2,1)S(1)}, u32[]{:S(2)}, u32[]{:S(2)}) collective-permute-start(bf16[1280,256]{1,0:T(8,128)(2,1)S(1)} %get-tuple-element.76), channel_id=1, source_target_pairs={{0,24},{8,0},{16,8},{24,16},{1,25},{9,1},{17,9},{25,17},{2,26},{10... | collective-permute-start | bytes 1966088 | tf_op jit(solution)/shard_map/ppermute | solution.py:403
  136.6 1.9 %collective-permute-start.26 = (bf16[2560,128]{1,0:T(8,128)(2,1)S(1)}, bf16[2560,128]{1,0:T(8,128)(2,1)S(1)}, u32[]{:S(2)}, u32[]{:S(2)}) collective-permute-start(bf16[2560,128]{1,0:T(8,128)(2,1)S(1)} %get-tuple-element.74), channel_id=1, source_target_pairs={{0,6},{1,7},{2,4},{3,5},{4,2},{5,3},{6,0},{7,1},{8,14},{9,15},{10,... | collective-permute-start | bytes 1966088 | tf_op jit(solution)/shard_map/ppermute | solution.py:346
  138.4 5.5 %gradients.3 = bf16[1280,256]{1,0:T(8,128)(2,1)S(1)} custom-call(bf16[2560,1280]{1,0:T(8,128)(2,1)} %get-tuple-element.50.w_ref, f32[1,128]{1,0:T(1,128)S(1)} %add.65._, bf16[2560,1024]{1,0:T(8,128)(2,1)} %get-tuple-element.42.images_ref.refs_1_.refs_2_.refs_0_), custom_call_target="tpu_custom_call" | custom-call | flops 11000000 | bytes 1 | tf_op jit(solution)/shard_map/gradients/pallas_call | solution.py:307
  145.2 3.4 %collective-permute-done.27 = bf16[1280,256]{1,0:T(8,128)(2,1)S(1)} collective-permute-done((bf16[1280,256]{1,0:T(8,128)(2,1)S(1)}, bf16[1280,256]{1,0:T(8,128)(2,1)S(1)}, u32[]{:S(2)}, u32[]{:S(2)}) %collective-permute-start.27) | collective-permute-done | bytes 655392 | tf_op jit(solution)/shard_map/ppermute | solution.py:402
  148.6 11.1 %collective-permute-done.28 = bf16[1280,256]{1,0:T(8,128)(2,1)S(1)} collective-permute-done((bf16[1280,256]{1,0:T(8,128)(2,1)S(1)}, bf16[1280,256]{1,0:T(8,128)(2,1)S(1)}, u32[]{:S(2)}, u32[]{:S(2)}) %collective-permute-start.28) | collective-permute-done | bytes 655392 | tf_op jit(solution)/shard_map/ppermute | solution.py:403
  160.9 3.9 %collective-permute-done.25 = bf16[2560,128]{1,0:T(8,128)(2,1)S(1)} collective-permute-done((bf16[2560,128]{1,0:T(8,128)(2,1)S(1)}, bf16[2560,128]{1,0:T(8,128)(2,1)S(1)}, u32[]{:S(2)}, u32[]{:S(2)}) %collective-permute-start.25) | collective-permute-done | bytes 655392 | tf_op jit(solution)/shard_map/ppermute | solution.py:346
  (62 shorter events, 19.4 us)
Async XLA Ops:
  0.6 20.9 %collective-permute-start = (bf16[1280,256]{1,0:T(8,128)(2,1)}, bf16[1280,256]{1,0:T(8,128)(2,1)S(1)}, u32[]{:S(2)}, u32[]{:S(2)}) collective-permute-start(bf16[1280,256]{1,0:T(8,128)(2,1)} %refs_0_.1), channel_id=1, source_target_pairs={{0,8},{8,16},{16,24},{24,0},{1,9},{9,17},{17,25},{25,1},{2,10},{10... | collective-permute-start | bytes 1966088 | tf_op jit(solution)/shard_map/ppermute | solution.py:362
  3.7 18.8 %collective-permute-start.6 = (bf16[2560,128]{1,0:T(8,128)(2,1)}, bf16[2560,128]{1,0:T(8,128)(2,1)S(1)}, u32[]{:S(2)}, u32[]{:S(2)}) collective-permute-start(bf16[2560,128]{1,0:T(8,128)(2,1)} %refs_3_.1), channel_id=1, source_target_pairs={{0,6},{1,7},{2,4},{3,5},{4,2},{5,3},{6,0},{7,1},{8,14},{9,15},{10,... | collective-permute-start | bytes 1966088 | tf_op jit(solution)/shard_map/ppermute | solution.py:346
  6.2 29.0 %collective-permute-start.5 = (bf16[2560,128]{1,0:T(8,128)(2,1)}, bf16[2560,128]{1,0:T(8,128)(2,1)}, u32[]{:S(2)}, u32[]{:S(2)}) collective-permute-start(bf16[2560,128]{1,0:T(8,128)(2,1)} %refs_3_.1), channel_id=1, source_target_pairs={{0,4},{1,5},{2,6},{3,7},{4,0},{5,1},{6,2},{7,3},{8,12},{9,13},{10,... | collective-permute-start | bytes 1966088 | tf_op jit(solution)/shard_map/ppermute | solution.py:346
  6.7 28.6 %collective-permute-start.4 = (bf16[2560,128]{1,0:T(8,128)(2,1)}, bf16[2560,128]{1,0:T(8,128)(2,1)}, u32[]{:S(2)}, u32[]{:S(2)}) collective-permute-start(bf16[2560,128]{1,0:T(8,128)(2,1)} %refs_3_.1), channel_id=1, source_target_pairs={{0,2},{1,3},{2,0},{3,1},{4,6},{5,7},{6,4},{7,5},{8,10},{9,11},{10,... | collective-permute-start | bytes 1966088 | tf_op jit(solution)/shard_map/ppermute | solution.py:346
  7.2 28.5 %collective-permute-start.1 = (bf16[1280,256]{1,0:T(8,128)(2,1)}, bf16[1280,256]{1,0:T(8,128)(2,1)S(1)}, u32[]{:S(2)}, u32[]{:S(2)}) collective-permute-start(bf16[1280,256]{1,0:T(8,128)(2,1)} %refs_0_.1), channel_id=1, source_target_pairs={{0,24},{8,0},{16,8},{24,16},{1,25},{9,1},{17,9},{25,17},{2,26},{10... | collective-permute-start | bytes 1966088 | tf_op jit(solution)/shard_map/ppermute | solution.py:363
  21.6 16.7 %collective-permute-start.7 = (bf16[2560,128]{1,0:T(8,128)(2,1)}, bf16[2560,128]{1,0:T(8,128)(2,1)S(1)}, u32[]{:S(2)}, u32[]{:S(2)}) collective-permute-start(bf16[2560,128]{1,0:T(8,128)(2,1)} %refs_3_.1), channel_id=1, source_target_pairs={{0,1},{1,0},{2,3},{3,2},{4,5},{5,4},{6,7},{7,6},{8,9},{9,8},{10,11... | collective-permute-start | bytes 1966088 | tf_op jit(solution)/shard_map/ppermute | solution.py:346
  22.5 17.3 %collective-permute-start.10 = (bf16[2560,128]{1,0:T(8,128)(2,1)S(1)}, bf16[2560,128]{1,0:T(8,128)(2,1)}, u32[]{:S(2)}, u32[]{:S(2)}) collective-permute-start(bf16[2560,128]{1,0:T(8,128)(2,1)S(1)} %collective-permute-done.6.refs_6_), channel_id=1, source_target_pairs={{0,1},{1,0},{2,3},{3,2},{4,5},{5,4},{6,7},{7,6},{8,9},{9,8},{10,11... | collective-permute-start | bytes 1966088 | tf_op jit(solution)/shard_map/ppermute | solution.py:346
  37.0 18.8 %collective-permute-start.3 = (bf16[1280,256]{1,0:T(8,128)(2,1)}, bf16[1280,256]{1,0:T(8,128)(2,1)S(1)}, u32[]{:S(2)}, u32[]{:S(2)}) collective-permute-start(bf16[1280,256]{1,0:T(8,128)(2,1)} %get-tuple-element.83), channel_id=1, source_target_pairs={{8,0},{16,24},{9,1},{17,25},{10,2},{18,26},{11,3},{19,27},{12,4},{... | collective-permute-start | bytes 1966088 | tf_op jit(solution)/shard_map/ppermute | solution.py:367
  39.1 16.7 %collective-permute-start.2 = (bf16[1280,256]{1,0:T(8,128)(2,1)}, bf16[1280,256]{1,0:T(8,128)(2,1)S(1)}, u32[]{:S(2)}, u32[]{:S(2)}) collective-permute-start(bf16[1280,256]{1,0:T(8,128)(2,1)} %get-tuple-element.84), channel_id=1, source_target_pairs={{8,16},{16,8},{9,17},{17,9},{10,18},{18,10},{11,19},{19,11},{12,20... | collective-permute-start | bytes 1966088 | tf_op jit(solution)/shard_map/ppermute | solution.py:366
  74.3 13.3 %collective-permute-start.14 = (f32[5,640]{1,0:T(8,128)S(1)}, f32[5,640]{1,0:T(8,128)S(1)}, u32[]{:S(2)}, u32[]{:S(2)}) collective-permute-start(f32[5,640]{1,0:T(8,128)S(1)} %add_select_fusion.refs_0_._), channel_id=1, source_target_pairs={{0,6},{1,7},{2,4},{3,5},{4,2},{5,3},{6,0},{7,1},{8,14},{9,15},{10,... | collective-permute-start | bytes 38408 | tf_op jit(solution)/shard_map/ppermute | solution.py:346
  76.0 11.6 %collective-permute-start.13 = (f32[5,640]{1,0:T(8,128)S(1)}, f32[5,640]{1,0:T(8,128)S(1)}, u32[]{:S(2)}, u32[]{:S(2)}) collective-permute-start(f32[5,640]{1,0:T(8,128)S(1)} %add_select_fusion.refs_0_._), channel_id=1, source_target_pairs={{0,4},{1,5},{2,6},{3,7},{4,0},{5,1},{6,2},{7,3},{8,12},{9,13},{10,... | collective-permute-start | bytes 38408 | tf_op jit(solution)/shard_map/ppermute | solution.py:346
  77.3 10.3 %collective-permute-start.12 = (f32[5,640]{1,0:T(8,128)S(1)}, f32[5,640]{1,0:T(8,128)S(1)}, u32[]{:S(2)}, u32[]{:S(2)}) collective-permute-start(f32[5,640]{1,0:T(8,128)S(1)} %add_select_fusion.refs_0_._), channel_id=1, source_target_pairs={{0,2},{1,3},{2,0},{3,1},{4,6},{5,7},{6,4},{7,5},{8,10},{9,11},{10,... | collective-permute-start | bytes 38408 | tf_op jit(solution)/shard_map/ppermute | solution.py:346
  77.8 6.0 %collective-permute-start.17 = (f32[1,1280]{1,0:T(1,128)S(1)}, f32[1,1280]{1,0:T(1,128)S(1)}, u32[]{:S(2)}, u32[]{:S(2)}) collective-permute-start(f32[1,1280]{1,0:T(1,128)S(1)} %get-tuple-element.48.refs_4_), channel_id=1, source_target_pairs={{0,24},{8,16},{16,8},{24,0},{1,25},{9,17},{17,9},{25,1},{2,26},{10... | collective-permute-start | bytes 15368 | tf_op jit(solution)/shard_map/ppermute | solution.py:349
  80.2 5.8 %collective-permute-start.16 = (f32[1,1280]{1,0:T(1,128)S(1)}, f32[1,1280]{1,0:T(1,128)S(1)}, u32[]{:S(2)}, u32[]{:S(2)}) collective-permute-start(f32[1,1280]{1,0:T(1,128)S(1)} %get-tuple-element.48.refs_4_), channel_id=1, source_target_pairs={{0,16},{8,24},{16,0},{24,8},{1,17},{9,25},{17,1},{25,9},{2,18},{10... | collective-permute-start | bytes 15368 | tf_op jit(solution)/shard_map/ppermute | solution.py:349
  99.2 22.0 %collective-permute-start.19 = (bf16[1280,256]{1,0:T(8,128)(2,1)S(1)}, bf16[1280,256]{1,0:T(8,128)(2,1)S(1)}, u32[]{:S(2)}, u32[]{:S(2)}) collective-permute-start(bf16[1280,256]{1,0:T(8,128)(2,1)S(1)} %get-tuple-element.49), channel_id=1, source_target_pairs={{0,8},{24,16},{1,9},{25,17},{2,10},{26,18},{3,11},{27,19},{4,12},{... | collective-permute-start | bytes 1966088 | tf_op jit(solution)/shard_map/ppermute | solution.py:384
  103.2 18.0 %collective-permute-start.18 = (bf16[1280,256]{1,0:T(8,128)(2,1)S(1)}, bf16[1280,256]{1,0:T(8,128)(2,1)S(1)}, u32[]{:S(2)}, u32[]{:S(2)}) collective-permute-start(bf16[1280,256]{1,0:T(8,128)(2,1)S(1)} %get-tuple-element.49), channel_id=1, source_target_pairs={{8,16},{16,8},{9,17},{17,9},{10,18},{18,10},{11,19},{19,11},{12,20... | collective-permute-start | bytes 1966088 | tf_op jit(solution)/shard_map/ppermute | solution.py:383
  104.0 17.1 %collective-permute-start.20 = (f32[1,128]{1,0:T(1,128)S(1)}, f32[1,128]{1,0:T(1,128)S(1)}, u32[]{:S(2)}, u32[]{:S(2)}) collective-permute-start(f32[1,128]{1,0:T(1,128)S(1)} %get-tuple-element.59), channel_id=1, source_target_pairs={{0,9},{1,8},{2,11},{3,10},{4,13},{5,12},{6,15},{7,14},{8,1},{9,0},... | collective-permute-start | bytes 1544 | tf_op jit(solution)/shard_map/ppermute | solution.py:353
  121.2 7.5 %collective-permute-start.21 = (bf16[2560,512]{1,0:T(8,128)(2,1)}, bf16[2560,512]{1,0:T(8,128)(2,1)S(1)}, u32[]{:S(2)}, u32[]{:S(2)}) collective-permute-start(bf16[2560,512]{1,0:T(8,128)(2,1)} %get-tuple-element.65), channel_id=1, source_target_pairs={{0,1},{1,0},{2,3},{3,2},{4,5},{5,4},{6,7},{7,6},{8,9},{9,8},{10,11... | collective-permute-start | bytes 7864328 | tf_op jit(solution)/shard_map/ppermute | solution.py:346
  123.4 5.3 %collective-permute-start.22 = (f32[1,128]{1,0:T(1,128)S(1)}, f32[1,128]{1,0:T(1,128)S(1)}, u32[]{:S(2)}, u32[]{:S(2)}) collective-permute-start(f32[1,128]{1,0:T(1,128)S(1)} %add.58), channel_id=1, source_target_pairs={{0,18},{1,19},{2,16},{3,17},{4,22},{5,23},{6,20},{7,21},{8,26},{9,... | collective-permute-start | bytes 1544 | tf_op jit(solution)/shard_map/ppermute | solution.py:353
  129.2 19.5 %collective-permute-start.27 = (bf16[1280,256]{1,0:T(8,128)(2,1)S(1)}, bf16[1280,256]{1,0:T(8,128)(2,1)S(1)}, u32[]{:S(2)}, u32[]{:S(2)}) collective-permute-start(bf16[1280,256]{1,0:T(8,128)(2,1)S(1)} %get-tuple-element.75), channel_id=1, source_target_pairs={{0,8},{8,16},{16,24},{24,0},{1,9},{9,17},{17,25},{25,1},{2,10},{10... | collective-permute-start | bytes 1966088 | tf_op jit(solution)/shard_map/ppermute | solution.py:402
  129.2 30.5 %collective-permute-start.28 = (bf16[1280,256]{1,0:T(8,128)(2,1)S(1)}, bf16[1280,256]{1,0:T(8,128)(2,1)S(1)}, u32[]{:S(2)}, u32[]{:S(2)}) collective-permute-start(bf16[1280,256]{1,0:T(8,128)(2,1)S(1)} %get-tuple-element.76), channel_id=1, source_target_pairs={{0,24},{8,0},{16,8},{24,16},{1,25},{9,1},{17,9},{25,17},{2,26},{10... | collective-permute-start | bytes 1966088 | tf_op jit(solution)/shard_map/ppermute | solution.py:403
  134.5 26.4 %collective-permute-start.24 = (bf16[2560,128]{1,0:T(8,128)(2,1)S(1)}, bf16[2560,128]{1,0:T(8,128)(2,1)S(1)}, u32[]{:S(2)}, u32[]{:S(2)}) collective-permute-start(bf16[2560,128]{1,0:T(8,128)(2,1)S(1)} %get-tuple-element.72), channel_id=1, source_target_pairs={{0,2},{1,3},{2,0},{3,1},{4,6},{5,7},{6,4},{7,5},{8,10},{9,11},{10,... | collective-permute-start | bytes 1966088 | tf_op jit(solution)/shard_map/ppermute | solution.py:346
  135.5 29.3 %collective-permute-start.25 = (bf16[2560,128]{1,0:T(8,128)(2,1)S(1)}, bf16[2560,128]{1,0:T(8,128)(2,1)S(1)}, u32[]{:S(2)}, u32[]{:S(2)}) collective-permute-start(bf16[2560,128]{1,0:T(8,128)(2,1)S(1)} %get-tuple-element.73), channel_id=1, source_target_pairs={{0,4},{1,5},{2,6},{3,7},{4,0},{5,1},{6,2},{7,3},{8,12},{9,13},{10,... | collective-permute-start | bytes 1966088 | tf_op jit(solution)/shard_map/ppermute | solution.py:346
  136.6 28.2 %collective-permute-start.26 = (bf16[2560,128]{1,0:T(8,128)(2,1)S(1)}, bf16[2560,128]{1,0:T(8,128)(2,1)S(1)}, u32[]{:S(2)}, u32[]{:S(2)}) collective-permute-start(bf16[2560,128]{1,0:T(8,128)(2,1)S(1)} %get-tuple-element.74), channel_id=1, source_target_pairs={{0,6},{1,7},{2,4},{3,5},{4,2},{5,3},{6,0},{7,1},{8,14},{9,15},{10,... | collective-permute-start | bytes 1966088 | tf_op jit(solution)/shard_map/ppermute | solution.py:346
  (10 other events, 68.1 us)

commit v5 on v4

--- a/solution.py
+++ b/solution.py
@@ -11,7 +11,6 @@
 log2e = math.log2(math.e)
 ln2 = math.log(2.0)
 strip = 32
-vmem_bytes = 48 * 1024 * 1024
 
 VMEM = pl.BlockSpec(memory_space=pltpu.VMEM)
 
@@ -20,12 +19,16 @@
     return pl.ds(pl.multiple_of(slot * width, width), width)
 
 
-def in_hbm(array):
-    return pltpu.with_memory_space_constraint(array, pltpu.HBM)
-
-
-def params():
-    return pltpu.CompilerParams(vmem_limit_bytes=vmem_bytes)
+def in_vmem(array):
+    return pltpu.with_memory_space_constraint(array, pltpu.VMEM)
+
+
+def block_of(step, size):
+    return pl.ds(pl.multiple_of(step * size, size), size)
+
+
+def params(mebibytes):
+    return pltpu.CompilerParams(vmem_limit_bytes=mebibytes * 1024 * 1024)
 
 
 def cost(microseconds):
@@ -39,6 +42,23 @@
 
 def lanes(x):
     return [x[:, k : k + 128] for k in range(0, x.shape[1], 128)]
+
+
+def merge_rows(row, other):
+    def kernel(row_ref, other_ref, out_ref):
+        row, other = row_ref[...], other_ref[...]
+        last = lax.broadcasted_iota(jnp.int32, row.shape, 0) == row.shape[0] - 1
+        out_ref[...] = jnp.where(last, row + other, log_add(row, other))
+
+    return pl.pallas_call(
+        kernel,
+        out_shape=jax.ShapeDtypeStruct(row.shape, jnp.float32),
+        in_specs=[VMEM, VMEM],
+        out_specs=VMEM,
+        compiler_params=params(4),
+        cost_estimate=cost(0.5),
+        name="merge_rows",
+    )(row, other)
 
 
 def side_by_side(image_pieces, text_pieces, width):
@@ -50,25 +70,23 @@
 
     def kernel(*refs):
         *sources, texts_ref, images_ref = refs
-        texts_ref[...] = jnp.zeros(texts_ref.shape, jnp.bfloat16)
+        step = pl.program_id(0)
+        texts_ref[block_of(step, bt), :] = jnp.zeros((bt, width), jnp.bfloat16)
         for k, (source, (_, slot)) in enumerate(zip(sources, pieces)):
-            target = texts_ref if k < len(text_pieces) else images_ref
-            target[:, columns(slot(), source.shape[1])] = source[...]
+            target, size = (texts_ref, bt) if k < len(text_pieces) else (images_ref, bm)
+            target[block_of(step, size), columns(slot(), source.shape[1])] = source[...]
 
     return pl.pallas_call(
         kernel,
         grid=(steps,),
-        out_shape=(
-            jax.ShapeDtypeStruct((rows, width), jnp.bfloat16),
-            pltpu.HBM((img_rows, width), jnp.bfloat16),
-        ),
+        out_shape=(pltpu.VMEM((rows, width), jnp.bfloat16), pltpu.VMEM((img_rows, width), jnp.bfloat16)),
         in_specs=[pl.BlockSpec((bt, piece.shape[1]), lambda i: (i, 0)) for piece, _ in text_pieces]
         + [pl.BlockSpec((bm, piece.shape[1]), lambda i: (i, 0)) for piece, _ in image_pieces],
-        out_specs=(pl.BlockSpec((bt, width), lambda i: (i, 0)), pl.BlockSpec((bm, width), lambda i: (i, 0))),
-        compiler_params=params(),
+        out_specs=(VMEM, VMEM),
+        compiler_params=params(12),
         cost_estimate=cost(0.01),
         name="side_by_side",
-    )(*[in_hbm(piece) for piece, _ in pieces])
+    )(*[piece for piece, _ in pieces])
 
 
 def logits_and_stats(images, texts, far, targets):
@@ -78,13 +96,10 @@
     pieces = rows // 256
     some = bm // pieces
 
-    def before(i):
-        return jnp.maximum(i - 1, 0)
-
     def kernel(images_ref, texts_ref, targets_ref, *refs):
         if far is not None:
             one_ref, other_ref, *refs = refs
-        u_ref, row_ref, col_ref, whole_ref, d_scr, rm_scr, rs_scr, cm_scr, cs_scr, target_scr, pos_scr = refs
+        u_ref, row_ref, col_ref, whole_ref, even_scr, odd_scr, rm_scr, rs_scr, cm_scr, cs_scr, target_scr, pos_scr = refs
         step = pl.program_id(0)
 
         @pl.when(step == 0)
@@ -96,22 +111,23 @@
             if far is not None:
                 whole_ref[:, columns(far[1](), one_ref.shape[1])] = jnp.where(far[2](), one_ref[...], other_ref[...])
 
-        def matmul(j):
+        def matmul(j, d_scr):
             at = slice(j * 256, (j + 1) * 256)
-            d_scr[step % 2, :, at] = lax.dot_general(
-                images_ref[...], whole_ref[at, :], (((1,), (1,)), ((), ())), preferred_element_type=jnp.float32
+            d_scr[:, at] = lax.dot_general(
+                images_ref[block_of(step, bm), :], whole_ref[at, :], (((1,), (1,)), ((), ())), preferred_element_type=jnp.float32
             )
 
-        def elementwise(j):
-            slot = (step + 1) % 2
+        def elementwise(j, d_scr):
+            base = (step - 1) * bm
             old = cm_scr[...]
             new = old
             ids = lax.broadcasted_iota(jnp.int32, (strip, 128), 1)
             picked = jnp.zeros((strip, 128), jnp.float32)
             for first in range(j * some, (j + 1) * some, strip):
                 at = slice(first, first + strip)
-                u = d_scr[slot, at, :] * (logit_scale * log2e)
-                u_ref[at, :] = u
+                here = pl.ds(pl.multiple_of(base + first, strip), strip)
+                u = d_scr[at, :] * (logit_scale * log2e)
+                u_ref[here, :] = u
                 target = target_scr[at, :] - ids
                 found = jnp.zeros((strip, 128), jnp.float32)
                 for k, v in enumerate(lanes(u)):
@@ -124,7 +140,7 @@
             total = cs_scr[...] * jnp.exp2(old - new)
             for first in range(j * some, (j + 1) * some, strip):
                 at = slice(first, first + strip)
-                u = u_ref[at, :]
+                u = u_ref[pl.ds(pl.multiple_of(base + first, strip), strip), :]
                 row_max = rm_scr[at, :]
                 rs_scr[at, :] = functools.reduce(jnp.add, [jnp.exp2(v - row_max) for v in lanes(u)])
                 total = total + jnp.sum(jnp.exp2(u.reshape(strip // 8, 8, rows) - new[None]), axis=0)
@@ -137,18 +153,24 @@
         @pl.when(step == 0)
         def _():
             for j in range(pieces):
-                matmul(j)
-
-        @pl.when(jnp.logical_and(step > 0, step < steps))
+                matmul(j, even_scr)
+
+        @pl.when(jnp.logical_and(step < steps, step % 2 == 1))
         def _():
             for j in range(pieces):
-                matmul(j)
-                elementwise(j)
+                matmul(j, odd_scr)
+                elementwise(j, even_scr)
+
+        @pl.when(jnp.logical_and(step > 0, jnp.logical_and(step < steps, step % 2 == 0)))
+        def _():
+            for j in range(pieces):
+                matmul(j, even_scr)
+                elementwise(j, odd_scr)
 
         @pl.when(step == steps)
         def _():
             for j in range(pieces):
-                elementwise(j)
+                elementwise(j, odd_scr if steps % 2 == 0 else even_scr)
 
         @pl.when(step > 0)
         def _():
@@ -168,16 +190,16 @@
         kernel,
         grid=(steps + 1,),
         out_shape=(
-            pltpu.HBM((img_rows, rows), jnp.float32),
+            pltpu.VMEM((img_rows, rows), jnp.float32),
             jax.ShapeDtypeStruct((steps + 1, bm), jnp.float32),
             jax.ShapeDtypeStruct((1, rows), jnp.float32),
-            pltpu.HBM((rows, width), jnp.bfloat16),
+            pltpu.VMEM((rows, width), jnp.bfloat16),
         ),
-        in_specs=[pl.BlockSpec((bm, width), lambda i: (jnp.minimum(i, steps - 1), 0)), VMEM, VMEM]
-        + ([] if far is None else [VMEM, VMEM]),
-        out_specs=(pl.BlockSpec((bm, rows), lambda i: (before(i), 0)), VMEM, VMEM, VMEM),
+        in_specs=[VMEM] * (3 if far is None else 5),
+        out_specs=(VMEM,) * 4,
         scratch_shapes=[
-            pltpu.VMEM((2, bm, rows), jnp.float32),
+            pltpu.VMEM((bm, rows), jnp.float32),
+            pltpu.VMEM((bm, rows), jnp.float32),
             pltpu.VMEM((bm, 128), jnp.float32),
             pltpu.VMEM((bm, 128), jnp.float32),
             pltpu.VMEM((8, rows), jnp.float32),
@@ -185,10 +207,10 @@
             pltpu.VMEM((bm, 128), jnp.int32),
             pltpu.VMEM((strip, 128), jnp.float32),
         ],
-        compiler_params=params(),
+        compiler_params=params(12),
         cost_estimate=cost(13),
         name="logits_and_stats",
-    )(in_hbm(images), texts, targets, *(() if far is None else far[0]))
+    )(in_vmem(images), in_vmem(texts), targets, *(() if far is None else far[0]))
 
 
 def weights_and_far(u, images, targets, row_lses, col_lses, slot, wide, cuts):
@@ -196,10 +218,13 @@
     rows = u.shape[1]
     steps, bm = targets.shape
     n_row, n_col = len(row_lses), len(col_lses)
+    groups = [(first, min(first + 256, bm)) for first in range(0, bm, 256)]
 
     def kernel(u_ref, images_ref, targets_ref, *refs):
         row_refs, col_refs, refs = refs[:n_row], refs[n_row : n_row + n_col], refs[n_row + n_col :]
-        w_ref, loss_ref, *far_refs, acc, row_ref, col_ref, row_scr, target_scr = refs
+        w_ref, loss_ref, *refs = refs
+        far_refs, refs = refs[: len(cuts) - 1], refs[len(cuts) - 1 :]
+        group_scrs, (acc, row_ref, col_ref, row_scr, target_scr) = refs[: len(groups)], refs[len(groups) :]
         step = pl.program_id(0)
 
         @pl.when(step == 0)
@@ -217,19 +242,22 @@
         target_scr[...] = jnp.broadcast_to(targets_ref[pl.ds(step, 1), :], (128, bm)).T
         ids = lax.broadcasted_iota(jnp.int32, (strip, 128), 1)
         col = col_ref[...]
-        for group in range(0, bm, 256):
-            end = min(group + 256, bm)
+        for (group, end), w_scr in zip(groups, group_scrs):
+            rows_here = pl.ds(pl.multiple_of(step * bm + group, 128), end - group)
             for first in range(group, end, strip):
                 at = slice(first, first + strip)
+                here = pl.ds(pl.multiple_of(step * bm + first, strip), strip)
                 row = row_scr[at, :]
                 target = target_scr[at, :] - ids
                 for k in range(0, rows, 128):
-                    v = u_ref[at, k : k + 128]
+                    v = u_ref[here, k : k + 128]
                     weight = jnp.exp2(v - row) + jnp.exp2(v - col[:, k : k + 128]) - jnp.where(target == k, 2.0, 0.0)
-                    w_ref[at, k : k + 128] = weight.astype(jnp.bfloat16)
+                    weight = weight.astype(jnp.bfloat16)
+                    w_ref[here, k : k + 128] = weight
+                    w_scr[first - group : first - group + strip, k : k + 128] = weight
             acc[...] += lax.dot_general(
-                w_ref[group:end, :],
-                images_ref[group:end, :],
+                w_scr[...],
+                images_ref[rows_here, columns(slot(), wide)],
                 (((0,), (0,)), ((), ())),
                 preferred_element_type=jnp.float32,
             )
@@ -243,27 +271,24 @@
         kernel,
         grid=(steps,),
         out_shape=(
-            pltpu.HBM((img_rows, rows), jnp.bfloat16),
+            pltpu.VMEM((img_rows, rows), jnp.bfloat16),
             jax.ShapeDtypeStruct((1, 128), jnp.float32),
         )
         + tuple(jax.ShapeDtypeStruct((end - first, wide), jnp.bfloat16) for first, end in zip(cuts, cuts[1:])),
-        in_specs=[
-            pl.BlockSpec((bm, rows), lambda i: (i, 0)),
-            pl.BlockSpec((bm, wide), lambda i: (i, slot())),
-        ]
-        + [VMEM] * (1 + n_row + n_col),
-        out_specs=(pl.BlockSpec((bm, rows), lambda i: (i, 0)), VMEM) + (VMEM,) * (len(cuts) - 1),
-        scratch_shapes=[
+        in_specs=[VMEM] * (3 + n_row + n_col),
+        out_specs=(VMEM,) * (len(cuts) + 1),
+        scratch_shapes=[pltpu.VMEM((end - first, rows), jnp.bfloat16) for first, end in groups]
+        + [
             pltpu.VMEM((rows, wide), jnp.float32),
             pltpu.VMEM((steps, bm), jnp.float32),
             pltpu.VMEM((1, rows), jnp.float32),
             pltpu.VMEM((bm, 128), jnp.float32),
             pltpu.VMEM((bm, 128), jnp.int32),
         ],
-        compiler_params=params(),
+        compiler_params=params(8),
         cost_estimate=cost(8),
         name="weights_and_far",
-    )(in_hbm(u), in_hbm(images), targets, *row_lses, *col_lses)
+    )(in_vmem(u), in_vmem(images), targets, *row_lses, *col_lses)
 
 
 def gradients(weights, images, texts, slots, text_wide, groups, order, microseconds=10):
@@ -277,8 +302,11 @@
     def kernel(w_ref, _, *refs):
         if groups:
             texts_ref, *refs = refs
-        image_refs, text_outs, (*image_outs, acc, image_acc) = refs[:n_text], refs[n_text : 2 * n_text], refs[2 * n_text :]
+        if slots:
+            images_ref, *refs = refs
+        text_outs, (*image_outs, acc, image_acc) = refs[:n_text], refs[n_text:]
         step = pl.program_id(0)
+        here = block_of(step, bm)
 
         if slots:
 
@@ -286,12 +314,17 @@
             def _():
                 acc[...] = jnp.zeros(acc.shape, jnp.float32)
 
-        for k, image_ref in enumerate(image_refs):
+        for k, slot in enumerate(slots):
             acc[k] += lax.dot_general(
-                w_ref[...], image_ref[...], (((0,), (0,)), ((), ())), preferred_element_type=jnp.float32
+                w_ref[here, :],
+                images_ref[here, columns(slot(), text_wide)],
+                (((0,), (0,)), ((), ())),
+                preferred_element_type=jnp.float32,
             )
         if groups:
-            image_acc[...] = logit_scale * jnp.dot(w_ref[...], texts_ref[...], preferred_element_type=jnp.float32)
+            image_acc[...] = logit_scale * jnp.dot(
+                w_ref[here, :], texts_ref[...], preferred_element_type=jnp.float32
+            )
         for out, group in zip(image_outs, groups):
             for k, slot in enumerate(group):
                 out[:, k * wide : (k + 1) * wide] = image_acc[:, columns(slot(), wide)].astype(jnp.bfloat16)
@@ -300,25 +333,22 @@
         def _():
             for k, out in enumerate(text_outs):
                 out[...] = (logit_scale * acc[k]).astype(jnp.bfloat16)
-
-    def image_spec(slot):
-        return pl.BlockSpec((bm, text_wide), lambda i: (i, slot()))
 
     return pl.pallas_call(
         kernel,
         grid=(steps,),
         out_shape=(jax.ShapeDtypeStruct((rows, text_wide), jnp.bfloat16),) * n_text
         + tuple(jax.ShapeDtypeStruct((img_rows, wide * len(group)), jnp.bfloat16) for group in groups),
-        in_specs=[pl.BlockSpec((bm, rows), lambda i: (i, 0)), VMEM] + [VMEM] * bool(groups) + [image_spec(slot) for slot in slots],
+        in_specs=[VMEM] * (2 + bool(groups) + bool(slots)),
         out_specs=(VMEM,) * n_text + tuple(pl.BlockSpec((bm, wide * len(g)), lambda i: (i, 0)) for g in groups),
         scratch_shapes=[
             pltpu.VMEM((max(1, n_text), rows, text_wide), jnp.float32),
             pltpu.VMEM((bm, width), jnp.float32),
         ],
-        compiler_params=params(),
+        compiler_params=params(14),
         cost_estimate=cost(microseconds),
         name="gradients",
-    )(in_hbm(weights), order, *([texts] if groups else []), *[in_hbm(images)] * n_text)
+    )(in_vmem(weights), order, *([in_vmem(texts)] if groups else []), *([in_vmem(images)] if slots else []))
 
 
 def together(*values):
@@ -373,9 +403,7 @@
     far = ((from_middle, from_inner), img_slot(2), lambda: lax.rem(lax.axis_index("img"), 3) > 0)
     u, row, col, whole_txt = logits_and_stats(whole_img, most_txt, far, targets)
 
-    other = swap(row, 1)
-    last = lax.broadcasted_iota(jnp.int32, row.shape, 0) == 4
-    row = jnp.where(last, row + other, log_add(row, other))
+    row = merge_rows(row, swap(row, 1))
     rows = [row] + [swap(row, by) for by in (2, 4, 6)]
     cols = [col] + [over_z(col, by) for by in (1, 2, 3)]
 

time: 167 us -> 162 us (0.970)
  Pallas kernels: 58 us -> 48.1 us
  waiting for transfers between devices: 59.8 us -> 64.6 us
    pallas_call x2, Pallas kernels: 22.5 us -> 16.8 us  [gradients(): pl.pallas_call(kernel, grid=(steps,), out_shape=(jax.ShapeDtypeStruct((ro...]
    pallas_call x3 -> x4, Pallas kernels: 35.5 us -> 31.2 us  [the longest x1 17.8 us: logits_and_stats(): pl.pallas_call(kernel, grid=(steps + 1,), out_shape=(pltpu.VMEM((img_rows...]
    ppermute x1, waiting for transfers between devices: 9.22 us -> 12 us  [per_device_4x8(): lax.ppermute(jnp.where(is_first, from_next, from_prev), 'img', [(1, 0), (...]
    ppermute x1, waiting for transfers between devices: 3.42 us -> 5.71 us  [per_device_4x8(): from_prev = lax.ppermute(to_next, 'img', shifted(4, 1))]
  transfers between devices with their start and end apart: 29 -> 29, of which waited for: 11 -> 11; matrix products, arithmetic and copies ran while one was open for 2% -> 2% of each run, Pallas kernels for 17% -> 13%
where the time goes in v5:
time: 162 us
  waiting for transfers between devices  64.6 us (40%)
  Pallas kernels  48.1 us (30%)
  starting transfers between devices  41.8 us (26%)
  other arithmetic  4.07 us (3%)
  between operations  2.65 us (2%)
    ppermute x16, waiting for transfers between devices, swap(): return lax.ppermute(part, 'txt', paired(8, by))  18.9 us
    pallas_call x1, Pallas kernels, logits_and_stats(): pl.pallas_call(kernel, grid=(steps + 1,), out_shape=(pltpu.VMEM((img_rows...  17.8 us
    pallas_call x2, Pallas kernels, gradients(): pl.pallas_call(kernel, grid=(steps,), out_shape=(jax.ShapeDtypeStruct((ro...  16.8 us
    ppermute x16, starting transfers between devices, swap(): return lax.ppermute(part, 'txt', paired(8, by))  15.2 us
    ppermute x1, waiting for transfers between devices, per_device_4x8(): from_prev = lax.ppermute(texts, 'img', shifted(4, 1))  12.2 us
    ppermute x1, waiting for transfers between devices, per_device_4x8(): lax.ppermute(jnp.where(is_first, from_next, from_prev), 'img', [(1, 0), (...  12 us
    ppermute x1, waiting for transfers between devices, per_device_4x8(): from_next = lax.ppermute(to_prev, 'img', shifted(4, -1))  10.9 us
    pallas_call x1, Pallas kernels, weights_and_far(): pl.pallas_call(kernel, grid=(steps,), out_shape=(pltpu.VMEM((img_rows, ro...  9.33 us
  transfers between devices with their start and end apart: 29, of which 11 were waited for; matrix products, arithmetic and copies ran while one was open for 2% of the time, Pallas kernels for 13%

profile of v5, /device:TPU:0, one launch (start us, length us, event | category | flops | bytes accessed | tf_op | source)
XLA Modules:
  0.0 161.8 jit_solution(17080546182822230237)
XLA Ops:
  0.6 3.1 %collective-permute-start = (bf16[1280,256]{1,0:T(8,128)(2,1)}, bf16[1280,256]{1,0:T(8,128)(2,1)S(1)}, u32[]{:S(2)}, u32[]{:S(2)}) collective-permute-start(bf16[1280,256]{1,0:T(8,128)(2,1)} %refs_0_.1), channel_id=1, source_target_pairs={{0,8},{8,16},{16,24},{24,0},{1,9},{9,17},{17,25},{25,1},{2,10},{10... | collective-permute-start | bytes 1966088 | tf_op jit(solution)/shard_map/ppermute | solution.py:392
  3.7 2.4 %collective-permute-start.6 = (bf16[2560,128]{1,0:T(8,128)(2,1)}, bf16[2560,128]{1,0:T(8,128)(2,1)S(1)}, u32[]{:S(2)}, u32[]{:S(2)}) collective-permute-start(bf16[2560,128]{1,0:T(8,128)(2,1)} %refs_3_.1), channel_id=1, source_target_pairs={{0,6},{1,7},{2,4},{3,5},{4,2},{5,3},{6,0},{7,1},{8,14},{9,15},{10,... | collective-permute-start | bytes 1966088 | tf_op jit(solution)/shard_map/ppermute | solution.py:376
  7.2 2.1 %collective-permute-start.1 = (bf16[1280,256]{1,0:T(8,128)(2,1)}, bf16[1280,256]{1,0:T(8,128)(2,1)S(1)}, u32[]{:S(2)}, u32[]{:S(2)}) collective-permute-start(bf16[1280,256]{1,0:T(8,128)(2,1)} %refs_0_.1), channel_id=1, source_target_pairs={{0,24},{8,0},{16,8},{24,16},{1,25},{9,1},{17,9},{25,17},{2,26},{10... | collective-permute-start | bytes 1966088 | tf_op jit(solution)/shard_map/ppermute | solution.py:393
  9.3 12.2 %collective-permute-done.refs_1_ = bf16[1280,256]{1,0:T(8,128)(2,1)S(1)} collective-permute-done((bf16[1280,256]{1,0:T(8,128)(2,1)}, bf16[1280,256]{1,0:T(8,128)(2,1)S(1)}, u32[]{:S(2)}, u32[]{:S(2)}) %collective-permute-start) | collective-permute-done | bytes 655392 | tf_op jit(solution)/shard_map/ppermute | solution.py:392
  22.5 12.6 %collective-permute-done.5.refs_5_ = bf16[2560,128]{1,0:T(8,128)(2,1)} collective-permute-done((bf16[2560,128]{1,0:T(8,128)(2,1)}, bf16[2560,128]{1,0:T(8,128)(2,1)}, u32[]{:S(2)}, u32[]{:S(2)}) %collective-permute-start.5) | collective-permute-done | bytes 655392 | tf_op jit(solution)/shard_map/ppermute | solution.py:376
  39.7 4.1 %side_by_side.1 = (bf16[1280,1024]{1,0:T(8,128)(2,1)S(1)}, bf16[2560,1024]{1,0:T(8,128)(2,1)S(1)}) custom-call(bf16[1280,256]{1,0:T(8,128)(2,1)S(1)} %copy-done, bf16[1280,256]{1,0:T(8,128)(2,1)S(1)} %collective-permute-done.refs_1_, bf16[1280,256]{1,0:T(8,128)(2,1)S(1)} %collective-permute-done.1.refs_2_, bf16[2560,128]{1,0:T(8,128)(2,1)S(1)} %copy-done.1, ...), custom_call_target="tpu_custom_call" | custom-call | flops 11000000 | bytes 1 | tf_op jit(solution)/shard_map/side_by_side/pallas_call | solution.py:79
  43.8 12.0 %collective-permute-done.3.refs_1_ = bf16[1280,256]{1,0:T(8,128)(2,1)} collective-permute-done((bf16[1280,256]{1,0:T(8,128)(2,1)}, bf16[1280,256]{1,0:T(8,128)(2,1)}, u32[]{:S(2)}, u32[]{:S(2)}) %collective-permute-start.3) | collective-permute-done | bytes 655392 | tf_op jit(solution)/shard_map/ppermute | solution.py:397
  55.8 17.8 %logits_and_stats.1 = (f32[2560,1280]{1,0:T(8,128)S(1)}, f32[5,640]{1,0:T(8,128)S(1)}, f32[1,1280]{1,0:T(1,128)S(1)}, bf16[1280,1024]{1,0:T(8,128)(2,1)S(1)}) custom-call(bf16[2560,1024]{1,0:T(8,128)(2,1)S(1)} %get-tuple-element.42.images_ref.refs_1_.refs_0_, bf16[1280,1024]{1,0:T(8,128)(2,1)S(1)} %get-tuple-element.43.texts_ref, ...), custom_call_target="tpu_custom_call" | custom-call | flops 14300000256 | bytes 1 | tf_op jit(solution)/shard_map/logits_and_stats/pallas_call | solution.py:189
  74.8 1.7 %collective-permute-start.14 = (f32[5,640]{1,0:T(8,128)S(1)}, f32[5,640]{1,0:T(8,128)S(1)}, u32[]{:S(2)}, u32[]{:S(2)}) collective-permute-start(f32[5,640]{1,0:T(8,128)S(1)} %merge_rows.1.refs_0_._), channel_id=1, source_target_pairs={{0,6},{1,7},{2,4},{3,5},{4,2},{5,3},{6,0},{7,1},{8,14},{9,15},{10,... | collective-permute-start | bytes 38408 | tf_op jit(solution)/shard_map/ppermute | solution.py:376
  78.4 2.4 %collective-permute-start.17 = (f32[1,1280]{1,0:T(1,128)S(1)}, f32[1,1280]{1,0:T(1,128)S(1)}, u32[]{:S(2)}, u32[]{:S(2)}) collective-permute-start(f32[1,1280]{1,0:T(1,128)S(1)} %get-tuple-element.48.refs_4_), channel_id=1, source_target_pairs={{0,24},{8,16},{16,8},{24,0},{1,25},{9,17},{17,9},{25,1},{2,26},{10... | collective-permute-start | bytes 15368 | tf_op jit(solution)/shard_map/ppermute | solution.py:379
  80.8 3.6 %collective-permute-start.16 = (f32[1,1280]{1,0:T(1,128)S(1)}, f32[1,1280]{1,0:T(1,128)S(1)}, u32[]{:S(2)}, u32[]{:S(2)}) collective-permute-start(f32[1,1280]{1,0:T(1,128)S(1)} %get-tuple-element.48.refs_4_), channel_id=1, source_target_pairs={{0,16},{8,24},{16,0},{24,8},{1,17},{9,25},{17,1},{25,9},{2,18},{10... | collective-permute-start | bytes 15368 | tf_op jit(solution)/shard_map/ppermute | solution.py:379
  84.4 2.2 %collective-permute-start.15 = (f32[1,1280]{1,0:T(1,128)S(1)}, f32[1,1280]{1,0:T(1,128)S(1)}, u32[]{:S(2)}, u32[]{:S(2)}) collective-permute-start(f32[1,1280]{1,0:T(1,128)S(1)} %get-tuple-element.48.refs_4_), channel_id=1, source_target_pairs={{0,8},{8,0},{16,24},{24,16},{1,9},{9,1},{17,25},{25,17},{2,10},{10... | collective-permute-start | bytes 15368 | tf_op jit(solution)/shard_map/ppermute | solution.py:379
  88.1 9.3 %weights_and_far.1 = (bf16[2560,1280]{1,0:T(8,128)(2,1)S(1)}, f32[1,128]{1,0:T(1,128)S(1)}, bf16[1280,256]{1,0:T(8,128)(2,1)S(1)}) custom-call(f32[2560,1280]{1,0:T(8,128)S(1)} %get-tuple-element.46.u_ref, bf16[2560,1024]{1,0:T(8,128)(2,1)S(1)} %get-tuple-element.42.images_ref.refs_1_.refs_0_, s32[4,640]{1,0:T(4,128)S(1)} %reshape.12.targets_ref, ...), custom_call_target="tpu_custom_call" | custom-call | flops 8800000000 | bytes 1 | tf_op jit(solution)/shard_map/weights_and_far/pallas_call | solution.py:270
  97.5 3.9 %collective-permute-start.19 = (bf16[1280,256]{1,0:T(8,128)(2,1)S(1)}, bf16[1280,256]{1,0:T(8,128)(2,1)S(1)}, u32[]{:S(2)}, u32[]{:S(2)}) collective-permute-start(bf16[1280,256]{1,0:T(8,128)(2,1)S(1)} %get-tuple-element.49), channel_id=1, source_target_pairs={{0,8},{24,16},{1,9},{25,17},{2,10},{26,18},{3,11},{27,19},{4,12},{... | collective-permute-start | bytes 1966088 | tf_op jit(solution)/shard_map/ppermute | solution.py:412
  102.2 13.7 %gradients.2 = (bf16[1280,256]{1,0:T(8,128)(2,1)S(1)}, bf16[1280,256]{1,0:T(8,128)(2,1)S(1)}, bf16[2560,128]{1,0:T(8,128)(2,1)S(1)}, bf16[2560,128]{1,0:T(8,128)...) custom-call(bf16[2560,1280]{1,0:T(8,128)(2,1)S(1)} %get-tuple-element.50.w_re, ...), custom_call_target="tpu_custom_call" | custom-call | flops 11000000512 | bytes 1 | tf_op jit(solution)/shard_map/gradients/pallas_call | solution.py:337
  116.0 2.2 %collective-permute-start.21 = (bf16[2560,512]{1,0:T(8,128)(2,1)S(1)}, bf16[2560,512]{1,0:T(8,128)(2,1)S(1)}, u32[]{:S(2)}, u32[]{:S(2)}) collective-permute-start(bf16[2560,512]{1,0:T(8,128)(2,1)S(1)} %get-tuple-element.65), channel_id=1, source_target_pairs={{0,1},{1,0},{2,3},{3,2},{4,5},{5,4},{6,7},{7,6},{8,9},{9,8},{10,11... | collective-permute-start | bytes 7864328 | tf_op jit(solution)/shard_map/ppermute | solution.py:376
  118.2 1.9 %collective-permute-start.22 = (f32[1,128]{1,0:T(1,128)S(1)}, f32[1,128]{1,0:T(1,128)S(1)}, u32[]{:S(2)}, u32[]{:S(2)}) collective-permute-start(f32[1,128]{1,0:T(1,128)S(1)} %add.46), channel_id=1, source_target_pairs={{0,18},{1,19},{2,16},{3,17},{4,22},{5,23},{6,20},{7,21},{8,26},{9,... | collective-permute-start | bytes 1544 | tf_op jit(solution)/shard_map/ppermute | solution.py:383
  120.2 3.3 %collective-permute-done.22 = f32[1,128]{1,0:T(1,128)S(1)} collective-permute-done((f32[1,128]{1,0:T(1,128)S(1)}, f32[1,128]{1,0:T(1,128)S(1)}, u32[]{:S(2)}, u32[]{:S(2)}) %collective-permute-start.22) | collective-permute-done | bytes 544 | tf_op jit(solution)/shard_map/ppermute | solution.py:383
  124.0 3.8 %collective-permute-start.28 = (bf16[1280,256]{1,0:T(8,128)(2,1)S(1)}, bf16[1280,256]{1,0:T(8,128)(2,1)S(1)}, u32[]{:S(2)}, u32[]{:S(2)}) collective-permute-start(bf16[1280,256]{1,0:T(8,128)(2,1)S(1)} %get-tuple-element.76), channel_id=1, source_target_pairs={{0,24},{8,0},{16,8},{24,16},{1,25},{9,1},{17,9},{25,17},{2,26},{10... | collective-permute-start | bytes 1966088 | tf_op jit(solution)/shard_map/ppermute | solution.py:431
  131.3 2.0 %collective-permute-start.26 = (bf16[2560,128]{1,0:T(8,128)(2,1)S(1)}, bf16[2560,128]{1,0:T(8,128)(2,1)S(1)}, u32[]{:S(2)}, u32[]{:S(2)}) collective-permute-start(bf16[2560,128]{1,0:T(8,128)(2,1)S(1)} %get-tuple-element.74), channel_id=1, source_target_pairs={{0,6},{1,7},{2,4},{3,5},{4,2},{5,3},{6,0},{7,1},{8,14},{9,15},{10,... | collective-permute-start | bytes 1966088 | tf_op jit(solution)/shard_map/ppermute | solution.py:376
  133.3 3.1 %gradients.3 = bf16[1280,256]{1,0:T(8,128)(2,1)S(1)} custom-call(bf16[2560,1280]{1,0:T(8,128)(2,1)S(1)} %get-tuple-element.50.w_ref, f32[1,128]{1,0:T(1,128)S(1)} %add.53._, bf16[2560,1024]{1,0:T(8,128)(2,1)S(1)} %get-tuple-element.42.images_ref.refs_1_.refs_0_), custom_call_target="tpu_custom_call" | custom-call | flops 11000000 | bytes 1 | tf_op jit(solution)/shard_map/gradients/pallas_call | solution.py:337
  137.7 5.7 %collective-permute-done.27 = bf16[1280,256]{1,0:T(8,128)(2,1)S(1)} collective-permute-done((bf16[1280,256]{1,0:T(8,128)(2,1)S(1)}, bf16[1280,256]{1,0:T(8,128)(2,1)S(1)}, u32[]{:S(2)}, u32[]{:S(2)}) %collective-permute-start.27) | collective-permute-done | bytes 655392 | tf_op jit(solution)/shard_map/ppermute | solution.py:430
  143.4 10.9 %collective-permute-done.28 = bf16[1280,256]{1,0:T(8,128)(2,1)S(1)} collective-permute-done((bf16[1280,256]{1,0:T(8,128)(2,1)S(1)}, bf16[1280,256]{1,0:T(8,128)(2,1)S(1)}, u32[]{:S(2)}, u32[]{:S(2)}) %collective-permute-start.28) | collective-permute-done | bytes 655392 | tf_op jit(solution)/shard_map/ppermute | solution.py:431
  155.4 4.0 %collective-permute-done.25 = bf16[2560,128]{1,0:T(8,128)(2,1)S(1)} collective-permute-done((bf16[2560,128]{1,0:T(8,128)(2,1)S(1)}, bf16[2560,128]{1,0:T(8,128)(2,1)S(1)}, u32[]{:S(2)}, u32[]{:S(2)}) %collective-permute-start.25) | collective-permute-done | bytes 655392 | tf_op jit(solution)/shard_map/ppermute | solution.py:376
  (57 shorter events, 19.1 us)
Async XLA Ops:
  0.6 20.9 %collective-permute-start = (bf16[1280,256]{1,0:T(8,128)(2,1)}, bf16[1280,256]{1,0:T(8,128)(2,1)S(1)}, u32[]{:S(2)}, u32[]{:S(2)}) collective-permute-start(bf16[1280,256]{1,0:T(8,128)(2,1)} %refs_0_.1), channel_id=1, source_target_pairs={{0,8},{8,16},{16,24},{24,0},{1,9},{9,17},{17,25},{25,1},{2,10},{10... | collective-permute-start | bytes 1966088 | tf_op jit(solution)/shard_map/ppermute | solution.py:392
  3.7 18.8 %collective-permute-start.6 = (bf16[2560,128]{1,0:T(8,128)(2,1)}, bf16[2560,128]{1,0:T(8,128)(2,1)S(1)}, u32[]{:S(2)}, u32[]{:S(2)}) collective-permute-start(bf16[2560,128]{1,0:T(8,128)(2,1)} %refs_3_.1), channel_id=1, source_target_pairs={{0,6},{1,7},{2,4},{3,5},{4,2},{5,3},{6,0},{7,1},{8,14},{9,15},{10,... | collective-permute-start | bytes 1966088 | tf_op jit(solution)/shard_map/ppermute | solution.py:376
  6.2 29.0 %collective-permute-start.5 = (bf16[2560,128]{1,0:T(8,128)(2,1)}, bf16[2560,128]{1,0:T(8,128)(2,1)}, u32[]{:S(2)}, u32[]{:S(2)}) collective-permute-start(bf16[2560,128]{1,0:T(8,128)(2,1)} %refs_3_.1), channel_id=1, source_target_pairs={{0,4},{1,5},{2,6},{3,7},{4,0},{5,1},{6,2},{7,3},{8,12},{9,13},{10,... | collective-permute-start | bytes 1966088 | tf_op jit(solution)/shard_map/ppermute | solution.py:376
  6.7 28.6 %collective-permute-start.4 = (bf16[2560,128]{1,0:T(8,128)(2,1)}, bf16[2560,128]{1,0:T(8,128)(2,1)}, u32[]{:S(2)}, u32[]{:S(2)}) collective-permute-start(bf16[2560,128]{1,0:T(8,128)(2,1)} %refs_3_.1), channel_id=1, source_target_pairs={{0,2},{1,3},{2,0},{3,1},{4,6},{5,7},{6,4},{7,5},{8,10},{9,11},{10,... | collective-permute-start | bytes 1966088 | tf_op jit(solution)/shard_map/ppermute | solution.py:376
  7.2 28.5 %collective-permute-start.1 = (bf16[1280,256]{1,0:T(8,128)(2,1)}, bf16[1280,256]{1,0:T(8,128)(2,1)S(1)}, u32[]{:S(2)}, u32[]{:S(2)}) collective-permute-start(bf16[1280,256]{1,0:T(8,128)(2,1)} %refs_0_.1), channel_id=1, source_target_pairs={{0,24},{8,0},{16,8},{24,16},{1,25},{9,1},{17,9},{25,17},{2,26},{10... | collective-permute-start | bytes 1966088 | tf_op jit(solution)/shard_map/ppermute | solution.py:393
  21.5 16.6 %collective-permute-start.7 = (bf16[2560,128]{1,0:T(8,128)(2,1)}, bf16[2560,128]{1,0:T(8,128)(2,1)}, u32[]{:S(2)}, u32[]{:S(2)}) collective-permute-start(bf16[2560,128]{1,0:T(8,128)(2,1)} %refs_3_.1), channel_id=1, source_target_pairs={{0,1},{1,0},{2,3},{3,2},{4,5},{5,4},{6,7},{7,6},{8,9},{9,8},{10,11... | collective-permute-start | bytes 1966088 | tf_op jit(solution)/shard_map/ppermute | solution.py:376
  22.5 17.2 %collective-permute-start.10 = (bf16[2560,128]{1,0:T(8,128)(2,1)S(1)}, bf16[2560,128]{1,0:T(8,128)(2,1)}, u32[]{:S(2)}, u32[]{:S(2)}) collective-permute-start(bf16[2560,128]{1,0:T(8,128)(2,1)S(1)} %collective-permute-done.6.refs_6_), channel_id=1, source_target_pairs={{0,1},{1,0},{2,3},{3,2},{4,5},{5,4},{6,7},{7,6},{8,9},{9,8},{10,11... | collective-permute-start | bytes 1966088 | tf_op jit(solution)/shard_map/ppermute | solution.py:376
  36.8 18.9 %collective-permute-start.3 = (bf16[1280,256]{1,0:T(8,128)(2,1)}, bf16[1280,256]{1,0:T(8,128)(2,1)}, u32[]{:S(2)}, u32[]{:S(2)}) collective-permute-start(bf16[1280,256]{1,0:T(8,128)(2,1)} %get-tuple-element.83), channel_id=1, source_target_pairs={{8,0},{16,24},{9,1},{17,25},{10,2},{18,26},{11,3},{19,27},{12,4},{... | collective-permute-start | bytes 1966088 | tf_op jit(solution)/shard_map/ppermute | solution.py:397
  38.1 17.6 %collective-permute-start.2 = (bf16[1280,256]{1,0:T(8,128)(2,1)}, bf16[1280,256]{1,0:T(8,128)(2,1)}, u32[]{:S(2)}, u32[]{:S(2)}) collective-permute-start(bf16[1280,256]{1,0:T(8,128)(2,1)} %get-tuple-element.84), channel_id=1, source_target_pairs={{8,16},{16,8},{9,17},{17,9},{10,18},{18,10},{11,19},{19,11},{12,20... | collective-permute-start | bytes 1966088 | tf_op jit(solution)/shard_map/ppermute | solution.py:396
  74.8 13.3 %collective-permute-start.14 = (f32[5,640]{1,0:T(8,128)S(1)}, f32[5,640]{1,0:T(8,128)S(1)}, u32[]{:S(2)}, u32[]{:S(2)}) collective-permute-start(f32[5,640]{1,0:T(8,128)S(1)} %merge_rows.1.refs_0_._), channel_id=1, source_target_pairs={{0,6},{1,7},{2,4},{3,5},{4,2},{5,3},{6,0},{7,1},{8,14},{9,15},{10,... | collective-permute-start | bytes 38408 | tf_op jit(solution)/shard_map/ppermute | solution.py:376
  76.6 11.6 %collective-permute-start.13 = (f32[5,640]{1,0:T(8,128)S(1)}, f32[5,640]{1,0:T(8,128)S(1)}, u32[]{:S(2)}, u32[]{:S(2)}) collective-permute-start(f32[5,640]{1,0:T(8,128)S(1)} %merge_rows.1.refs_0_._), channel_id=1, source_target_pairs={{0,4},{1,5},{2,6},{3,7},{4,0},{5,1},{6,2},{7,3},{8,12},{9,13},{10,... | collective-permute-start | bytes 38408 | tf_op jit(solution)/shard_map/ppermute | solution.py:376
  77.9 10.3 %collective-permute-start.12 = (f32[5,640]{1,0:T(8,128)S(1)}, f32[5,640]{1,0:T(8,128)S(1)}, u32[]{:S(2)}, u32[]{:S(2)}) collective-permute-start(f32[5,640]{1,0:T(8,128)S(1)} %merge_rows.1.refs_0_._), channel_id=1, source_target_pairs={{0,2},{1,3},{2,0},{3,1},{4,6},{5,7},{6,4},{7,5},{8,10},{9,11},{10,... | collective-permute-start | bytes 38408 | tf_op jit(solution)/shard_map/ppermute | solution.py:376
  78.4 6.0 %collective-permute-start.17 = (f32[1,1280]{1,0:T(1,128)S(1)}, f32[1,1280]{1,0:T(1,128)S(1)}, u32[]{:S(2)}, u32[]{:S(2)}) collective-permute-start(f32[1,1280]{1,0:T(1,128)S(1)} %get-tuple-element.48.refs_4_), channel_id=1, source_target_pairs={{0,24},{8,16},{16,8},{24,0},{1,25},{9,17},{17,9},{25,1},{2,26},{10... | collective-permute-start | bytes 15368 | tf_op jit(solution)/shard_map/ppermute | solution.py:379
  80.8 5.8 %collective-permute-start.16 = (f32[1,1280]{1,0:T(1,128)S(1)}, f32[1,1280]{1,0:T(1,128)S(1)}, u32[]{:S(2)}, u32[]{:S(2)}) collective-permute-start(f32[1,1280]{1,0:T(1,128)S(1)} %get-tuple-element.48.refs_4_), channel_id=1, source_target_pairs={{0,16},{8,24},{16,0},{24,8},{1,17},{9,25},{17,1},{25,9},{2,18},{10... | collective-permute-start | bytes 15368 | tf_op jit(solution)/shard_map/ppermute | solution.py:379
  97.5 18.5 %collective-permute-start.19 = (bf16[1280,256]{1,0:T(8,128)(2,1)S(1)}, bf16[1280,256]{1,0:T(8,128)(2,1)S(1)}, u32[]{:S(2)}, u32[]{:S(2)}) collective-permute-start(bf16[1280,256]{1,0:T(8,128)(2,1)S(1)} %get-tuple-element.49), channel_id=1, source_target_pairs={{0,8},{24,16},{1,9},{25,17},{2,10},{26,18},{3,11},{27,19},{4,12},{... | collective-permute-start | bytes 1966088 | tf_op jit(solution)/shard_map/ppermute | solution.py:412
  101.4 14.5 %collective-permute-start.18 = (bf16[1280,256]{1,0:T(8,128)(2,1)S(1)}, bf16[1280,256]{1,0:T(8,128)(2,1)S(1)}, u32[]{:S(2)}, u32[]{:S(2)}) collective-permute-start(bf16[1280,256]{1,0:T(8,128)(2,1)S(1)} %get-tuple-element.49), channel_id=1, source_target_pairs={{8,16},{16,8},{9,17},{17,9},{10,18},{18,10},{11,19},{19,11},{12,20... | collective-permute-start | bytes 1966088 | tf_op jit(solution)/shard_map/ppermute | solution.py:411
  102.1 13.8 %collective-permute-start.20 = (f32[1,128]{1,0:T(1,128)S(1)}, f32[1,128]{1,0:T(1,128)S(1)}, u32[]{:S(2)}, u32[]{:S(2)}) collective-permute-start(f32[1,128]{1,0:T(1,128)S(1)} %get-tuple-element.59), channel_id=1, source_target_pairs={{0,9},{1,8},{2,11},{3,10},{4,13},{5,12},{6,15},{7,14},{8,1},{9,0},... | collective-permute-start | bytes 1544 | tf_op jit(solution)/shard_map/ppermute | solution.py:383
  116.0 7.5 %collective-permute-start.21 = (bf16[2560,512]{1,0:T(8,128)(2,1)S(1)}, bf16[2560,512]{1,0:T(8,128)(2,1)S(1)}, u32[]{:S(2)}, u32[]{:S(2)}) collective-permute-start(bf16[2560,512]{1,0:T(8,128)(2,1)S(1)} %get-tuple-element.65), channel_id=1, source_target_pairs={{0,1},{1,0},{2,3},{3,2},{4,5},{5,4},{6,7},{7,6},{8,9},{9,8},{10,11... | collective-permute-start | bytes 7864328 | tf_op jit(solution)/shard_map/ppermute | solution.py:376
  118.2 5.3 %collective-permute-start.22 = (f32[1,128]{1,0:T(1,128)S(1)}, f32[1,128]{1,0:T(1,128)S(1)}, u32[]{:S(2)}, u32[]{:S(2)}) collective-permute-start(f32[1,128]{1,0:T(1,128)S(1)} %add.46), channel_id=1, source_target_pairs={{0,18},{1,19},{2,16},{3,17},{4,22},{5,23},{6,20},{7,21},{8,26},{9,... | collective-permute-start | bytes 1544 | tf_op jit(solution)/shard_map/ppermute | solution.py:383
  123.9 19.5 %collective-permute-start.27 = (bf16[1280,256]{1,0:T(8,128)(2,1)S(1)}, bf16[1280,256]{1,0:T(8,128)(2,1)S(1)}, u32[]{:S(2)}, u32[]{:S(2)}) collective-permute-start(bf16[1280,256]{1,0:T(8,128)(2,1)S(1)} %get-tuple-element.75), channel_id=1, source_target_pairs={{0,8},{8,16},{16,24},{24,0},{1,9},{9,17},{17,25},{25,1},{2,10},{10... | collective-permute-start | bytes 1966088 | tf_op jit(solution)/shard_map/ppermute | solution.py:430
  124.0 30.3 %collective-permute-start.28 = (bf16[1280,256]{1,0:T(8,128)(2,1)S(1)}, bf16[1280,256]{1,0:T(8,128)(2,1)S(1)}, u32[]{:S(2)}, u32[]{:S(2)}) collective-permute-start(bf16[1280,256]{1,0:T(8,128)(2,1)S(1)} %get-tuple-element.76), channel_id=1, source_target_pairs={{0,24},{8,0},{16,8},{24,16},{1,25},{9,1},{17,9},{25,17},{2,26},{10... | collective-permute-start | bytes 1966088 | tf_op jit(solution)/shard_map/ppermute | solution.py:431
  129.3 26.2 %collective-permute-start.24 = (bf16[2560,128]{1,0:T(8,128)(2,1)S(1)}, bf16[2560,128]{1,0:T(8,128)(2,1)S(1)}, u32[]{:S(2)}, u32[]{:S(2)}) collective-permute-start(bf16[2560,128]{1,0:T(8,128)(2,1)S(1)} %get-tuple-element.72), channel_id=1, source_target_pairs={{0,2},{1,3},{2,0},{3,1},{4,6},{5,7},{6,4},{7,5},{8,10},{9,11},{10,... | collective-permute-start | bytes 1966088 | tf_op jit(solution)/shard_map/ppermute | solution.py:376
  130.3 29.1 %collective-permute-start.25 = (bf16[2560,128]{1,0:T(8,128)(2,1)S(1)}, bf16[2560,128]{1,0:T(8,128)(2,1)S(1)}, u32[]{:S(2)}, u32[]{:S(2)}) collective-permute-start(bf16[2560,128]{1,0:T(8,128)(2,1)S(1)} %get-tuple-element.73), channel_id=1, source_target_pairs={{0,4},{1,5},{2,6},{3,7},{4,0},{5,1},{6,2},{7,3},{8,12},{9,13},{10,... | collective-permute-start | bytes 1966088 | tf_op jit(solution)/shard_map/ppermute | solution.py:376
  131.3 28.1 %collective-permute-start.26 = (bf16[2560,128]{1,0:T(8,128)(2,1)S(1)}, bf16[2560,128]{1,0:T(8,128)(2,1)S(1)}, u32[]{:S(2)}, u32[]{:S(2)}) collective-permute-start(bf16[2560,128]{1,0:T(8,128)(2,1)S(1)} %get-tuple-element.74), channel_id=1, source_target_pairs={{0,6},{1,7},{2,4},{3,5},{4,2},{5,3},{6,0},{7,1},{8,14},{9,15},{10,... | collective-permute-start | bytes 1966088 | tf_op jit(solution)/shard_map/ppermute | solution.py:376
  (8 other events, 71.9 us)

commit v6 on v5

--- a/solution.py
+++ b/solution.py
@@ -61,7 +61,7 @@
     )(row, other)
 
 
-def side_by_side(image_pieces, text_pieces, width):
+def side_by_side(image_pieces, text_pieces, width, targets):
     img_rows = image_pieces[0][0].shape[0]
     rows = text_pieces[0][0].shape[0]
     steps = 4
@@ -69,8 +69,9 @@
     pieces = text_pieces + image_pieces
 
     def kernel(*refs):
-        *sources, texts_ref, images_ref = refs
+        *sources, targets_ref, texts_ref, images_ref, spread_ref = refs
         step = pl.program_id(0)
+        spread_ref[block_of(step, bm), :] = jnp.broadcast_to(targets_ref[pl.ds(step, 1), :], (128, bm)).T
         texts_ref[block_of(step, bt), :] = jnp.zeros((bt, width), jnp.bfloat16)
         for k, (source, (_, slot)) in enumerate(zip(sources, pieces)):
             target, size = (texts_ref, bt) if k < len(text_pieces) else (images_ref, bm)
@@ -79,27 +80,33 @@
     return pl.pallas_call(
         kernel,
         grid=(steps,),
-        out_shape=(pltpu.VMEM((rows, width), jnp.bfloat16), pltpu.VMEM((img_rows, width), jnp.bfloat16)),
+        out_shape=(
+            pltpu.VMEM((rows, width), jnp.bfloat16),
+            pltpu.VMEM((img_rows, width), jnp.bfloat16),
+            pltpu.VMEM((img_rows, 128), jnp.int32),
+        ),
         in_specs=[pl.BlockSpec((bt, piece.shape[1]), lambda i: (i, 0)) for piece, _ in text_pieces]
-        + [pl.BlockSpec((bm, piece.shape[1]), lambda i: (i, 0)) for piece, _ in image_pieces],
-        out_specs=(VMEM, VMEM),
+        + [pl.BlockSpec((bm, piece.shape[1]), lambda i: (i, 0)) for piece, _ in image_pieces]
+        + [VMEM],
+        out_specs=(VMEM, VMEM, VMEM),
         compiler_params=params(12),
         cost_estimate=cost(0.01),
         name="side_by_side",
-    )(*[piece for piece, _ in pieces])
+    )(*[piece for piece, _ in pieces], targets)
 
 
 def logits_and_stats(images, texts, far, targets):
     img_rows, width = images.shape
     rows = texts.shape[0]
-    steps, bm = targets.shape
+    steps = 4
+    bm = img_rows // steps
     pieces = rows // 256
     some = bm // pieces
 
     def kernel(images_ref, texts_ref, targets_ref, *refs):
         if far is not None:
             one_ref, other_ref, *refs = refs
-        u_ref, row_ref, col_ref, whole_ref, even_scr, odd_scr, rm_scr, rs_scr, cm_scr, cs_scr, target_scr, pos_scr = refs
+        u_ref, row_ref, col_ref, whole_ref, even_scr, odd_scr, rm_scr, rs_scr, cm_scr, cs_scr, pos_scr = refs
         step = pl.program_id(0)
 
         @pl.when(step == 0)
@@ -128,7 +135,7 @@
                 here = pl.ds(pl.multiple_of(base + first, strip), strip)
                 u = d_scr[at, :] * (logit_scale * log2e)
                 u_ref[here, :] = u
-                target = target_scr[at, :] - ids
+                target = targets_ref[here, :] - ids
                 found = jnp.zeros((strip, 128), jnp.float32)
                 for k, v in enumerate(lanes(u)):
                     found = jnp.where(target == 128 * k, v, found)
@@ -145,10 +152,6 @@
                 rs_scr[at, :] = functools.reduce(jnp.add, [jnp.exp2(v - row_max) for v in lanes(u)])
                 total = total + jnp.sum(jnp.exp2(u.reshape(strip // 8, 8, rows) - new[None]), axis=0)
             cs_scr[...] = total
-
-        @pl.when(step > 0)
-        def _():
-            target_scr[...] = jnp.broadcast_to(targets_ref[pl.ds(step - 1, 1), :], (128, bm)).T
 
         @pl.when(step == 0)
         def _():
@@ -204,19 +207,19 @@
             pltpu.VMEM((bm, 128), jnp.float32),
             pltpu.VMEM((8, rows), jnp.float32),
             pltpu.VMEM((8, rows), jnp.float32),
-            pltpu.VMEM((bm, 128), jnp.int32),
             pltpu.VMEM((strip, 128), jnp.float32),
         ],
         compiler_params=params(12),
         cost_estimate=cost(13),
         name="logits_and_stats",
-    )(in_vmem(images), in_vmem(texts), targets, *(() if far is None else far[0]))
+    )(in_vmem(images), in_vmem(texts), in_vmem(targets), *(() if far is None else map(in_vmem, far[0])))
 
 
 def weights_and_far(u, images, targets, row_lses, col_lses, slot, wide, cuts):
     img_rows = images.shape[0]
     rows = u.shape[1]
-    steps, bm = targets.shape
+    steps = 4
+    bm = img_rows // steps
     n_row, n_col = len(row_lses), len(col_lses)
     groups = [(first, min(first + 256, bm)) for first in range(0, bm, 256)]
 
@@ -224,7 +227,7 @@
         row_refs, col_refs, refs = refs[:n_row], refs[n_row : n_row + n_col], refs[n_row + n_col :]
         w_ref, loss_ref, *refs = refs
         far_refs, refs = refs[: len(cuts) - 1], refs[len(cuts) - 1 :]
-        group_scrs, (acc, row_ref, col_ref, row_scr, target_scr) = refs[: len(groups)], refs[len(groups) :]
+        group_scrs, (acc, row_ref, col_ref, row_scr) = refs[: len(groups)], refs[len(groups) :]
         step = pl.program_id(0)
 
         @pl.when(step == 0)
@@ -239,7 +242,6 @@
             loss_ref[...] = jnp.where(lane == 0, row_loss, jnp.where(lane == 1, col_loss, 0.0))
 
         row_scr[...] = jnp.broadcast_to(row_ref[pl.ds(step, 1), :], (128, bm)).T
-        target_scr[...] = jnp.broadcast_to(targets_ref[pl.ds(step, 1), :], (128, bm)).T
         ids = lax.broadcasted_iota(jnp.int32, (strip, 128), 1)
         col = col_ref[...]
         for (group, end), w_scr in zip(groups, group_scrs):
@@ -248,7 +250,7 @@
                 at = slice(first, first + strip)
                 here = pl.ds(pl.multiple_of(step * bm + first, strip), strip)
                 row = row_scr[at, :]
-                target = target_scr[at, :] - ids
+                target = targets_ref[here, :] - ids
                 for k in range(0, rows, 128):
                     v = u_ref[here, k : k + 128]
                     weight = jnp.exp2(v - row) + jnp.exp2(v - col[:, k : k + 128]) - jnp.where(target == k, 2.0, 0.0)
@@ -274,7 +276,7 @@
             pltpu.VMEM((img_rows, rows), jnp.bfloat16),
             jax.ShapeDtypeStruct((1, 128), jnp.float32),
         )
-        + tuple(jax.ShapeDtypeStruct((end - first, wide), jnp.bfloat16) for first, end in zip(cuts, cuts[1:])),
+        + tuple(pltpu.VMEM((end - first, wide), jnp.bfloat16) for first, end in zip(cuts, cuts[1:])),
         in_specs=[VMEM] * (3 + n_row + n_col),
         out_specs=(VMEM,) * (len(cuts) + 1),
         scratch_shapes=[pltpu.VMEM((end - first, rows), jnp.bfloat16) for first, end in groups]
@@ -283,12 +285,11 @@
             pltpu.VMEM((steps, bm), jnp.float32),
             pltpu.VMEM((1, rows), jnp.float32),
             pltpu.VMEM((bm, 128), jnp.float32),
-            pltpu.VMEM((bm, 128), jnp.int32),
         ],
         compiler_params=params(8),
         cost_estimate=cost(8),
         name="weights_and_far",
-    )(in_vmem(u), in_vmem(images), targets, *row_lses, *col_lses)
+    )(in_vmem(u), in_vmem(images), in_vmem(targets), *map(in_vmem, row_lses), *map(in_vmem, col_lses))
 
 
 def gradients(weights, images, texts, slots, text_wide, groups, order, microseconds=10):
@@ -327,7 +328,7 @@
             )
         for out, group in zip(image_outs, groups):
             for k, slot in enumerate(group):
-                out[:, k * wide : (k + 1) * wide] = image_acc[:, columns(slot(), wide)].astype(jnp.bfloat16)
+                out[here, k * wide : (k + 1) * wide] = image_acc[:, columns(slot(), wide)].astype(jnp.bfloat16)
 
         @pl.when(step == steps - 1)
         def _():
@@ -337,10 +338,10 @@
     return pl.pallas_call(
         kernel,
         grid=(steps,),
-        out_shape=(jax.ShapeDtypeStruct((rows, text_wide), jnp.bfloat16),) * n_text
-        + tuple(jax.ShapeDtypeStruct((img_rows, wide * len(group)), jnp.bfloat16) for group in groups),
+        out_shape=(pltpu.VMEM((rows, text_wide), jnp.bfloat16),) * n_text
+        + tuple(pltpu.VMEM((img_rows, wide * len(group)), jnp.bfloat16) for group in groups),
         in_specs=[VMEM] * (2 + bool(groups) + bool(slots)),
-        out_specs=(VMEM,) * n_text + tuple(pl.BlockSpec((bm, wide * len(g)), lambda i: (i, 0)) for g in groups),
+        out_specs=(VMEM,) * (n_text + len(groups)),
         scratch_shapes=[
             pltpu.VMEM((max(1, n_text), rows, text_wide), jnp.float32),
             pltpu.VMEM((bm, width), jnp.float32),
@@ -398,7 +399,7 @@
     parts += [swap(part, 1) for part in parts]
     image_pieces = [(part, txt_slot(flip)) for part, flip in zip(parts, (0, 2, 4, 6, 1, 3, 5, 7))]
     text_pieces = [(texts, img_slot(0)), (from_prev, img_slot(3)), (from_next, img_slot(1))]
-    most_txt, whole_img = side_by_side(image_pieces, text_pieces, width)
+    most_txt, whole_img, targets = side_by_side(image_pieces, text_pieces, width, targets)
     from_middle, from_inner, most_txt, whole_img = together(from_middle, from_inner, most_txt, whole_img)
     far = ((from_middle, from_inner), img_slot(2), lambda: lax.rem(lax.axis_index("img"), 3) > 0)
     u, row, col, whole_txt = logits_and_stats(whole_img, most_txt, far, targets)
@@ -452,6 +453,7 @@
     whole_txt = lax.all_gather(texts, "img", axis=1, tiled=True)
     txt_rows, width = whole_txt.shape
     targets = (positive - lax.axis_index("txt") * txt_rows).reshape(4, whole_img.shape[0] // 4)
+    whole_txt, whole_img, targets = side_by_side([(whole_img, first_slot)], [(whole_txt, first_slot)], width, targets)
     u, row, col, whole_txt = logits_and_stats(whole_img, whole_txt, None, targets)
     rows, cols = gathered(row, "txt"), gathered(col, "img")
     w, loss, _ = weights_and_far(u, whole_img, targets, rows, cols, first_slot, 256, (0, txt_rows))

time: 162 us -> 161 us (level)
  no operation moved by 1% of the time
where the time goes in v6:
time: 161 us
  waiting for transfers between devices  64.2 us (40%)
  Pallas kernels  47.4 us (29%)
  starting transfers between devices  41.7 us (26%)
  other arithmetic  4.07 us (3%)
  between operations  2.65 us (2%)
    ppermute x16, waiting for transfers between devices, swap(): return lax.ppermute(part, 'txt', paired(8, by))  18.9 us
    pallas_call x1, Pallas kernels, logits_and_stats(): pl.pallas_call(kernel, grid=(steps + 1,), out_shape=(pltpu.VMEM((img_rows...  17.1 us
    pallas_call x2, Pallas kernels, gradients(): pl.pallas_call(kernel, grid=(steps,), out_shape=(pltpu.VMEM((rows, text_w...  16.8 us
    ppermute x16, starting transfers between devices, swap(): return lax.ppermute(part, 'txt', paired(8, by))  15.2 us
    ppermute x1, waiting for transfers between devices, per_device_4x8(): from_prev = lax.ppermute(texts, 'img', shifted(4, 1))  12.2 us
    ppermute x1, waiting for transfers between devices, per_device_4x8(): lax.ppermute(jnp.where(is_first, from_next, from_prev), 'img', [(1, 0), (...  11.5 us
    ppermute x1, waiting for transfers between devices, per_device_4x8(): from_next = lax.ppermute(to_prev, 'img', shifted(4, -1))  10.9 us
    pallas_call x1, Pallas kernels, weights_and_far(): pl.pallas_call(kernel, grid=(steps,), out_shape=(pltpu.VMEM((img_rows, ro...  8.92 us
  transfers between devices with their start and end apart: 29, of which 11 were waited for; matrix products, arithmetic and copies ran while one was open for 2% of the time, Pallas kernels for 13%

profile of v6, /device:TPU:0, one launch (start us, length us, event | category | flops | bytes accessed | tf_op | source)
XLA Modules:
  0.0 160.7 jit_solution(8752669620302741263)
XLA Ops:
  0.6 3.1 %collective-permute-start = (bf16[1280,256]{1,0:T(8,128)(2,1)}, bf16[1280,256]{1,0:T(8,128)(2,1)S(1)}, u32[]{:S(2)}, u32[]{:S(2)}) collective-permute-start(bf16[1280,256]{1,0:T(8,128)(2,1)} %refs_0_.1), channel_id=1, source_target_pairs={{0,8},{8,16},{16,24},{24,0},{1,9},{9,17},{17,25},{25,1},{2,10},{10... | collective-permute-start | bytes 1966088 | tf_op jit(solution)/shard_map/ppermute | solution.py:393
  3.7 2.4 %collective-permute-start.6 = (bf16[2560,128]{1,0:T(8,128)(2,1)}, bf16[2560,128]{1,0:T(8,128)(2,1)S(1)}, u32[]{:S(2)}, u32[]{:S(2)}) collective-permute-start(bf16[2560,128]{1,0:T(8,128)(2,1)} %refs_3_.1), channel_id=1, source_target_pairs={{0,6},{1,7},{2,4},{3,5},{4,2},{5,3},{6,0},{7,1},{8,14},{9,15},{10,... | collective-permute-start | bytes 1966088 | tf_op jit(solution)/shard_map/ppermute | solution.py:377
  7.2 2.1 %collective-permute-start.1 = (bf16[1280,256]{1,0:T(8,128)(2,1)}, bf16[1280,256]{1,0:T(8,128)(2,1)S(1)}, u32[]{:S(2)}, u32[]{:S(2)}) collective-permute-start(bf16[1280,256]{1,0:T(8,128)(2,1)} %refs_0_.1), channel_id=1, source_target_pairs={{0,24},{8,0},{16,8},{24,16},{1,25},{9,1},{17,9},{25,17},{2,26},{10... | collective-permute-start | bytes 1966088 | tf_op jit(solution)/shard_map/ppermute | solution.py:394
  9.3 12.2 %collective-permute-done.refs_1_ = bf16[1280,256]{1,0:T(8,128)(2,1)S(1)} collective-permute-done((bf16[1280,256]{1,0:T(8,128)(2,1)}, bf16[1280,256]{1,0:T(8,128)(2,1)S(1)}, u32[]{:S(2)}, u32[]{:S(2)}) %collective-permute-start) | collective-permute-done | bytes 655392 | tf_op jit(solution)/shard_map/ppermute | solution.py:393
  22.5 12.6 %collective-permute-done.5.refs_5_ = bf16[2560,128]{1,0:T(8,128)(2,1)} collective-permute-done((bf16[2560,128]{1,0:T(8,128)(2,1)}, bf16[2560,128]{1,0:T(8,128)(2,1)}, u32[]{:S(2)}, u32[]{:S(2)}) %collective-permute-start.5) | collective-permute-done | bytes 655392 | tf_op jit(solution)/shard_map/ppermute | solution.py:377
  39.7 4.5 %side_by_side.1 = (bf16[1280,1024]{1,0:T(8,128)(2,1)S(1)}, bf16[2560,1024]{1,0:T(8,128)(2,1)S(1)}, s32[2560,128]{1,0:T(8,128)S(1)}) custom-call(bf16[1280,256]{1,0:T(8,128)(2,1)S(1)} %copy-done, bf16[1280,256]{1,0:T(8,128)(2,1)S(1)} %collective-permute-done.refs_1_, bf16[1280,256]{1,0:T(8,128)(2,1)S(1)} %collective-permute-done.1.refs_2_, ...), custom_call_target="tpu_custom_call" | custom-call | flops 11000000 | bytes 1 | tf_op jit(solution)/shard_map/side_by_side/pallas_call | solution.py:80
  44.2 11.5 %collective-permute-done.3.refs_1_ = bf16[1280,256]{1,0:T(8,128)(2,1)} collective-permute-done((bf16[1280,256]{1,0:T(8,128)(2,1)}, bf16[1280,256]{1,0:T(8,128)(2,1)}, u32[]{:S(2)}, u32[]{:S(2)}) %collective-permute-start.3) | collective-permute-done | bytes 655392 | tf_op jit(solution)/shard_map/ppermute | solution.py:398
  55.8 17.1 %logits_and_stats.1 = (f32[2560,1280]{1,0:T(8,128)S(1)}, f32[5,640]{1,0:T(8,128)S(1)}, f32[1,1280]{1,0:T(1,128)S(1)}, bf16[1280,1024]{1,0:T(8,128)(2,1)S(1)}) custom-call(bf16[2560,1024]{1,0:T(8,128)(2,1)S(1)} %get-tuple-element.43.images_ref.refs_1_.refs_0_, bf16[1280,1024]{1,0:T(8,128)(2,1)S(1)} %get-tuple-element.44.texts_ref, ...), custom_call_target="tpu_custom_call" | custom-call | flops 14300000256 | bytes 1 | tf_op jit(solution)/shard_map/logits_and_stats/pallas_call | solution.py:192
  74.2 1.7 %collective-permute-start.14 = (f32[5,640]{1,0:T(8,128)S(1)}, f32[5,640]{1,0:T(8,128)S(1)}, u32[]{:S(2)}, u32[]{:S(2)}) collective-permute-start(f32[5,640]{1,0:T(8,128)S(1)} %merge_rows.1.refs_0_._), channel_id=1, source_target_pairs={{0,6},{1,7},{2,4},{3,5},{4,2},{5,3},{6,0},{7,1},{8,14},{9,15},{10,... | collective-permute-start | bytes 38408 | tf_op jit(solution)/shard_map/ppermute | solution.py:377
  77.7 2.4 %collective-permute-start.17 = (f32[1,1280]{1,0:T(1,128)S(1)}, f32[1,1280]{1,0:T(1,128)S(1)}, u32[]{:S(2)}, u32[]{:S(2)}) collective-permute-start(f32[1,1280]{1,0:T(1,128)S(1)} %get-tuple-element.50.refs_4_), channel_id=1, source_target_pairs={{0,24},{8,16},{16,8},{24,0},{1,25},{9,17},{17,9},{25,1},{2,26},{10... | collective-permute-start | bytes 15368 | tf_op jit(solution)/shard_map/ppermute | solution.py:380
  80.1 3.6 %collective-permute-start.16 = (f32[1,1280]{1,0:T(1,128)S(1)}, f32[1,1280]{1,0:T(1,128)S(1)}, u32[]{:S(2)}, u32[]{:S(2)}) collective-permute-start(f32[1,1280]{1,0:T(1,128)S(1)} %get-tuple-element.50.refs_4_), channel_id=1, source_target_pairs={{0,16},{8,24},{16,0},{24,8},{1,17},{9,25},{17,1},{25,9},{2,18},{10... | collective-permute-start | bytes 15368 | tf_op jit(solution)/shard_map/ppermute | solution.py:380
  83.7 2.2 %collective-permute-start.15 = (f32[1,1280]{1,0:T(1,128)S(1)}, f32[1,1280]{1,0:T(1,128)S(1)}, u32[]{:S(2)}, u32[]{:S(2)}) collective-permute-start(f32[1,1280]{1,0:T(1,128)S(1)} %get-tuple-element.50.refs_4_), channel_id=1, source_target_pairs={{0,8},{8,0},{16,24},{24,16},{1,9},{9,1},{17,25},{25,17},{2,10},{10... | collective-permute-start | bytes 15368 | tf_op jit(solution)/shard_map/ppermute | solution.py:380
  87.5 8.9 %weights_and_far.1 = (bf16[2560,1280]{1,0:T(8,128)(2,1)S(1)}, f32[1,128]{1,0:T(1,128)S(1)}, bf16[1280,256]{1,0:T(8,128)(2,1)S(1)}) custom-call(f32[2560,1280]{1,0:T(8,128)S(1)} %get-tuple-element.48.u_ref, bf16[2560,1024]{1,0:T(8,128)(2,1)S(1)} %get-tuple-element.43.images_ref.refs_1_.refs_0_, s32[2560,128]{1,0:T(8,128)S(1)} %get-tuple-element.45.targets_ref, ...), custom_call_target="tpu_custom_call" | custom-call | flops 8800000000 | bytes 1 | tf_op jit(solution)/shard_map/weights_and_far/pallas_call | solution.py:272
  96.4 3.9 %collective-permute-start.19 = (bf16[1280,256]{1,0:T(8,128)(2,1)S(1)}, bf16[1280,256]{1,0:T(8,128)(2,1)S(1)}, u32[]{:S(2)}, u32[]{:S(2)}) collective-permute-start(bf16[1280,256]{1,0:T(8,128)(2,1)S(1)} %get-tuple-element.51), channel_id=1, source_target_pairs={{0,8},{24,16},{1,9},{25,17},{2,10},{26,18},{3,11},{27,19},{4,12},{... | collective-permute-start | bytes 1966088 | tf_op jit(solution)/shard_map/ppermute | solution.py:413
  101.1 13.7 %gradients.2 = (bf16[1280,256]{1,0:T(8,128)(2,1)S(1)}, bf16[1280,256]{1,0:T(8,128)(2,1)S(1)}, bf16[2560,128]{1,0:T(8,128)(2,1)S(1)}, bf16[2560,128]{1,0:T(8,128)...) custom-call(bf16[2560,1280]{1,0:T(8,128)(2,1)S(1)} %get-tuple-element.52.w_re, ...), custom_call_target="tpu_custom_call" | custom-call | flops 11000000512 | bytes 1 | tf_op jit(solution)/shard_map/gradients/pallas_call | solution.py:338
  114.9 2.2 %collective-permute-start.21 = (bf16[2560,512]{1,0:T(8,128)(2,1)S(1)}, bf16[2560,512]{1,0:T(8,128)(2,1)S(1)}, u32[]{:S(2)}, u32[]{:S(2)}) collective-permute-start(bf16[2560,512]{1,0:T(8,128)(2,1)S(1)} %get-tuple-element.67), channel_id=1, source_target_pairs={{0,1},{1,0},{2,3},{3,2},{4,5},{5,4},{6,7},{7,6},{8,9},{9,8},{10,11... | collective-permute-start | bytes 7864328 | tf_op jit(solution)/shard_map/ppermute | solution.py:377
  117.1 1.8 %collective-permute-start.22 = (f32[1,128]{1,0:T(1,128)S(1)}, f32[1,128]{1,0:T(1,128)S(1)}, u32[]{:S(2)}, u32[]{:S(2)}) collective-permute-start(f32[1,128]{1,0:T(1,128)S(1)} %add.46), channel_id=1, source_target_pairs={{0,18},{1,19},{2,16},{3,17},{4,22},{5,23},{6,20},{7,21},{8,26},{9,... | collective-permute-start | bytes 1544 | tf_op jit(solution)/shard_map/ppermute | solution.py:384
  119.1 3.3 %collective-permute-done.22 = f32[1,128]{1,0:T(1,128)S(1)} collective-permute-done((f32[1,128]{1,0:T(1,128)S(1)}, f32[1,128]{1,0:T(1,128)S(1)}, u32[]{:S(2)}, u32[]{:S(2)}) %collective-permute-start.22) | collective-permute-done | bytes 544 | tf_op jit(solution)/shard_map/ppermute | solution.py:384
  122.9 3.8 %collective-permute-start.28 = (bf16[1280,256]{1,0:T(8,128)(2,1)S(1)}, bf16[1280,256]{1,0:T(8,128)(2,1)S(1)}, u32[]{:S(2)}, u32[]{:S(2)}) collective-permute-start(bf16[1280,256]{1,0:T(8,128)(2,1)S(1)} %get-tuple-element.78), channel_id=1, source_target_pairs={{0,24},{8,0},{16,8},{24,16},{1,25},{9,1},{17,9},{25,17},{2,26},{10... | collective-permute-start | bytes 1966088 | tf_op jit(solution)/shard_map/ppermute | solution.py:432
  130.3 1.9 %collective-permute-start.26 = (bf16[2560,128]{1,0:T(8,128)(2,1)S(1)}, bf16[2560,128]{1,0:T(8,128)(2,1)S(1)}, u32[]{:S(2)}, u32[]{:S(2)}) collective-permute-start(bf16[2560,128]{1,0:T(8,128)(2,1)S(1)} %get-tuple-element.76), channel_id=1, source_target_pairs={{0,6},{1,7},{2,4},{3,5},{4,2},{5,3},{6,0},{7,1},{8,14},{9,15},{10,... | collective-permute-start | bytes 1966088 | tf_op jit(solution)/shard_map/ppermute | solution.py:377
  132.2 3.1 %gradients.3 = bf16[1280,256]{1,0:T(8,128)(2,1)S(1)} custom-call(bf16[2560,1280]{1,0:T(8,128)(2,1)S(1)} %get-tuple-element.52.w_ref, f32[1,128]{1,0:T(1,128)S(1)} %add.53._, bf16[2560,1024]{1,0:T(8,128)(2,1)S(1)} %get-tuple-element.43.images_ref.refs_1_.refs_0_), custom_call_target="tpu_custom_call" | custom-call | flops 11000000 | bytes 1 | tf_op jit(solution)/shard_map/gradients/pallas_call | solution.py:338
  136.6 5.7 %collective-permute-done.27 = bf16[1280,256]{1,0:T(8,128)(2,1)S(1)} collective-permute-done((bf16[1280,256]{1,0:T(8,128)(2,1)S(1)}, bf16[1280,256]{1,0:T(8,128)(2,1)S(1)}, u32[]{:S(2)}, u32[]{:S(2)}) %collective-permute-start.27) | collective-permute-done | bytes 655392 | tf_op jit(solution)/shard_map/ppermute | solution.py:431
  142.4 10.9 %collective-permute-done.28 = bf16[1280,256]{1,0:T(8,128)(2,1)S(1)} collective-permute-done((bf16[1280,256]{1,0:T(8,128)(2,1)S(1)}, bf16[1280,256]{1,0:T(8,128)(2,1)S(1)}, u32[]{:S(2)}, u32[]{:S(2)}) %collective-permute-start.28) | collective-permute-done | bytes 655392 | tf_op jit(solution)/shard_map/ppermute | solution.py:432
  154.4 4.0 %collective-permute-done.25 = bf16[2560,128]{1,0:T(8,128)(2,1)S(1)} collective-permute-done((bf16[2560,128]{1,0:T(8,128)(2,1)S(1)}, bf16[2560,128]{1,0:T(8,128)(2,1)S(1)}, u32[]{:S(2)}, u32[]{:S(2)}) %collective-permute-start.25) | collective-permute-done | bytes 655392 | tf_op jit(solution)/shard_map/ppermute | solution.py:377
  (57 shorter events, 19.1 us)
Async XLA Ops:
  0.6 20.9 %collective-permute-start = (bf16[1280,256]{1,0:T(8,128)(2,1)}, bf16[1280,256]{1,0:T(8,128)(2,1)S(1)}, u32[]{:S(2)}, u32[]{:S(2)}) collective-permute-start(bf16[1280,256]{1,0:T(8,128)(2,1)} %refs_0_.1), channel_id=1, source_target_pairs={{0,8},{8,16},{16,24},{24,0},{1,9},{9,17},{17,25},{25,1},{2,10},{10... | collective-permute-start | bytes 1966088 | tf_op jit(solution)/shard_map/ppermute | solution.py:393
  3.7 18.8 %collective-permute-start.6 = (bf16[2560,128]{1,0:T(8,128)(2,1)}, bf16[2560,128]{1,0:T(8,128)(2,1)S(1)}, u32[]{:S(2)}, u32[]{:S(2)}) collective-permute-start(bf16[2560,128]{1,0:T(8,128)(2,1)} %refs_3_.1), channel_id=1, source_target_pairs={{0,6},{1,7},{2,4},{3,5},{4,2},{5,3},{6,0},{7,1},{8,14},{9,15},{10,... | collective-permute-start | bytes 1966088 | tf_op jit(solution)/shard_map/ppermute | solution.py:377
  6.2 29.0 %collective-permute-start.5 = (bf16[2560,128]{1,0:T(8,128)(2,1)}, bf16[2560,128]{1,0:T(8,128)(2,1)}, u32[]{:S(2)}, u32[]{:S(2)}) collective-permute-start(bf16[2560,128]{1,0:T(8,128)(2,1)} %refs_3_.1), channel_id=1, source_target_pairs={{0,4},{1,5},{2,6},{3,7},{4,0},{5,1},{6,2},{7,3},{8,12},{9,13},{10,... | collective-permute-start | bytes 1966088 | tf_op jit(solution)/shard_map/ppermute | solution.py:377
  6.7 28.6 %collective-permute-start.4 = (bf16[2560,128]{1,0:T(8,128)(2,1)}, bf16[2560,128]{1,0:T(8,128)(2,1)}, u32[]{:S(2)}, u32[]{:S(2)}) collective-permute-start(bf16[2560,128]{1,0:T(8,128)(2,1)} %refs_3_.1), channel_id=1, source_target_pairs={{0,2},{1,3},{2,0},{3,1},{4,6},{5,7},{6,4},{7,5},{8,10},{9,11},{10,... | collective-permute-start | bytes 1966088 | tf_op jit(solution)/shard_map/ppermute | solution.py:377
  7.2 28.5 %collective-permute-start.1 = (bf16[1280,256]{1,0:T(8,128)(2,1)}, bf16[1280,256]{1,0:T(8,128)(2,1)S(1)}, u32[]{:S(2)}, u32[]{:S(2)}) collective-permute-start(bf16[1280,256]{1,0:T(8,128)(2,1)} %refs_0_.1), channel_id=1, source_target_pairs={{0,24},{8,0},{16,8},{24,16},{1,25},{9,1},{17,9},{25,17},{2,26},{10... | collective-permute-start | bytes 1966088 | tf_op jit(solution)/shard_map/ppermute | solution.py:394
  21.5 16.6 %collective-permute-start.7 = (bf16[2560,128]{1,0:T(8,128)(2,1)}, bf16[2560,128]{1,0:T(8,128)(2,1)}, u32[]{:S(2)}, u32[]{:S(2)}) collective-permute-start(bf16[2560,128]{1,0:T(8,128)(2,1)} %refs_3_.1), channel_id=1, source_target_pairs={{0,1},{1,0},{2,3},{3,2},{4,5},{5,4},{6,7},{7,6},{8,9},{9,8},{10,11... | collective-permute-start | bytes 1966088 | tf_op jit(solution)/shard_map/ppermute | solution.py:377
  22.5 17.2 %collective-permute-start.10 = (bf16[2560,128]{1,0:T(8,128)(2,1)S(1)}, bf16[2560,128]{1,0:T(8,128)(2,1)}, u32[]{:S(2)}, u32[]{:S(2)}) collective-permute-start(bf16[2560,128]{1,0:T(8,128)(2,1)S(1)} %collective-permute-done.6.refs_6_), channel_id=1, source_target_pairs={{0,1},{1,0},{2,3},{3,2},{4,5},{5,4},{6,7},{7,6},{8,9},{9,8},{10,11... | collective-permute-start | bytes 1966088 | tf_op jit(solution)/shard_map/ppermute | solution.py:377
  36.8 18.9 %collective-permute-start.3 = (bf16[1280,256]{1,0:T(8,128)(2,1)}, bf16[1280,256]{1,0:T(8,128)(2,1)}, u32[]{:S(2)}, u32[]{:S(2)}) collective-permute-start(bf16[1280,256]{1,0:T(8,128)(2,1)} %get-tuple-element.85), channel_id=1, source_target_pairs={{8,0},{16,24},{9,1},{17,25},{10,2},{18,26},{11,3},{19,27},{12,4},{... | collective-permute-start | bytes 1966088 | tf_op jit(solution)/shard_map/ppermute | solution.py:398
  38.1 17.6 %collective-permute-start.2 = (bf16[1280,256]{1,0:T(8,128)(2,1)}, bf16[1280,256]{1,0:T(8,128)(2,1)}, u32[]{:S(2)}, u32[]{:S(2)}) collective-permute-start(bf16[1280,256]{1,0:T(8,128)(2,1)} %get-tuple-element.86), channel_id=1, source_target_pairs={{8,16},{16,8},{9,17},{17,9},{10,18},{18,10},{11,19},{19,11},{12,20... | collective-permute-start | bytes 1966088 | tf_op jit(solution)/shard_map/ppermute | solution.py:397
  74.2 13.3 %collective-permute-start.14 = (f32[5,640]{1,0:T(8,128)S(1)}, f32[5,640]{1,0:T(8,128)S(1)}, u32[]{:S(2)}, u32[]{:S(2)}) collective-permute-start(f32[5,640]{1,0:T(8,128)S(1)} %merge_rows.1.refs_0_._), channel_id=1, source_target_pairs={{0,6},{1,7},{2,4},{3,5},{4,2},{5,3},{6,0},{7,1},{8,14},{9,15},{10,... | collective-permute-start | bytes 38408 | tf_op jit(solution)/shard_map/ppermute | solution.py:377
  75.9 11.5 %collective-permute-start.13 = (f32[5,640]{1,0:T(8,128)S(1)}, f32[5,640]{1,0:T(8,128)S(1)}, u32[]{:S(2)}, u32[]{:S(2)}) collective-permute-start(f32[5,640]{1,0:T(8,128)S(1)} %merge_rows.1.refs_0_._), channel_id=1, source_target_pairs={{0,4},{1,5},{2,6},{3,7},{4,0},{5,1},{6,2},{7,3},{8,12},{9,13},{10,... | collective-permute-start | bytes 38408 | tf_op jit(solution)/shard_map/ppermute | solution.py:377
  77.2 10.3 %collective-permute-start.12 = (f32[5,640]{1,0:T(8,128)S(1)}, f32[5,640]{1,0:T(8,128)S(1)}, u32[]{:S(2)}, u32[]{:S(2)}) collective-permute-start(f32[5,640]{1,0:T(8,128)S(1)} %merge_rows.1.refs_0_._), channel_id=1, source_target_pairs={{0,2},{1,3},{2,0},{3,1},{4,6},{5,7},{6,4},{7,5},{8,10},{9,11},{10,... | collective-permute-start | bytes 38408 | tf_op jit(solution)/shard_map/ppermute | solution.py:377
  77.7 6.0 %collective-permute-start.17 = (f32[1,1280]{1,0:T(1,128)S(1)}, f32[1,1280]{1,0:T(1,128)S(1)}, u32[]{:S(2)}, u32[]{:S(2)}) collective-permute-start(f32[1,1280]{1,0:T(1,128)S(1)} %get-tuple-element.50.refs_4_), channel_id=1, source_target_pairs={{0,24},{8,16},{16,8},{24,0},{1,25},{9,17},{17,9},{25,1},{2,26},{10... | collective-permute-start | bytes 15368 | tf_op jit(solution)/shard_map/ppermute | solution.py:380
  80.1 5.7 %collective-permute-start.16 = (f32[1,1280]{1,0:T(1,128)S(1)}, f32[1,1280]{1,0:T(1,128)S(1)}, u32[]{:S(2)}, u32[]{:S(2)}) collective-permute-start(f32[1,1280]{1,0:T(1,128)S(1)} %get-tuple-element.50.refs_4_), channel_id=1, source_target_pairs={{0,16},{8,24},{16,0},{24,8},{1,17},{9,25},{17,1},{25,9},{2,18},{10... | collective-permute-start | bytes 15368 | tf_op jit(solution)/shard_map/ppermute | solution.py:380
  96.4 18.5 %collective-permute-start.19 = (bf16[1280,256]{1,0:T(8,128)(2,1)S(1)}, bf16[1280,256]{1,0:T(8,128)(2,1)S(1)}, u32[]{:S(2)}, u32[]{:S(2)}) collective-permute-start(bf16[1280,256]{1,0:T(8,128)(2,1)S(1)} %get-tuple-element.51), channel_id=1, source_target_pairs={{0,8},{24,16},{1,9},{25,17},{2,10},{26,18},{3,11},{27,19},{4,12},{... | collective-permute-start | bytes 1966088 | tf_op jit(solution)/shard_map/ppermute | solution.py:413
  100.3 14.5 %collective-permute-start.18 = (bf16[1280,256]{1,0:T(8,128)(2,1)S(1)}, bf16[1280,256]{1,0:T(8,128)(2,1)S(1)}, u32[]{:S(2)}, u32[]{:S(2)}) collective-permute-start(bf16[1280,256]{1,0:T(8,128)(2,1)S(1)} %get-tuple-element.51), channel_id=1, source_target_pairs={{8,16},{16,8},{9,17},{17,9},{10,18},{18,10},{11,19},{19,11},{12,20... | collective-permute-start | bytes 1966088 | tf_op jit(solution)/shard_map/ppermute | solution.py:412
  101.0 13.8 %collective-permute-start.20 = (f32[1,128]{1,0:T(1,128)S(1)}, f32[1,128]{1,0:T(1,128)S(1)}, u32[]{:S(2)}, u32[]{:S(2)}) collective-permute-start(f32[1,128]{1,0:T(1,128)S(1)} %get-tuple-element.61), channel_id=1, source_target_pairs={{0,9},{1,8},{2,11},{3,10},{4,13},{5,12},{6,15},{7,14},{8,1},{9,0},... | collective-permute-start | bytes 1544 | tf_op jit(solution)/shard_map/ppermute | solution.py:384
  114.9 7.6 %collective-permute-start.21 = (bf16[2560,512]{1,0:T(8,128)(2,1)S(1)}, bf16[2560,512]{1,0:T(8,128)(2,1)S(1)}, u32[]{:S(2)}, u32[]{:S(2)}) collective-permute-start(bf16[2560,512]{1,0:T(8,128)(2,1)S(1)} %get-tuple-element.67), channel_id=1, source_target_pairs={{0,1},{1,0},{2,3},{3,2},{4,5},{5,4},{6,7},{7,6},{8,9},{9,8},{10,11... | collective-permute-start | bytes 7864328 | tf_op jit(solution)/shard_map/ppermute | solution.py:377
  117.1 5.3 %collective-permute-start.22 = (f32[1,128]{1,0:T(1,128)S(1)}, f32[1,128]{1,0:T(1,128)S(1)}, u32[]{:S(2)}, u32[]{:S(2)}) collective-permute-start(f32[1,128]{1,0:T(1,128)S(1)} %add.46), channel_id=1, source_target_pairs={{0,18},{1,19},{2,16},{3,17},{4,22},{5,23},{6,20},{7,21},{8,26},{9,... | collective-permute-start | bytes 1544 | tf_op jit(solution)/shard_map/ppermute | solution.py:384
  122.9 19.5 %collective-permute-start.27 = (bf16[1280,256]{1,0:T(8,128)(2,1)S(1)}, bf16[1280,256]{1,0:T(8,128)(2,1)S(1)}, u32[]{:S(2)}, u32[]{:S(2)}) collective-permute-start(bf16[1280,256]{1,0:T(8,128)(2,1)S(1)} %get-tuple-element.77), channel_id=1, source_target_pairs={{0,8},{8,16},{16,24},{24,0},{1,9},{9,17},{17,25},{25,1},{2,10},{10... | collective-permute-start | bytes 1966088 | tf_op jit(solution)/shard_map/ppermute | solution.py:431
  122.9 30.3 %collective-permute-start.28 = (bf16[1280,256]{1,0:T(8,128)(2,1)S(1)}, bf16[1280,256]{1,0:T(8,128)(2,1)S(1)}, u32[]{:S(2)}, u32[]{:S(2)}) collective-permute-start(bf16[1280,256]{1,0:T(8,128)(2,1)S(1)} %get-tuple-element.78), channel_id=1, source_target_pairs={{0,24},{8,0},{16,8},{24,16},{1,25},{9,1},{17,9},{25,17},{2,26},{10... | collective-permute-start | bytes 1966088 | tf_op jit(solution)/shard_map/ppermute | solution.py:432
  128.2 26.2 %collective-permute-start.24 = (bf16[2560,128]{1,0:T(8,128)(2,1)S(1)}, bf16[2560,128]{1,0:T(8,128)(2,1)S(1)}, u32[]{:S(2)}, u32[]{:S(2)}) collective-permute-start(bf16[2560,128]{1,0:T(8,128)(2,1)S(1)} %get-tuple-element.74), channel_id=1, source_target_pairs={{0,2},{1,3},{2,0},{3,1},{4,6},{5,7},{6,4},{7,5},{8,10},{9,11},{10,... | collective-permute-start | bytes 1966088 | tf_op jit(solution)/shard_map/ppermute | solution.py:377
  129.2 29.1 %collective-permute-start.25 = (bf16[2560,128]{1,0:T(8,128)(2,1)S(1)}, bf16[2560,128]{1,0:T(8,128)(2,1)S(1)}, u32[]{:S(2)}, u32[]{:S(2)}) collective-permute-start(bf16[2560,128]{1,0:T(8,128)(2,1)S(1)} %get-tuple-element.75), channel_id=1, source_target_pairs={{0,4},{1,5},{2,6},{3,7},{4,0},{5,1},{6,2},{7,3},{8,12},{9,13},{10,... | collective-permute-start | bytes 1966088 | tf_op jit(solution)/shard_map/ppermute | solution.py:377
  130.3 28.1 %collective-permute-start.26 = (bf16[2560,128]{1,0:T(8,128)(2,1)S(1)}, bf16[2560,128]{1,0:T(8,128)(2,1)S(1)}, u32[]{:S(2)}, u32[]{:S(2)}) collective-permute-start(bf16[2560,128]{1,0:T(8,128)(2,1)S(1)} %get-tuple-element.76), channel_id=1, source_target_pairs={{0,6},{1,7},{2,4},{3,5},{4,2},{5,3},{6,0},{7,1},{8,14},{9,15},{10,... | collective-permute-start | bytes 1966088 | tf_op jit(solution)/shard_map/ppermute | solution.py:377
  (8 other events, 71.9 us)

commit v7 on v6

--- a/solution.py
+++ b/solution.py
@@ -10,7 +10,7 @@
 logit_scale = 100.0
 log2e = math.log2(math.e)
 ln2 = math.log(2.0)
-strip = 32
+strip = 16
 
 VMEM = pl.BlockSpec(memory_space=pltpu.VMEM)
 

time: 161 us -> 160 us (level)
  no operation moved by 1% of the time
where the time goes in v7:
time: 160 us; the launch traced here: 159 us
  waiting for transfers between devices  64.2 us (40%)
  Pallas kernels  46 us (29%)
  starting transfers between devices  41.7 us (26%)
  other arithmetic  4.07 us (3%)
  between operations  2.65 us (2%)
    ppermute x16, waiting for transfers between devices, swap(): return lax.ppermute(part, 'txt', paired(8, by))  18.9 us
    pallas_call x2, Pallas kernels, gradients(): pl.pallas_call(kernel, grid=(steps,), out_shape=(pltpu.VMEM((rows, text_w...  16.8 us
    pallas_call x1, Pallas kernels, logits_and_stats(): pl.pallas_call(kernel, grid=(steps + 1,), out_shape=(pltpu.VMEM((img_rows...  15.8 us
    ppermute x16, starting transfers between devices, swap(): return lax.ppermute(part, 'txt', paired(8, by))  15.2 us
    ppermute x1, waiting for transfers between devices, per_device_4x8(): from_prev = lax.ppermute(texts, 'img', shifted(4, 1))  12.2 us
    ppermute x1, waiting for transfers between devices, per_device_4x8(): lax.ppermute(jnp.where(is_first, from_next, from_prev), 'img', [(1, 0), (...  11.5 us
    ppermute x1, waiting for transfers between devices, per_device_4x8(): from_next = lax.ppermute(to_prev, 'img', shifted(4, -1))  10.8 us
    pallas_call x1, Pallas kernels, weights_and_far(): pl.pallas_call(kernel, grid=(steps,), out_shape=(pltpu.VMEM((img_rows, ro...  8.8 us
  transfers between devices with their start and end apart: 29, of which 11 were waited for; matrix products, arithmetic and copies ran while one was open for 2% of the time, Pallas kernels for 13%

profile of v7, /device:TPU:0, one launch (start us, length us, event | category | flops | bytes accessed | tf_op | source)
XLA Modules:
  0.0 159.3 jit_solution(14486839896503819812)
XLA Ops:
  0.6 3.1 %collective-permute-start = (bf16[1280,256]{1,0:T(8,128)(2,1)}, bf16[1280,256]{1,0:T(8,128)(2,1)S(1)}, u32[]{:S(2)}, u32[]{:S(2)}) collective-permute-start(bf16[1280,256]{1,0:T(8,128)(2,1)} %refs_0_.1), channel_id=1, source_target_pairs={{0,8},{8,16},{16,24},{24,0},{1,9},{9,17},{17,25},{25,1},{2,10},{10... | collective-permute-start | bytes 1966088 | tf_op jit(solution)/shard_map/ppermute | solution.py:393
  3.7 2.4 %collective-permute-start.6 = (bf16[2560,128]{1,0:T(8,128)(2,1)}, bf16[2560,128]{1,0:T(8,128)(2,1)S(1)}, u32[]{:S(2)}, u32[]{:S(2)}) collective-permute-start(bf16[2560,128]{1,0:T(8,128)(2,1)} %refs_3_.1), channel_id=1, source_target_pairs={{0,6},{1,7},{2,4},{3,5},{4,2},{5,3},{6,0},{7,1},{8,14},{9,15},{10,... | collective-permute-start | bytes 1966088 | tf_op jit(solution)/shard_map/ppermute | solution.py:377
  7.2 2.1 %collective-permute-start.1 = (bf16[1280,256]{1,0:T(8,128)(2,1)}, bf16[1280,256]{1,0:T(8,128)(2,1)S(1)}, u32[]{:S(2)}, u32[]{:S(2)}) collective-permute-start(bf16[1280,256]{1,0:T(8,128)(2,1)} %refs_0_.1), channel_id=1, source_target_pairs={{0,24},{8,0},{16,8},{24,16},{1,25},{9,1},{17,9},{25,17},{2,26},{10... | collective-permute-start | bytes 1966088 | tf_op jit(solution)/shard_map/ppermute | solution.py:394
  9.3 12.2 %collective-permute-done.refs_1_ = bf16[1280,256]{1,0:T(8,128)(2,1)S(1)} collective-permute-done((bf16[1280,256]{1,0:T(8,128)(2,1)}, bf16[1280,256]{1,0:T(8,128)(2,1)S(1)}, u32[]{:S(2)}, u32[]{:S(2)}) %collective-permute-start) | collective-permute-done | bytes 655392 | tf_op jit(solution)/shard_map/ppermute | solution.py:393
  22.5 12.6 %collective-permute-done.5.refs_5_ = bf16[2560,128]{1,0:T(8,128)(2,1)} collective-permute-done((bf16[2560,128]{1,0:T(8,128)(2,1)}, bf16[2560,128]{1,0:T(8,128)(2,1)}, u32[]{:S(2)}, u32[]{:S(2)}) %collective-permute-start.5) | collective-permute-done | bytes 655392 | tf_op jit(solution)/shard_map/ppermute | solution.py:377
  39.7 4.5 %side_by_side.1 = (bf16[1280,1024]{1,0:T(8,128)(2,1)S(1)}, bf16[2560,1024]{1,0:T(8,128)(2,1)S(1)}, s32[2560,128]{1,0:T(8,128)S(1)}) custom-call(bf16[1280,256]{1,0:T(8,128)(2,1)S(1)} %copy-done, bf16[1280,256]{1,0:T(8,128)(2,1)S(1)} %collective-permute-done.refs_1_, bf16[1280,256]{1,0:T(8,128)(2,1)S(1)} %collective-permute-done.1.refs_2_, ...), custom_call_target="tpu_custom_call" | custom-call | flops 11000000 | bytes 1 | tf_op jit(solution)/shard_map/side_by_side/pallas_call | solution.py:80
  44.2 11.5 %collective-permute-done.3.refs_1_ = bf16[1280,256]{1,0:T(8,128)(2,1)} collective-permute-done((bf16[1280,256]{1,0:T(8,128)(2,1)}, bf16[1280,256]{1,0:T(8,128)(2,1)}, u32[]{:S(2)}, u32[]{:S(2)}) %collective-permute-start.3) | collective-permute-done | bytes 655392 | tf_op jit(solution)/shard_map/ppermute | solution.py:398
  55.8 15.8 %logits_and_stats.1 = (f32[2560,1280]{1,0:T(8,128)S(1)}, f32[5,640]{1,0:T(8,128)S(1)}, f32[1,1280]{1,0:T(1,128)S(1)}, bf16[1280,1024]{1,0:T(8,128)(2,1)S(1)}) custom-call(bf16[2560,1024]{1,0:T(8,128)(2,1)S(1)} %get-tuple-element.43.images_ref.refs_1_.refs_0_, bf16[1280,1024]{1,0:T(8,128)(2,1)S(1)} %get-tuple-element.44.texts_ref, ...), custom_call_target="tpu_custom_call" | custom-call | flops 14300000256 | bytes 1 | tf_op jit(solution)/shard_map/logits_and_stats/pallas_call | solution.py:192
  72.9 1.7 %collective-permute-start.14 = (f32[5,640]{1,0:T(8,128)S(1)}, f32[5,640]{1,0:T(8,128)S(1)}, u32[]{:S(2)}, u32[]{:S(2)}) collective-permute-start(f32[5,640]{1,0:T(8,128)S(1)} %merge_rows.1.refs_0_._), channel_id=1, source_target_pairs={{0,6},{1,7},{2,4},{3,5},{4,2},{5,3},{6,0},{7,1},{8,14},{9,15},{10,... | collective-permute-start | bytes 38408 | tf_op jit(solution)/shard_map/ppermute | solution.py:377
  76.5 2.4 %collective-permute-start.17 = (f32[1,1280]{1,0:T(1,128)S(1)}, f32[1,1280]{1,0:T(1,128)S(1)}, u32[]{:S(2)}, u32[]{:S(2)}) collective-permute-start(f32[1,1280]{1,0:T(1,128)S(1)} %get-tuple-element.50.refs_4_), channel_id=1, source_target_pairs={{0,24},{8,16},{16,8},{24,0},{1,25},{9,17},{17,9},{25,1},{2,26},{10... | collective-permute-start | bytes 15368 | tf_op jit(solution)/shard_map/ppermute | solution.py:380
  78.8 3.6 %collective-permute-start.16 = (f32[1,1280]{1,0:T(1,128)S(1)}, f32[1,1280]{1,0:T(1,128)S(1)}, u32[]{:S(2)}, u32[]{:S(2)}) collective-permute-start(f32[1,1280]{1,0:T(1,128)S(1)} %get-tuple-element.50.refs_4_), channel_id=1, source_target_pairs={{0,16},{8,24},{16,0},{24,8},{1,17},{9,25},{17,1},{25,9},{2,18},{10... | collective-permute-start | bytes 15368 | tf_op jit(solution)/shard_map/ppermute | solution.py:380
  82.4 2.2 %collective-permute-start.15 = (f32[1,1280]{1,0:T(1,128)S(1)}, f32[1,1280]{1,0:T(1,128)S(1)}, u32[]{:S(2)}, u32[]{:S(2)}) collective-permute-start(f32[1,1280]{1,0:T(1,128)S(1)} %get-tuple-element.50.refs_4_), channel_id=1, source_target_pairs={{0,8},{8,0},{16,24},{24,16},{1,9},{9,1},{17,25},{25,17},{2,10},{10... | collective-permute-start | bytes 15368 | tf_op jit(solution)/shard_map/ppermute | solution.py:380
  86.2 8.8 %weights_and_far.1 = (bf16[2560,1280]{1,0:T(8,128)(2,1)S(1)}, f32[1,128]{1,0:T(1,128)S(1)}, bf16[1280,256]{1,0:T(8,128)(2,1)S(1)}) custom-call(f32[2560,1280]{1,0:T(8,128)S(1)} %get-tuple-element.48.u_ref, bf16[2560,1024]{1,0:T(8,128)(2,1)S(1)} %get-tuple-element.43.images_ref.refs_1_.refs_0_, s32[2560,128]{1,0:T(8,128)S(1)} %get-tuple-element.45.targets_ref, ...), custom_call_target="tpu_custom_call" | custom-call | flops 8800000000 | bytes 1 | tf_op jit(solution)/shard_map/weights_and_far/pallas_call | solution.py:272
  95.0 3.9 %collective-permute-start.19 = (bf16[1280,256]{1,0:T(8,128)(2,1)S(1)}, bf16[1280,256]{1,0:T(8,128)(2,1)S(1)}, u32[]{:S(2)}, u32[]{:S(2)}) collective-permute-start(bf16[1280,256]{1,0:T(8,128)(2,1)S(1)} %get-tuple-element.51), channel_id=1, source_target_pairs={{0,8},{24,16},{1,9},{25,17},{2,10},{26,18},{3,11},{27,19},{4,12},{... | collective-permute-start | bytes 1966088 | tf_op jit(solution)/shard_map/ppermute | solution.py:413
  99.7 13.7 %gradients.2 = (bf16[1280,256]{1,0:T(8,128)(2,1)S(1)}, bf16[1280,256]{1,0:T(8,128)(2,1)S(1)}, bf16[2560,128]{1,0:T(8,128)(2,1)S(1)}, bf16[2560,128]{1,0:T(8,128)...) custom-call(bf16[2560,1280]{1,0:T(8,128)(2,1)S(1)} %get-tuple-element.52.w_re, ...), custom_call_target="tpu_custom_call" | custom-call | flops 11000000512 | bytes 1 | tf_op jit(solution)/shard_map/gradients/pallas_call | solution.py:338
  113.5 2.2 %collective-permute-start.21 = (bf16[2560,512]{1,0:T(8,128)(2,1)S(1)}, bf16[2560,512]{1,0:T(8,128)(2,1)S(1)}, u32[]{:S(2)}, u32[]{:S(2)}) collective-permute-start(bf16[2560,512]{1,0:T(8,128)(2,1)S(1)} %get-tuple-element.67), channel_id=1, source_target_pairs={{0,1},{1,0},{2,3},{3,2},{4,5},{5,4},{6,7},{7,6},{8,9},{9,8},{10,11... | collective-permute-start | bytes 7864328 | tf_op jit(solution)/shard_map/ppermute | solution.py:377
  115.7 1.8 %collective-permute-start.22 = (f32[1,128]{1,0:T(1,128)S(1)}, f32[1,128]{1,0:T(1,128)S(1)}, u32[]{:S(2)}, u32[]{:S(2)}) collective-permute-start(f32[1,128]{1,0:T(1,128)S(1)} %add.46), channel_id=1, source_target_pairs={{0,18},{1,19},{2,16},{3,17},{4,22},{5,23},{6,20},{7,21},{8,26},{9,... | collective-permute-start | bytes 1544 | tf_op jit(solution)/shard_map/ppermute | solution.py:384
  117.7 3.3 %collective-permute-done.22 = f32[1,128]{1,0:T(1,128)S(1)} collective-permute-done((f32[1,128]{1,0:T(1,128)S(1)}, f32[1,128]{1,0:T(1,128)S(1)}, u32[]{:S(2)}, u32[]{:S(2)}) %collective-permute-start.22) | collective-permute-done | bytes 544 | tf_op jit(solution)/shard_map/ppermute | solution.py:384
  121.5 3.8 %collective-permute-start.28 = (bf16[1280,256]{1,0:T(8,128)(2,1)S(1)}, bf16[1280,256]{1,0:T(8,128)(2,1)S(1)}, u32[]{:S(2)}, u32[]{:S(2)}) collective-permute-start(bf16[1280,256]{1,0:T(8,128)(2,1)S(1)} %get-tuple-element.78), channel_id=1, source_target_pairs={{0,24},{8,0},{16,8},{24,16},{1,25},{9,1},{17,9},{25,17},{2,26},{10... | collective-permute-start | bytes 1966088 | tf_op jit(solution)/shard_map/ppermute | solution.py:432
  128.9 1.9 %collective-permute-start.26 = (bf16[2560,128]{1,0:T(8,128)(2,1)S(1)}, bf16[2560,128]{1,0:T(8,128)(2,1)S(1)}, u32[]{:S(2)}, u32[]{:S(2)}) collective-permute-start(bf16[2560,128]{1,0:T(8,128)(2,1)S(1)} %get-tuple-element.76), channel_id=1, source_target_pairs={{0,6},{1,7},{2,4},{3,5},{4,2},{5,3},{6,0},{7,1},{8,14},{9,15},{10,... | collective-permute-start | bytes 1966088 | tf_op jit(solution)/shard_map/ppermute | solution.py:377
  130.8 3.1 %gradients.3 = bf16[1280,256]{1,0:T(8,128)(2,1)S(1)} custom-call(bf16[2560,1280]{1,0:T(8,128)(2,1)S(1)} %get-tuple-element.52.w_ref, f32[1,128]{1,0:T(1,128)S(1)} %add.53._, bf16[2560,1024]{1,0:T(8,128)(2,1)S(1)} %get-tuple-element.43.images_ref.refs_1_.refs_0_), custom_call_target="tpu_custom_call" | custom-call | flops 11000000 | bytes 1 | tf_op jit(solution)/shard_map/gradients/pallas_call | solution.py:338
  135.2 5.7 %collective-permute-done.27 = bf16[1280,256]{1,0:T(8,128)(2,1)S(1)} collective-permute-done((bf16[1280,256]{1,0:T(8,128)(2,1)S(1)}, bf16[1280,256]{1,0:T(8,128)(2,1)S(1)}, u32[]{:S(2)}, u32[]{:S(2)}) %collective-permute-start.27) | collective-permute-done | bytes 655392 | tf_op jit(solution)/shard_map/ppermute | solution.py:431
  141.0 10.8 %collective-permute-done.28 = bf16[1280,256]{1,0:T(8,128)(2,1)S(1)} collective-permute-done((bf16[1280,256]{1,0:T(8,128)(2,1)S(1)}, bf16[1280,256]{1,0:T(8,128)(2,1)S(1)}, u32[]{:S(2)}, u32[]{:S(2)}) %collective-permute-start.28) | collective-permute-done | bytes 655392 | tf_op jit(solution)/shard_map/ppermute | solution.py:432
  153.0 4.0 %collective-permute-done.25 = bf16[2560,128]{1,0:T(8,128)(2,1)S(1)} collective-permute-done((bf16[2560,128]{1,0:T(8,128)(2,1)S(1)}, bf16[2560,128]{1,0:T(8,128)(2,1)S(1)}, u32[]{:S(2)}, u32[]{:S(2)}) %collective-permute-start.25) | collective-permute-done | bytes 655392 | tf_op jit(solution)/shard_map/ppermute | solution.py:377
  (57 shorter events, 19.1 us)
Async XLA Ops:
  0.6 20.9 %collective-permute-start = (bf16[1280,256]{1,0:T(8,128)(2,1)}, bf16[1280,256]{1,0:T(8,128)(2,1)S(1)}, u32[]{:S(2)}, u32[]{:S(2)}) collective-permute-start(bf16[1280,256]{1,0:T(8,128)(2,1)} %refs_0_.1), channel_id=1, source_target_pairs={{0,8},{8,16},{16,24},{24,0},{1,9},{9,17},{17,25},{25,1},{2,10},{10... | collective-permute-start | bytes 1966088 | tf_op jit(solution)/shard_map/ppermute | solution.py:393
  3.7 18.8 %collective-permute-start.6 = (bf16[2560,128]{1,0:T(8,128)(2,1)}, bf16[2560,128]{1,0:T(8,128)(2,1)S(1)}, u32[]{:S(2)}, u32[]{:S(2)}) collective-permute-start(bf16[2560,128]{1,0:T(8,128)(2,1)} %refs_3_.1), channel_id=1, source_target_pairs={{0,6},{1,7},{2,4},{3,5},{4,2},{5,3},{6,0},{7,1},{8,14},{9,15},{10,... | collective-permute-start | bytes 1966088 | tf_op jit(solution)/shard_map/ppermute | solution.py:377
  6.2 29.0 %collective-permute-start.5 = (bf16[2560,128]{1,0:T(8,128)(2,1)}, bf16[2560,128]{1,0:T(8,128)(2,1)}, u32[]{:S(2)}, u32[]{:S(2)}) collective-permute-start(bf16[2560,128]{1,0:T(8,128)(2,1)} %refs_3_.1), channel_id=1, source_target_pairs={{0,4},{1,5},{2,6},{3,7},{4,0},{5,1},{6,2},{7,3},{8,12},{9,13},{10,... | collective-permute-start | bytes 1966088 | tf_op jit(solution)/shard_map/ppermute | solution.py:377
  6.7 28.6 %collective-permute-start.4 = (bf16[2560,128]{1,0:T(8,128)(2,1)}, bf16[2560,128]{1,0:T(8,128)(2,1)}, u32[]{:S(2)}, u32[]{:S(2)}) collective-permute-start(bf16[2560,128]{1,0:T(8,128)(2,1)} %refs_3_.1), channel_id=1, source_target_pairs={{0,2},{1,3},{2,0},{3,1},{4,6},{5,7},{6,4},{7,5},{8,10},{9,11},{10,... | collective-permute-start | bytes 1966088 | tf_op jit(solution)/shard_map/ppermute | solution.py:377
  7.2 28.5 %collective-permute-start.1 = (bf16[1280,256]{1,0:T(8,128)(2,1)}, bf16[1280,256]{1,0:T(8,128)(2,1)S(1)}, u32[]{:S(2)}, u32[]{:S(2)}) collective-permute-start(bf16[1280,256]{1,0:T(8,128)(2,1)} %refs_0_.1), channel_id=1, source_target_pairs={{0,24},{8,0},{16,8},{24,16},{1,25},{9,1},{17,9},{25,17},{2,26},{10... | collective-permute-start | bytes 1966088 | tf_op jit(solution)/shard_map/ppermute | solution.py:394
  21.5 16.6 %collective-permute-start.7 = (bf16[2560,128]{1,0:T(8,128)(2,1)}, bf16[2560,128]{1,0:T(8,128)(2,1)}, u32[]{:S(2)}, u32[]{:S(2)}) collective-permute-start(bf16[2560,128]{1,0:T(8,128)(2,1)} %refs_3_.1), channel_id=1, source_target_pairs={{0,1},{1,0},{2,3},{3,2},{4,5},{5,4},{6,7},{7,6},{8,9},{9,8},{10,11... | collective-permute-start | bytes 1966088 | tf_op jit(solution)/shard_map/ppermute | solution.py:377
  22.5 17.2 %collective-permute-start.10 = (bf16[2560,128]{1,0:T(8,128)(2,1)S(1)}, bf16[2560,128]{1,0:T(8,128)(2,1)}, u32[]{:S(2)}, u32[]{:S(2)}) collective-permute-start(bf16[2560,128]{1,0:T(8,128)(2,1)S(1)} %collective-permute-done.6.refs_6_), channel_id=1, source_target_pairs={{0,1},{1,0},{2,3},{3,2},{4,5},{5,4},{6,7},{7,6},{8,9},{9,8},{10,11... | collective-permute-start | bytes 1966088 | tf_op jit(solution)/shard_map/ppermute | solution.py:377
  36.8 18.9 %collective-permute-start.3 = (bf16[1280,256]{1,0:T(8,128)(2,1)}, bf16[1280,256]{1,0:T(8,128)(2,1)}, u32[]{:S(2)}, u32[]{:S(2)}) collective-permute-start(bf16[1280,256]{1,0:T(8,128)(2,1)} %get-tuple-element.85), channel_id=1, source_target_pairs={{8,0},{16,24},{9,1},{17,25},{10,2},{18,26},{11,3},{19,27},{12,4},{... | collective-permute-start | bytes 1966088 | tf_op jit(solution)/shard_map/ppermute | solution.py:398
  38.1 17.6 %collective-permute-start.2 = (bf16[1280,256]{1,0:T(8,128)(2,1)}, bf16[1280,256]{1,0:T(8,128)(2,1)}, u32[]{:S(2)}, u32[]{:S(2)}) collective-permute-start(bf16[1280,256]{1,0:T(8,128)(2,1)} %get-tuple-element.86), channel_id=1, source_target_pairs={{8,16},{16,8},{9,17},{17,9},{10,18},{18,10},{11,19},{19,11},{12,20... | collective-permute-start | bytes 1966088 | tf_op jit(solution)/shard_map/ppermute | solution.py:397
  72.9 13.3 %collective-permute-start.14 = (f32[5,640]{1,0:T(8,128)S(1)}, f32[5,640]{1,0:T(8,128)S(1)}, u32[]{:S(2)}, u32[]{:S(2)}) collective-permute-start(f32[5,640]{1,0:T(8,128)S(1)} %merge_rows.1.refs_0_._), channel_id=1, source_target_pairs={{0,6},{1,7},{2,4},{3,5},{4,2},{5,3},{6,0},{7,1},{8,14},{9,15},{10,... | collective-permute-start | bytes 38408 | tf_op jit(solution)/shard_map/ppermute | solution.py:377
  74.6 11.6 %collective-permute-start.13 = (f32[5,640]{1,0:T(8,128)S(1)}, f32[5,640]{1,0:T(8,128)S(1)}, u32[]{:S(2)}, u32[]{:S(2)}) collective-permute-start(f32[5,640]{1,0:T(8,128)S(1)} %merge_rows.1.refs_0_._), channel_id=1, source_target_pairs={{0,4},{1,5},{2,6},{3,7},{4,0},{5,1},{6,2},{7,3},{8,12},{9,13},{10,... | collective-permute-start | bytes 38408 | tf_op jit(solution)/shard_map/ppermute | solution.py:377
  75.9 10.3 %collective-permute-start.12 = (f32[5,640]{1,0:T(8,128)S(1)}, f32[5,640]{1,0:T(8,128)S(1)}, u32[]{:S(2)}, u32[]{:S(2)}) collective-permute-start(f32[5,640]{1,0:T(8,128)S(1)} %merge_rows.1.refs_0_._), channel_id=1, source_target_pairs={{0,2},{1,3},{2,0},{3,1},{4,6},{5,7},{6,4},{7,5},{8,10},{9,11},{10,... | collective-permute-start | bytes 38408 | tf_op jit(solution)/shard_map/ppermute | solution.py:377
  76.5 6.0 %collective-permute-start.17 = (f32[1,1280]{1,0:T(1,128)S(1)}, f32[1,1280]{1,0:T(1,128)S(1)}, u32[]{:S(2)}, u32[]{:S(2)}) collective-permute-start(f32[1,1280]{1,0:T(1,128)S(1)} %get-tuple-element.50.refs_4_), channel_id=1, source_target_pairs={{0,24},{8,16},{16,8},{24,0},{1,25},{9,17},{17,9},{25,1},{2,26},{10... | collective-permute-start | bytes 15368 | tf_op jit(solution)/shard_map/ppermute | solution.py:380
  78.8 5.7 %collective-permute-start.16 = (f32[1,1280]{1,0:T(1,128)S(1)}, f32[1,1280]{1,0:T(1,128)S(1)}, u32[]{:S(2)}, u32[]{:S(2)}) collective-permute-start(f32[1,1280]{1,0:T(1,128)S(1)} %get-tuple-element.50.refs_4_), channel_id=1, source_target_pairs={{0,16},{8,24},{16,0},{24,8},{1,17},{9,25},{17,1},{25,9},{2,18},{10... | collective-permute-start | bytes 15368 | tf_op jit(solution)/shard_map/ppermute | solution.py:380
  95.0 18.5 %collective-permute-start.19 = (bf16[1280,256]{1,0:T(8,128)(2,1)S(1)}, bf16[1280,256]{1,0:T(8,128)(2,1)S(1)}, u32[]{:S(2)}, u32[]{:S(2)}) collective-permute-start(bf16[1280,256]{1,0:T(8,128)(2,1)S(1)} %get-tuple-element.51), channel_id=1, source_target_pairs={{0,8},{24,16},{1,9},{25,17},{2,10},{26,18},{3,11},{27,19},{4,12},{... | collective-permute-start | bytes 1966088 | tf_op jit(solution)/shard_map/ppermute | solution.py:413
  98.9 14.5 %collective-permute-start.18 = (bf16[1280,256]{1,0:T(8,128)(2,1)S(1)}, bf16[1280,256]{1,0:T(8,128)(2,1)S(1)}, u32[]{:S(2)}, u32[]{:S(2)}) collective-permute-start(bf16[1280,256]{1,0:T(8,128)(2,1)S(1)} %get-tuple-element.51), channel_id=1, source_target_pairs={{8,16},{16,8},{9,17},{17,9},{10,18},{18,10},{11,19},{19,11},{12,20... | collective-permute-start | bytes 1966088 | tf_op jit(solution)/shard_map/ppermute | solution.py:412
  99.7 13.8 %collective-permute-start.20 = (f32[1,128]{1,0:T(1,128)S(1)}, f32[1,128]{1,0:T(1,128)S(1)}, u32[]{:S(2)}, u32[]{:S(2)}) collective-permute-start(f32[1,128]{1,0:T(1,128)S(1)} %get-tuple-element.61), channel_id=1, source_target_pairs={{0,9},{1,8},{2,11},{3,10},{4,13},{5,12},{6,15},{7,14},{8,1},{9,0},... | collective-permute-start | bytes 1544 | tf_op jit(solution)/shard_map/ppermute | solution.py:384
  113.5 7.5 %collective-permute-start.21 = (bf16[2560,512]{1,0:T(8,128)(2,1)S(1)}, bf16[2560,512]{1,0:T(8,128)(2,1)S(1)}, u32[]{:S(2)}, u32[]{:S(2)}) collective-permute-start(bf16[2560,512]{1,0:T(8,128)(2,1)S(1)} %get-tuple-element.67), channel_id=1, source_target_pairs={{0,1},{1,0},{2,3},{3,2},{4,5},{5,4},{6,7},{7,6},{8,9},{9,8},{10,11... | collective-permute-start | bytes 7864328 | tf_op jit(solution)/shard_map/ppermute | solution.py:377
  115.7 5.3 %collective-permute-start.22 = (f32[1,128]{1,0:T(1,128)S(1)}, f32[1,128]{1,0:T(1,128)S(1)}, u32[]{:S(2)}, u32[]{:S(2)}) collective-permute-start(f32[1,128]{1,0:T(1,128)S(1)} %add.46), channel_id=1, source_target_pairs={{0,18},{1,19},{2,16},{3,17},{4,22},{5,23},{6,20},{7,21},{8,26},{9,... | collective-permute-start | bytes 1544 | tf_op jit(solution)/shard_map/ppermute | solution.py:384
  121.5 19.5 %collective-permute-start.27 = (bf16[1280,256]{1,0:T(8,128)(2,1)S(1)}, bf16[1280,256]{1,0:T(8,128)(2,1)S(1)}, u32[]{:S(2)}, u32[]{:S(2)}) collective-permute-start(bf16[1280,256]{1,0:T(8,128)(2,1)S(1)} %get-tuple-element.77), channel_id=1, source_target_pairs={{0,8},{8,16},{16,24},{24,0},{1,9},{9,17},{17,25},{25,1},{2,10},{10... | collective-permute-start | bytes 1966088 | tf_op jit(solution)/shard_map/ppermute | solution.py:431
  121.5 30.3 %collective-permute-start.28 = (bf16[1280,256]{1,0:T(8,128)(2,1)S(1)}, bf16[1280,256]{1,0:T(8,128)(2,1)S(1)}, u32[]{:S(2)}, u32[]{:S(2)}) collective-permute-start(bf16[1280,256]{1,0:T(8,128)(2,1)S(1)} %get-tuple-element.78), channel_id=1, source_target_pairs={{0,24},{8,0},{16,8},{24,16},{1,25},{9,1},{17,9},{25,17},{2,26},{10... | collective-permute-start | bytes 1966088 | tf_op jit(solution)/shard_map/ppermute | solution.py:432
  126.8 26.2 %collective-permute-start.24 = (bf16[2560,128]{1,0:T(8,128)(2,1)S(1)}, bf16[2560,128]{1,0:T(8,128)(2,1)S(1)}, u32[]{:S(2)}, u32[]{:S(2)}) collective-permute-start(bf16[2560,128]{1,0:T(8,128)(2,1)S(1)} %get-tuple-element.74), channel_id=1, source_target_pairs={{0,2},{1,3},{2,0},{3,1},{4,6},{5,7},{6,4},{7,5},{8,10},{9,11},{10,... | collective-permute-start | bytes 1966088 | tf_op jit(solution)/shard_map/ppermute | solution.py:377
  127.8 29.1 %collective-permute-start.25 = (bf16[2560,128]{1,0:T(8,128)(2,1)S(1)}, bf16[2560,128]{1,0:T(8,128)(2,1)S(1)}, u32[]{:S(2)}, u32[]{:S(2)}) collective-permute-start(bf16[2560,128]{1,0:T(8,128)(2,1)S(1)} %get-tuple-element.75), channel_id=1, source_target_pairs={{0,4},{1,5},{2,6},{3,7},{4,0},{5,1},{6,2},{7,3},{8,12},{9,13},{10,... | collective-permute-start | bytes 1966088 | tf_op jit(solution)/shard_map/ppermute | solution.py:377
  128.9 28.1 %collective-permute-start.26 = (bf16[2560,128]{1,0:T(8,128)(2,1)S(1)}, bf16[2560,128]{1,0:T(8,128)(2,1)S(1)}, u32[]{:S(2)}, u32[]{:S(2)}) collective-permute-start(bf16[2560,128]{1,0:T(8,128)(2,1)S(1)} %get-tuple-element.76), channel_id=1, source_target_pairs={{0,6},{1,7},{2,4},{3,5},{4,2},{5,3},{6,0},{7,1},{8,14},{9,15},{10,... | collective-permute-start | bytes 1966088 | tf_op jit(solution)/shard_map/ppermute | solution.py:377
  (8 other events, 71.9 us)
